TPU v7x, 256 devices: a whole 4x4x8 slice. The times are simulated.
256 devices in a mesh: lat: 32 (over x, y, core), ch: 8 (over z).
Axes of the slice: x: 4, y: 4, z: 8, core: 2. Of those that a mesh axis runs over, the one named last changes fastest.
Arguments:
- field_in: bfloat16 [480, 256, 1024], P('lat', 'ch'), may hold values from -6 to 6
- mix_weight: bfloat16 [2, 256, 256, 480], P(None, None, 'ch', 'lat'), may hold values from -0.375 to 0.375
- order_slots: int32 [480], replicated, may hold values from 0 to 479, each once
Outputs:
- field_out: bfloat16 [480, 256, 1024], P('lat', 'ch')
- spectrum: bfloat16 [480, 2, 256, 480], P('lat', None, 'ch')
Inputs may be any that keep to these rules, and one draw needn't show every extreme that they name: `order_slots`: every order of 0 to 479 stands in exactly one slot.
All inputs are finite; a program needn't handle non-finite values.
Results may differ from a plain program's by a relative error of at most 0.009.
Values may be sent and summed in bfloat16 or wider, within the bound.
No kernel may reach another device: no remote copies, remote signals or barrier semaphores. Data moves between devices by JAX's collectives and lax.ppermute only.
A program may use at most 128 MiB of HBM per device.

v0:
```python
import math

import jax
import jax.numpy as jnp
from jax import lax
from jax.sharding import PartitionSpec as P

rescale_bits = 60
degree_block = 16


def fourier_tables(orders, lon_total):
    longitude = jnp.arange(lon_total, dtype=jnp.int32)
    phases = orders[None, :] * longitude[:, None] % lon_total
    angles = phases.astype(jnp.float32) * (2.0 * math.pi / lon_total)
    return (jnp.cos(angles), jnp.sin(angles))


def legendre_tables(orders, lat_total, mode_total):
    colatitude = (jnp.arange(lat_total, dtype=jnp.float32) + 0.5) * (math.pi / lat_total)
    cosine_lat = jnp.cos(colatitude)
    sine_lat = jnp.sin(colatitude)
    factor_idx = jnp.arange(1, mode_total, dtype=jnp.float32)
    log_prod = jnp.concatenate(
        [
            jnp.zeros((1,), jnp.float32),
            jnp.cumsum(0.5 * jnp.log((2.0 * factor_idx - 1.0) / (2.0 * factor_idx))),
        ]
    )
    order_vals = orders.astype(jnp.float32)
    matches = orders[:, None] == jnp.arange(mode_total, dtype=jnp.int32)[None, :]
    picked = jnp.sum(jnp.where(matches, log_prod[None, :], jnp.float32(0.0)), axis=1)
    log_start = (
        0.5 * jnp.log(order_vals + 0.5)[:, None]
        + picked[:, None]
        + order_vals[:, None] * jnp.log(sine_lat)[None, :]
    )
    quadrature = math.pi / lat_total * sine_lat
    ord_sq = order_vals * order_vals
    shrink = jnp.float32(2.0 ** (-rescale_bits))
    limit = jnp.float32(2.0**rescale_bits)
    log_step = jnp.float32(rescale_bits * math.log(2.0))

    def advance(state_now, block_start):
        before, current, rescales = state_now
        forward_rows = []
        inverse_rows = []
        for offset in range(degree_block):
            degree = (block_start + offset).astype(jnp.float32)
            deg_sq = degree * degree
            deg_prev = degree - 1.0
            alpha_coef = jnp.sqrt(
                jnp.maximum(4.0 * deg_sq - 1.0, 1.0) / jnp.maximum(deg_sq - ord_sq, 1.0)
            )
            beta_coef = jnp.sqrt(
                jnp.maximum(deg_prev * deg_prev - ord_sq, 0.0)
                / jnp.maximum(4.0 * deg_prev * deg_prev - 1.0, 1.0)
            )
            next_value = alpha_coef[:, None] * (
                cosine_lat[None, :] * current - beta_coef[:, None] * before
            )
            is_start = (degree == order_vals)[:, None]
            is_below = (degree < order_vals)[:, None]
            next_value = jnp.where(
                is_start, jnp.float32(1.0), jnp.where(is_below, jnp.float32(0.0), next_value)
            )
            before = jnp.where(is_start | is_below, jnp.float32(0.0), current)
            too_large = jnp.abs(next_value) > limit
            next_value = jnp.where(too_large, next_value * shrink, next_value)
            before = jnp.where(too_large, before * shrink, before)
            rescales = rescales + jnp.where(too_large, jnp.float32(1.0), jnp.float32(0.0))
            current = next_value
            p_value = current * jnp.exp(log_start + rescales * log_step)
            forward_rows.append((p_value * quadrature[None, :]).astype(jnp.bfloat16))
            inverse_rows.append(p_value.astype(jnp.bfloat16))
        return ((before, current, rescales), (jnp.stack(forward_rows), jnp.stack(inverse_rows)))

    zeros = jnp.zeros((orders.shape[0], lat_total), jnp.float32)
    starts = jnp.arange(0, mode_total, degree_block, dtype=jnp.int32)
    _, (forward_all, inverse_all) = lax.scan(advance, (zeros, zeros, zeros), starts)
    shape = (mode_total, orders.shape[0], lat_total)
    return (forward_all.reshape(shape), inverse_all.reshape(shape))


def mix_channels(coeffs, weight):
    products = jnp.einsum("wiol,mxil->mwxol", weight, coeffs, preferred_element_type=jnp.float32)
    real_part = products[:, 0, 0] - products[:, 1, 1]
    imag_part = products[:, 0, 1] + products[:, 1, 0]
    return jnp.stack([real_part, imag_part], axis=1)


def on_device(field_in, mix_weight, order_slots):
    lat_dev, ch_dev, lon_total = field_in.shape
    lat_count = lax.axis_size("lat")
    lat_total = lat_dev * lat_count
    mode_total = order_slots.shape[0]
    ord_dev = mode_total // lat_count
    cosines, sines = fourier_tables(order_slots, lon_total)
    forward_table = jnp.stack([cosines, -sines], axis=1).astype(jnp.bfloat16)
    spectral_rows = jnp.einsum(
        "acn,nxm->xacm", field_in, forward_table, preferred_element_type=jnp.float32
    ).astype(jnp.bfloat16)
    my_orders = lax.dynamic_slice_in_dim(order_slots, lax.axis_index("lat") * ord_dev, ord_dev)
    analysis, synthesis = legendre_tables(my_orders, lat_total, mode_total)
    coeffs = jnp.einsum(
        "lmj,xjcm->mxcl",
        analysis,
        lax.all_to_all(spectral_rows, "lat", split_axis=3, concat_axis=1, tiled=True),
        preferred_element_type=jnp.float32,
    ).astype(jnp.bfloat16)
    all_channels = lax.all_gather(coeffs, "ch", axis=2, tiled=True)
    w_piece = lax.all_gather(mix_weight, "lat", axis=3, tiled=True)
    block_part = lax.slice_in_dim(all_channels, 0, w_piece.shape[3], axis=3)
    spectrum = mix_channels(block_part, w_piece).astype(jnp.bfloat16)
    synth_rows = jnp.einsum(
        "lmj,mxcl->xjcm", synthesis, spectrum, preferred_element_type=jnp.float32
    ).astype(jnp.bfloat16)
    order_weight = jnp.where(order_slots == 0, jnp.float32(1.0), jnp.float32(2.0)) / lon_total
    inverse_table = jnp.stack(
        [cosines.T * order_weight[:, None], -sines.T * order_weight[:, None]], axis=0
    ).astype(jnp.bfloat16)
    wave_out = jnp.einsum(
        "xacm,xmn->acn",
        lax.all_to_all(synth_rows, "lat", split_axis=1, concat_axis=3, tiled=True),
        inverse_table,
        preferred_element_type=jnp.float32,
    )
    field_out = (field_in.astype(jnp.float32) + jax.nn.gelu(wave_out)).astype(jnp.bfloat16)
    return (field_out, spectrum)


def solution(mesh):
    placed = (P("lat", "ch", None), P(None, None, "ch", "lat"), P())
    return jax.shard_map(
        on_device,
        mesh=mesh,
        in_specs=placed,
        out_specs=(P("lat", "ch", None), P("lat", None, "ch", None)),
        check_vma=False,
    )
```

profile of v0, /device:TPU:1, one launch (start us, length us, event | category | flops | bytes accessed | tf_op | source)
XLA Modules:
  0.0 754.8 jit_solution(19946780066204542)
XLA Ops:
  7.2 9.6 %cosine_convert_fusion = (bf16[1024,1,480]{0,2,1:T(8,128)(2,1)S(1)}, bf16[1024,1,480]{0,2,1:T(8,128)(2,1)S(1)}) fusion(s32[480]{0:T(512)} %param.7), kind=kLoop, calls=%fused_computation.379 | loop fusion | flops 8355840 | bytes 1968000 | tf_op jit(solution)/shard_map/convert.6
  16.7 1.2 fusion.206
  18.0 6.1 copy.51
  24.1 5.6 reshape.796
  29.8 8.6 %all-to-all-start = ((bf16[32,2,7200]{2,1,0:T(2,128)(2,1)}), bf16[32,2,7200]{2,1,0:T(2,128)(2,1)S(1)}, u32[]{:S(2)}, u32[]{:S(2)}) async-start(bf16[32,2,7200]{2,1,0:T(2,128)(2,1)} %reshape.796), calls=%async_computation | async-start | bytes 1867776 | tf_op jit(solution)/shard_map/all_to_all | solution.py:108
  39.5 424.9 %while.25 = (s32[]{:T(128)}, f32[15,480]{1,0:T(8,128)S(1)}, f32[15,480]{1,0:T(8,128)S(1)}, f32[15,480]{1,0:T(8,128)S(1)}, bf16[30,16,15,480]{3,2,1,0:T(8,128)(2,...) while((s32[]{:T(128)}, f32[15,480]{1,0:T(8,128)S(1)}, ...), condition=%wide.region_4.5_spmd.clone.clone.clone.clone, body=%wide.region_3.4_spmd.clone.clone.clone.clone.sunk | while | flops 4389552 | bytes 4247420 | solution.py:80
  52.7 0.9 bitcast_dynamic-update-slice_fusion.3
  66.9 0.8 bitcast_dynamic-update-slice_fusion.3
  81.1 0.9 bitcast_dynamic-update-slice_fusion.3
  95.2 0.9 bitcast_dynamic-update-slice_fusion.3
  123.6 0.9 bitcast_dynamic-update-slice_fusion.3
  151.9 0.8 bitcast_dynamic-update-slice_fusion.3
  166.1 0.8 bitcast_dynamic-update-slice_fusion.3
  180.2 0.9 bitcast_dynamic-update-slice_fusion.3
  194.4 0.9 bitcast_dynamic-update-slice_fusion.3
  208.6 0.8 bitcast_dynamic-update-slice_fusion.3
  222.7 0.9 bitcast_dynamic-update-slice_fusion.3
  236.9 0.9 bitcast_dynamic-update-slice_fusion.3
  279.4 0.9 bitcast_dynamic-update-slice_fusion.3
  293.5 0.8 bitcast_dynamic-update-slice_fusion.3
  321.8 0.9 bitcast_dynamic-update-slice_fusion.3
  350.2 0.8 bitcast_dynamic-update-slice_fusion.3
  378.5 0.9 bitcast_dynamic-update-slice_fusion.3
  406.8 0.9 bitcast_dynamic-update-slice_fusion.3
  421.0 0.9 bitcast_dynamic-update-slice_fusion.3
  435.1 0.8 bitcast_dynamic-update-slice_fusion.3
  449.3 0.8 bitcast_dynamic-update-slice_fusion.3
  463.4 0.9 bitcast_dynamic-update-slice_fusion.3
  464.4 4.7 reshape.797
  469.1 4.6 copy.53
  473.7 12.4 %fusion.198 = bf16[15,2,32,480]{3,2,1,0:T(8,128)(2,1)S(1)} fusion(bf16[480,15,480,1]{2,1,0,3:T(8,128)(2,1)} %bitcast.259, bf16[2,480,32,15]{2,0,3,1:T(2,128)(2,1)S(1)} %bitcast.257), kind=kOutput, calls=%fused_computation.386 | convolution fusion | flops 442828800 | bytes 8755200 | tf_op jit(solution)/shard_map/lmj,xjcm->mxcl/dot_general | solution.py:105
  486.1 2.5 copy.56
  489.5 91.1 %all-gather.3.cloned.1.call-done = bf16[15,2,256,480]{3,1,0,2:T(2,128)(2,1)} async-done(((bf16[15,2,32,480]{3,1,0,2:T(2,128)(2,1)}), bf16[15,2,256,480]{3,1,0,2:T(2,128)(2,1)}) %all-gather.3.cloned.1.call-update) | async-done | bytes 7372816 | tf_op jit(solution)/shard_map/all_gather | solution.py:111
  580.5 16.7 %copy.67 = bf16[15,2,256,480,1]{2,0,4,1,3:T(8,128)(2,1)} copy(bf16[15,2,256,480,1]{3,1,0,2,4:T(2,128)(2,1)} %bitcast.255) | data formatting | bytes 14745600 | tf_op jit(solution)/shard_map/all_gather | solution.py:111
  597.2 60.7 %all-gather.5.cloned.1.call-done = bf16[2,256,32,480]{1,2,0,3:T(8,128)(2,1)} async-done(((bf16[2,256,32,15]{1,2,0,3:T(8,128)(2,1)}), bf16[2,256,32,480]{1,2,0,3:T(8,128)(2,1)}) %all-gather.5.cloned.1.call-update) | async-done | bytes 15728656 | tf_op jit(solution)/shard_map/all_gather | solution.py:112
  658.0 19.9 %fusion.152 = f32[15,2,2,32,480]{3,0,1,2,4:T(8,128)} fusion(bf16[15,2,256,480,1]{2,0,4,1,3:T(8,128)(2,1)} %copy.67, bf16[2,256,32,480]{1,2,0,3:T(8,128)(2,1)} %all-gather.5.cloned.1.call-done), kind=kOutput, calls=%fused_computation.331 | convolution fusion | flops 471859200 | bytes 26787840 | tf_op jit(solution)/shard_map/wiol,mxil->mwxol/dot_general | solution.py:86
  677.9 7.9 %fusion.179 = (bf16[15,1,32,480]{2,0,3,1:T(8,128)(2,1)}, bf16[15,1,32,480]{2,0,3,1:T(8,128)(2,1)S(1)}) fusion(f32[15,2,2,32,480]{3,0,1,2,4:T(8,128)} %fusion.152), kind=kLoop, calls=%fused_computation.365 | loop fusion | flops 921600 | bytes 4608000 | tf_op jit(solution)/shard_map/sub | solution.py:87
  685.8 2.6 copy.59
  688.4 1.9 copy.60
  690.5 11.4 %fusion.203 = bf16[2,480,32,15]{1,2,0,3:T(8,128)(2,1)S(1)} fusion(bf16[15,2,32,480]{3,2,1,0:T(8,128)(2,1)S(1)} %pad_maximum_fusion, bf16[480,15,480,1]{2,1,0,3:T(8,128)(2,1)} %bitcast.260), kind=kOutput, calls=%fused_computation.387 | convolution fusion | flops 442828800 | bytes 8755200 | tf_op jit(solution)/shard_map/lmj,mxcl->xjcm/dot_general | solution.py:115
  701.9 6.1 copy.62
  708.1 5.6 reshape.798
  713.7 5.7 all-to-all-start.1
  719.4 8.9 %multiply_convert_fusion.17 = (bf16[1,480,1024]{2,1,0:T(8,128)(2,1)S(1)}, bf16[1,480,1024]{2,1,0:T(8,128)(2,1)S(1)}) fusion(f32[480]{0:T(512)S(1)} %select_multiply_fusion.1, s32[480]{0:T(512)S(1)} %copy-done.2), kind=kLoop, calls=%fused_computation.375 | loop fusion | flops 9338880 | bytes 1969920 | tf_op jit(solution)/shard_map/convert
  728.3 6.6 all-to-all-done.1
  735.0 4.3 reshape.799
  739.3 5.6 copy.63
  744.9 2.8 fusion.178
  (885 shorter events, 97.8 us)
Async XLA Ops:
  7.2 9.6 %copy-start.3 = (bf16[15,32,1024]{2,1,0:T(8,128)(2,1)S(1)}, bf16[15,32,1024]{2,1,0:T(8,128)(2,1)}, u32[]{:S(2)}) copy-start(bf16[15,32,1024]{2,1,0:T(8,128)(2,1)} %param.5) | copy-start | bytes 2949124
  24.1 14.4 %copy-start.2 = (s32[480]{0:T(512)S(1)}, s32[480]{0:T(512)}, u32[]{:S(2)}) copy-start(s32[480]{0:T(512)} %param.7) | copy-start | bytes 5764
  29.8 434.7 %all-to-all-start = ((bf16[32,2,7200]{2,1,0:T(2,128)(2,1)}), bf16[32,2,7200]{2,1,0:T(2,128)(2,1)S(1)}, u32[]{:S(2)}, u32[]{:S(2)}) async-start(bf16[32,2,7200]{2,1,0:T(2,128)(2,1)} %reshape.796), calls=%async_computation | async-start | bytes 1867776 | tf_op jit(solution)/shard_map/all_to_all | solution.py:108
  38.3 542.2 %all-gather.3.cloned.1.call-start = ((), (), s32[]{:S(2)}) async-start(), calls=%async_computation.2 | async-start | bytes 8847360 | tf_op jit(solution)/shard_map/all_gather | solution.py:111
  486.0 2.6 copy-start.1
  488.6 169.4 %all-gather.5.cloned.1.call-start = ((), (), s32[]{:S(2)}) async-start(), calls=%async_computation.3 | async-start | bytes 16220160 | tf_op jit(solution)/shard_map/all_gather | solution.py:112
  690.5 11.5 %copy-start = (bf16[15,2,32,480]{3,2,1,0:T(8,128)(2,1)}, bf16[15,2,32,480]{3,2,1,0:T(8,128)(2,1)S(1)}, u32[]{:S(2)}) copy-start(bf16[15,2,32,480]{3,2,1,0:T(8,128)(2,1)S(1)} %pad_maximum_fusion) | copy-start | bytes 2764804
  713.7 21.3 %all-to-all-start.1 = ((bf16[32,2,7200]{2,1,0:T(2,128)(2,1)}), bf16[32,2,7200]{2,1,0:T(2,128)(2,1)S(1)}, u32[]{:S(2)}, u32[]{:S(2)}) async-start(bf16[32,2,7200]{2,1,0:T(2,128)(2,1)} %reshape.798), calls=%async_computation.1 | async-start | bytes 1867776 | tf_op jit(solution)/shard_map/all_to_all | solution.py:124
  739.3 5.6 copy-start.4
Sparse Core Ops, SparseCore 0:
  488.7 91.8 all-gather.2
  583.7 74.2 all-gather.4
where the time goes:
time: 765 us; the launch traced here: 755 us
  loops' own time  310 us (41%)
  waiting for transfers between devices  158 us (21%)
  local copies, waits for them, and re-layouts  112 us (15%)
  other arithmetic  96.8 us (13%)
  matrix products  47.8 us (6%)
  between operations  14.5 us (2%)
  starting transfers between devices  14.4 us (2%)
    another operation x1, loops' own time, legendre_tables(): lax.scan(advance, (zeros, zeros, zeros), starts)  310 us
    all_gather x1, waiting for transfers between devices, on_device(): all_channels = lax.all_gather(coeffs, 'ch', axis=2, tiled=True)  91.1 us
    all_gather x1, waiting for transfers between devices, on_device(): w_piece = lax.all_gather(mix_weight, 'lat', axis=3, tiled=True)  60.7 us
    while x510, other arithmetic  51.8 us
    dynamic_update_slice x30, local copies, waits for them, and re-layouts, legendre_tables(): lax.scan(advance, (zeros, zeros, zeros), starts)  25.5 us
    unnamed x15, local copies, waits for them, and re-layouts  21.1 us
    dot_general x1, matrix products, mix_channels(): jnp.einsum('wiol,mxil->mwxol', weight, coeffs, preferred_element_type=jnp...  19.9 us
    dynamic_slice x30, local copies, waits for them, and re-layouts, legendre_tables(): lax.scan(advance, (zeros, zeros, zeros), starts)  19.5 us
  transfers between devices with their start and end apart: 4, of which 3 were waited for; matrix products, arithmetic and copies ran while one was open for 19% of the time, Pallas kernels for 0%

commit v1 on v0

v1 whole, which is shorter than its diff:
```python
import functools
import math

import jax
import jax.numpy as jnp
import numpy as np
from jax import lax
from jax.experimental import pallas as pl
from jax.experimental.pallas import tpu as pltpu
from jax.sharding import PartitionSpec as P

PAD = 16
PAIRS = 8
LANES = 128
NO_ORDER = 1000
RESCALE_BITS = 60
f32 = jnp.float32
bf16 = jnp.bfloat16


def cos_turns(turns):
    part = turns - jnp.floor(turns + 0.5)
    y = part * math.pi
    z = y * y
    s = 1.0 / 362880 - z * (1.0 / 39916800)
    s = -1.0 / 5040 + z * s
    s = 1.0 / 120 + z * s
    s = -1.0 / 6 + z * s
    s = y * (1.0 + z * s)
    return 1.0 - 2.0 * s * s


def minus_sin_turns(turns):
    return cos_turns(turns + 0.25)


def chunk_transpose(rows):
    lane = lax.broadcasted_iota(jnp.int32, rows[0].shape, 1)
    low = lane < 64
    even = (lane // 32) % 2 == 0
    mid = [None] * 4
    for i in range(2):
        a, b = rows[i], rows[i + 2]
        mid[i] = jnp.where(low, a, pltpu.roll(b, 64, 1))
        mid[i + 2] = jnp.where(low, pltpu.roll(a, 64, 1), b)
    out = []
    for i in (0, 2):
        a, b = mid[i], mid[i + 1]
        out.append(jnp.where(even, a, pltpu.roll(b, 32, 1)))
        out.append(jnp.where(even, pltpu.roll(a, 96, 1), b))
    return out


def forward_kernel(lat_dev, index_ref, quad_ref, field_ref, order_ref, out_ref, table, rows, turned):
    lon = table.shape[0]
    half = table.shape[1] // 4
    order = order_ref[...]
    step_cos = cos_turns(order * (LANES / lon))
    step_sin = -minus_sin_turns(order * (LANES / lon))

    @pl.loop(0, LANES // PAD)
    def _(r):
        n = (lax.broadcasted_iota(jnp.int32, (PAD, order.shape[1]), 0) + r * PAD).astype(f32)
        turns = order * n * (1.0 / lon)
        re, im = cos_turns(turns), minus_sin_turns(turns)
        for k in range(lon // LANES):
            at = pl.ds(pl.multiple_of(k * LANES + r * PAD, PAD), PAD)
            for m2 in range(2):
                cut = slice(m2 * half, (m2 + 1) * half)
                table[at, 2 * m2 * half : (2 * m2 + 1) * half] = re[:, cut].astype(bf16)
                table[at, (2 * m2 + 1) * half : (2 * m2 + 2) * half] = im[:, cut].astype(bf16)
            re, im = re * step_cos + im * step_sin, im * step_cos - re * step_sin

    ch_dev = field_ref.shape[1]
    field = field_ref[...].reshape(lat_dev * ch_dev, lon)
    for q in range(4):
        part = jnp.dot(field, table[:, q * half : (q + 1) * half], preferred_element_type=f32)
        rows[:, q] = part.reshape(lat_dev, ch_dev, half)
    first = index_ref[0] * lat_dev
    for j in range(lat_dev):
        block = rows[j].reshape(4 * ch_dev, half) * quad_ref[first + j]
        turned[pl.ds(j, half, stride=PAD), :] = block.T
    turned[pl.ds(lat_dev, half, stride=PAD), :] = jnp.zeros((half, LANES), f32)
    out_ref[...] = turned[...].astype(bf16).reshape(out_ref.shape)


def inverse_table_kernel(order_ref, out_ref):
    lon = out_ref.shape[1]
    half = out_ref.shape[0] // 4
    steps = half // PAD

    @pl.loop(0, 2 * steps)
    def _(r):
        order = order_ref[pl.ds(pl.multiple_of(r * PAD, PAD), PAD), :]
        step_cos = cos_turns(order * (LANES / lon))
        step_sin = -minus_sin_turns(order * (LANES / lon))
        n = lax.broadcasted_iota(jnp.int32, (PAD, LANES), 1).astype(f32)
        turns = order * n * (1.0 / lon)
        re, im = cos_turns(turns), minus_sin_turns(turns)
        top = (r // steps) * (2 * half) + (r % steps) * PAD
        for k in range(lon // LANES):
            cut = slice(k * LANES, (k + 1) * LANES)
            out_ref[pl.ds(pl.multiple_of(top, PAD), PAD), cut] = re.astype(bf16)
            out_ref[pl.ds(pl.multiple_of(top + half, PAD), PAD), cut] = im.astype(bf16)
            re, im = re * step_cos + im * step_sin, im * step_cos - re * step_sin


def legendre_kernel(
    deg_dev, blocks, scale_ref, order_ref, geo_ref, prod_ref, out_ref, cur, bef, resc, start, expo, root, buf
):
    groups = cur.shape[0]
    log_step = RESCALE_BITS * math.log(2.0)
    shrink = 2.0 ** (-RESCALE_BITS)
    limit = 2.0**RESCALE_BITS
    order = order_ref[...]
    order_sq = order * order

    @pl.when(pl.program_id(0) == 0)
    def _():
        cur[...] = jnp.zeros_like(cur)
        bef[...] = jnp.zeros_like(bef)
        resc[...] = jnp.zeros_like(resc)
        root[...] = jnp.zeros_like(root)
        picked = jnp.zeros((PAD, 1), f32)
        for g in range(groups):
            lane = lax.broadcasted_iota(jnp.int32, (PAD, LANES), 1) + g * LANES
            hit = order == lane.astype(f32)
            term = jnp.where(hit, prod_ref[:, g * LANES : (g + 1) * LANES], 0.0)
            picked = picked + jnp.sum(term, axis=1, keepdims=True)
        head = 0.5 * jnp.log(order + 0.5) + picked
        for g in range(groups):
            log_start = head + order * geo_ref[1:2, g * LANES : (g + 1) * LANES]
            start[g] = log_start
            expo[g] = jnp.exp(log_start)
            buf[g, pl.ds(deg_dev, PAD, stride=PAD), :] = jnp.zeros((PAD, LANES), f32)

    @pl.loop(0, blocks)
    def _(block):
        first = (pl.program_id(0) * blocks + block) * deg_dev
        now = [cur[g] for g in range(groups)]
        old = [bef[g] for g in range(groups)]
        factor = [expo[g] for g in range(groups)]
        cosine = [geo_ref[0:1, g * LANES : (g + 1) * LANES] for g in range(groups)]
        root_prev = root[...]
        for i in range(deg_dev):
            degree = first + i
            deg = degree.astype(f32)
            gap = deg * deg - order_sq
            gap_one = jnp.maximum(gap, 1.0)
            inv = lax.rsqrt(gap_one)
            inv = inv * (1.5 - 0.5 * gap_one * inv * inv)
            alpha = inv * scale_ref[0, degree]
            beta = root_prev * scale_ref[1, degree]
            root_prev = jnp.maximum(gap, 0.0) * inv
            begin = jnp.where(order == deg, 1.0, 0.0)
            for g in range(groups):
                new = alpha * (cosine[g] * now[g] - beta * old[g]) + begin
                old[g], now[g] = now[g], new
                buf[g, pl.ds(i, PAD, stride=PAD), :] = new * factor[g]
            if i in (deg_dev // 2, deg_dev - 1):
                for g in range(groups):
                    large = jnp.abs(now[g]) > limit
                    ratio = jnp.where(large, shrink, 1.0)
                    now[g] = now[g] * ratio
                    old[g] = old[g] * ratio
                    count = resc[g] + jnp.where(large, 1.0, 0.0)
                    resc[g] = count
                    factor[g] = jnp.exp(start[g] + count * log_step)
        root[...] = root_prev
        for g in range(groups):
            cur[g] = now[g]
            bef[g] = old[g]
            expo[g] = factor[g]
            tile = buf[g].reshape(PAD, PAD, LANES).astype(bf16)
            out_ref[:, block, :, g * LANES : (g + 1) * LANES] = tile


def analysis_kernel(rows_ref, table_ref, out_ref):
    rows = rows_ref[...].reshape(-1, LANES)
    even = jnp.dot(table_ref[0], rows, preferred_element_type=f32)
    odd = jnp.dot(table_ref[1], rows, preferred_element_type=f32)
    lane = lax.broadcasted_iota(jnp.int32, even.shape, 1)
    out_ref[...] = jnp.where(lane < LANES // 2, even, odd).astype(bf16).reshape(out_ref.shape)


def mix_kernel(blocks, ch_count, coef_ref, weight_ref, out_ref, wide, mixed):
    degree = pl.program_id(0)
    jump = ch_count * PAD
    ch_dev = LANES // 4

    @pl.when(degree == 0)
    def _():
        wide[...] = coef_ref[...].reshape(wide.shape).astype(f32)
        count = blocks * ch_count
        mixed[pl.ds(PAD - 1, count, stride=PAD), :] = jnp.zeros((count, LANES), f32)

    groups = []
    for h in range(ch_count // 4):
        quads = [wide[pl.ds((4 * h + e) * PAD + degree, blocks, stride=jump), :] for e in range(4)]
        groups.append(chunk_transpose(quads))
    left = jnp.concatenate(
        [jnp.concatenate([g[q] for g in groups], axis=1) for q in range(4)], axis=0
    ).astype(bf16)
    channels = ch_count * ch_dev
    contract = (((1,), (1,)), ((), ()))
    prod = [
        lax.dot_general(
            left, weight_ref[:, w, 0].reshape(channels, channels), contract, preferred_element_type=f32
        )
        for w in range(2)
    ]

    def take(w, q):
        return prod[w][q * blocks : (q + 1) * blocks]

    results = []
    for m2 in range(2):
        results.append(take(0, 2 * m2) - take(1, 2 * m2 + 1))
        results.append(take(1, 2 * m2) + take(0, 2 * m2 + 1))
    for h in range(ch_count // 4):
        quads = chunk_transpose([r[:, h * LANES : (h + 1) * LANES] for r in results])
        for e in range(4):
            mixed[pl.ds((4 * h + e) * PAD + degree, blocks, stride=jump), :] = quads[e]

    @pl.when(degree == pl.num_programs(0) - 1)
    def _():
        out_ref[...] = mixed[...].astype(bf16).reshape(out_ref.shape)


def synthesis_kernel(ord_dev, lon, order_ref, mixed_ref, table_ref, pick_ref, out_ref, spec_ref):
    pair = pl.program_id(0)
    side = mixed_ref[...].reshape(-1, LANES).astype(f32).T.astype(bf16)
    half = LANES // 2
    spec = jnp.dot(side, pick_ref[...], preferred_element_type=f32).astype(bf16)
    shape = spec_ref.shape[1:]
    spec_ref[2 * pair] = spec[:half].reshape(shape)

    @pl.when(2 * pair + 1 < ord_dev)
    def _():
        spec_ref[2 * pair + 1] = spec[half:].reshape(shape)

    parts = []
    for m2 in range(2):
        weight = jnp.where(order_ref[2 * pair + m2] == 0, 1.0 / lon, 2.0 / lon)
        part = jnp.dot(
            side[m2 * half : (m2 + 1) * half], table_ref[m2], preferred_element_type=f32
        )
        parts.append(part * weight)
    out_ref[...] = jnp.concatenate(parts, axis=0).T.astype(bf16).reshape(out_ref.shape)


def backward_kernel(lat_dev, rows_ref, table_ref, field_ref, out_ref, wide, left):
    half = rows_ref.shape[0] * rows_ref.shape[1]
    ch_dev = LANES // 4
    wide[...] = rows_ref[...].reshape(wide.shape).astype(f32)
    for j in range(lat_dev):
        block = wide[pl.ds(j, half, stride=PAD), :].T.astype(bf16)
        for q in range(4):
            left[j * ch_dev : (j + 1) * ch_dev, q * half : (q + 1) * half] = block[
                q * ch_dev : (q + 1) * ch_dev
            ]
    lon = out_ref.shape[2]
    for b in range(4):
        cut = slice(b * lon // 4, (b + 1) * lon // 4)
        wave = jnp.dot(left[...], table_ref[:, cut], preferred_element_type=f32)
        cubic = wave * wave * wave
        grown = 0.5 * wave * (1.0 + jnp.tanh(math.sqrt(2.0 / math.pi) * (wave + 0.044715 * cubic)))
        field = field_ref[:, :, cut].astype(f32)
        out_ref[:, :, cut] = (field + grown.reshape(field.shape)).astype(bf16)


def params(mib, grid=False):
    more = dict(dimension_semantics=("arbitrary",)) if grid else {}
    return pltpu.CompilerParams(vmem_limit_bytes=mib << 20, **more)


def cost(flops, moved):
    return pl.CostEstimate(flops=int(flops), bytes_accessed=int(moved), transcendentals=0)


def on_device(field_in, mix_weight, order_slots):
    lat_dev, ch_dev, lon = field_in.shape
    lat_count = lax.axis_size("lat")
    ch_count = lax.axis_size("ch")
    lat_total = lat_dev * lat_count
    modes = order_slots.shape[0]
    ord_dev = modes // lat_count
    full = lat_count * PAD
    half = lat_count * PAIRS
    index = lax.axis_index("lat")
    vmem = pl.BlockSpec(memory_space=pltpu.VMEM)
    smem = pl.BlockSpec(memory_space=pltpu.SMEM)
    buffer = jax.ShapeDtypeStruct((lat_count, PAIRS, PAD, LANES), bf16)

    angle = math.pi * (np.arange(lat_total) + 0.5) / lat_total
    quad = (math.pi / lat_total * np.sin(angle)).astype(np.float32)
    geo = np.zeros((2, lat_count, PAD), np.float32)
    geo[0, :, :lat_dev] = np.cos(angle).reshape(lat_count, lat_dev)
    geo[1, :, :lat_dev] = np.log(np.sin(angle)).reshape(lat_count, lat_dev)
    geo = geo.reshape(2, full)
    k = np.arange(1, modes)
    prod = np.zeros((1, full), np.float32)
    prod[0, 1:modes] = np.cumsum(0.5 * np.log((2.0 * k - 1.0) / (2.0 * k)))
    deg = np.arange(modes, dtype=np.float64)
    scale = np.sqrt(np.maximum(4.0 * deg * deg - 1.0, 1.0))
    scales = np.ones((2, modes), np.float32)
    scales[0] = scale
    scales[1, 1:] = 1.0 / scale[:-1]
    pick = np.zeros((lat_count, PAD, modes), np.float32)
    pick[:, :ord_dev] = np.eye(modes, dtype=np.float32).reshape(lat_count, ord_dev, modes)
    pick = jnp.asarray(pick.reshape(full, modes), bf16)

    padded = jnp.pad(
        order_slots.reshape(lat_count, ord_dev), ((0, 0), (0, PAD - ord_dev)), constant_values=NO_ORDER
    )
    mine = lax.dynamic_slice_in_dim(padded, index, 1, 0).reshape(PAD)
    by_pair = padded.reshape(lat_count, PAIRS, 2).transpose(2, 0, 1).astype(f32)

    weights = lax.all_gather(jnp.transpose(mix_weight, (0, 3, 2, 1)), "ch", axis=0)

    rows = pl.pallas_call(
        functools.partial(forward_kernel, lat_dev),
        out_shape=buffer,
        in_specs=[smem, smem, vmem, vmem],
        out_specs=vmem,
        scratch_shapes=[
            pltpu.VMEM((lon, 4 * half), bf16),
            pltpu.VMEM((lat_dev, 4, ch_dev, half), f32),
            pltpu.VMEM((half * PAD, LANES), f32),
        ],
        compiler_params=params(32),
        name="forward",
    )(index.reshape(1), jnp.asarray(quad), field_in, by_pair.reshape(1, 2 * half))
    rows = lax.all_to_all(rows, "lat", 0, 0, tiled=True)

    blocks = 4
    groups = full // LANES
    state = pltpu.VMEM((groups, PAD, LANES), f32)
    legendre = pl.pallas_call(
        functools.partial(legendre_kernel, ord_dev, blocks),
        grid=(lat_count // blocks,),
        out_shape=jax.ShapeDtypeStruct((PAD, lat_count, PAD, full), bf16),
        in_specs=[smem, vmem, vmem, vmem],
        out_specs=pl.BlockSpec((PAD, blocks, PAD, full), lambda i: (0, i, 0, 0)),
        scratch_shapes=[state] * 5
        + [pltpu.VMEM((PAD, LANES), f32), pltpu.VMEM((groups, PAD * PAD, LANES), f32)],
        compiler_params=params(32, True),
        cost_estimate=cost(8e9, 2e7),
        name="legendre",
    )(
        jnp.asarray(scales),
        jnp.broadcast_to(mine.astype(f32)[:, None], (PAD, LANES)),
        jnp.asarray(geo),
        jnp.asarray(prod),
    )
    legendre = legendre.reshape(PAD, full, full)
    inverse_table = pl.pallas_call(
        inverse_table_kernel,
        out_shape=jax.ShapeDtypeStruct((4 * half, lon), bf16),
        in_specs=[vmem],
        out_specs=vmem,
        compiler_params=params(32),
        cost_estimate=cost(2e9, 4e6),
        name="inverse_table",
    )(jnp.broadcast_to(by_pair.reshape(2 * half, 1), (2 * half, LANES)))

    pair_block = pl.BlockSpec((lat_count, 1, PAD, LANES), lambda p: (0, p, 0, 0))
    table_block = pl.BlockSpec((2, full, full), lambda p: (p, 0, 0))
    coeffs = pl.pallas_call(
        analysis_kernel,
        grid=(PAIRS,),
        out_shape=buffer,
        in_specs=[pair_block, table_block],
        out_specs=pair_block,
        compiler_params=params(32, True),
        name="analysis",
    )(rows, legendre)
    everywhere = lat_count * ch_count
    coeffs = lax.all_to_all(
        coeffs.reshape(everywhere, PAD, LANES), ("lat", "ch"), 0, 0, tiled=True
    )

    mixed = pl.pallas_call(
        functools.partial(mix_kernel, lat_count, ch_count),
        grid=(ord_dev,),
        out_shape=jax.ShapeDtypeStruct((everywhere, PAD, LANES), bf16),
        in_specs=[
            pl.BlockSpec((everywhere, PAD, LANES), lambda i: (0, 0, 0)),
            pl.BlockSpec((ch_count, 2, 1, ch_dev, ch_count * ch_dev), lambda i: (0, 0, i, 0, 0)),
        ],
        out_specs=pl.BlockSpec((everywhere, PAD, LANES), lambda i: (0, 0, 0)),
        scratch_shapes=[pltpu.VMEM((everywhere * PAD, LANES), f32)] * 2,
        compiler_params=params(32, True),
        name="mix",
    )(coeffs, weights)
    mixed = lax.all_to_all(mixed, ("lat", "ch"), 0, 0, tiled=True)

    synth, spectrum = pl.pallas_call(
        functools.partial(synthesis_kernel, ord_dev, lon),
        grid=(PAIRS,),
        out_shape=(buffer, jax.ShapeDtypeStruct((ord_dev, 2, ch_dev, modes), bf16)),
        in_specs=[smem, pair_block, table_block, pl.BlockSpec((full, modes), lambda p: (0, 0))],
        out_specs=(pair_block, pl.BlockSpec((ord_dev, 2, ch_dev, modes), lambda p: (0, 0, 0, 0))),
        compiler_params=params(32, True),
        name="synthesis",
    )(mine, mixed.reshape(buffer.shape), legendre, pick)
    synth = lax.all_to_all(synth, "lat", 0, 0, tiled=True)

    field_out = pl.pallas_call(
        functools.partial(backward_kernel, lat_dev),
        out_shape=jax.ShapeDtypeStruct(field_in.shape, bf16),
        in_specs=[vmem, vmem, vmem],
        out_specs=vmem,
        scratch_shapes=[
            pltpu.VMEM((half * PAD, LANES), f32),
            pltpu.VMEM((lat_dev * ch_dev, 4 * half), bf16),
        ],
        compiler_params=params(32),
        name="backward",
    )(synth, inverse_table, field_in)
    return (field_out, spectrum)


def solution(mesh):
    placed = (P("lat", "ch", None), P(None, None, "ch", "lat"), P())
    return jax.shard_map(
        on_device,
        mesh=mesh,
        in_specs=placed,
        out_specs=(P("lat", "ch", None), P("lat", None, "ch", None)),
        check_vma=False,
    )
```

time: 765 us -> 189 us (0.25); the launches traced: 755 us -> 189 us
  loops' own time: 310 us -> 0 us
  waiting for transfers between devices: 158 us -> 14.6 us
  other arithmetic: 96.8 us -> 0.02 us
  local copies, waits for them, and re-layouts: 112 us -> 18.6 us
  blocking collectives: 0 us -> 84.3 us
  matrix products: 47.8 us -> 0 us
  Pallas kernels: 0 us -> 44.1 us
    another operation x1 -> x0, loops' own time: 310 us -> none  [legendre_tables(): lax.scan(advance, (zeros, zeros, zeros), starts)]
    all_gather x2 -> x1, waiting for transfers between devices: 152 us -> 0.01 us  [on_device(): lax.all_gather(jnp.transpose(mix_weight, (0, 3, 2, 1)), 'ch', axis=0)]
    all_to_all x0 -> x2, blocking collectives: none -> 84.3 us  [the longest x1 46.4 us: on_device(): lax.all_to_all(coeffs.reshape(everywhere, PAD, LANES), ('lat', 'ch'), 0,...]
    while x510 -> x0, other arithmetic: 51.8 us -> none
    dot_general x5 -> x0, matrix products: 47.8 us -> none  [the longest x1 19.9 us: mix_channels(): jnp.einsum('wiol,mxil->mwxol', weight, coeffs, preferred_element_type=jnp...]
    pallas_call x0 -> x7, Pallas kernels: none -> 44.1 us  [the longest x1 14.3 us: on_device(): pl.pallas_call(functools.partial(legendre_kernel, ord_dev, blocks), grid=...]
    dynamic_update_slice x30 -> x0, local copies, waits for them, and re-layouts: 25.5 us -> none  [legendre_tables(): lax.scan(advance, (zeros, zeros, zeros), starts)]
    another operation x68 -> x0, other arithmetic: 25.3 us -> none
  transfers between devices with their start and end apart: 4 -> 3, of which waited for: 3 -> 1; matrix products, arithmetic and copies ran while one was open for 19% -> 1% of each run, Pallas kernels for 0% -> 13%
where the time goes in v1:
time: 189 us
  blocking collectives  84.3 us (45%)
  Pallas kernels  44.1 us (23%)
  local copies, waits for them, and re-layouts  18.6 us (10%)
  waiting for transfers between devices  14.6 us (8%)
  between operations  14.2 us (8%)
  starting transfers between devices  13.1 us (7%)
    all_to_all x1, blocking collectives, on_device(): lax.all_to_all(coeffs.reshape(everywhere, PAD, LANES), ('lat', 'ch'), 0,...  46.4 us
    all_to_all x1, blocking collectives, on_device(): mixed = lax.all_to_all(mixed, ('lat', 'ch'), 0, 0, tiled=True)  37.9 us
    unnamed x26, local copies, waits for them, and re-layouts  17 us
    pallas_call x1, Pallas kernels, on_device(): pl.pallas_call(functools.partial(legendre_kernel, ord_dev, blocks), grid=...  14.3 us
    all_to_all x1, waiting for transfers between devices, on_device(): synth = lax.all_to_all(synth, 'lat', 0, 0, tiled=True)  13.9 us
    pallas_call x1, Pallas kernels, on_device(): pl.pallas_call(functools.partial(mix_kernel, lat_count, ch_count), grid=(...  9.21 us
    all_to_all x1, starting transfers between devices, on_device(): rows = lax.all_to_all(rows, 'lat', 0, 0, tiled=True)  8.59 us
    pallas_call x1, Pallas kernels, on_device(): pl.pallas_call(functools.partial(synthesis_kernel, ord_dev, lon), grid=(P...  7.09 us
  transfers between devices with their start and end apart: 3, of which 1 were waited for; matrix products, arithmetic and copies ran while one was open for 1% of the time, Pallas kernels for 13%

profile of v1, /device:TPU:1, one launch (start us, length us, event | category | flops | bytes accessed | tf_op | source)
XLA Modules:
  0.0 188.8 jit_solution(15357695322824143099)
XLA Ops:
  7.2 0.0 copy-start.10
  7.2 0.0 copy-start.11
  7.2 0.0 copy-start.12
  7.2 0.0 all-gather.3.cloned.1.call-start
  7.2 0.7 all-gather.3.cloned.1.call-update
  7.9 0.8 reshape.34
  8.7 0.1 copy.20
  8.8 0.1 copy.21
  8.9 0.1 reshape.37.order_ref
  9.0 0.0 copy-start.3
  9.0 1.2 copy-done.3
  10.2 0.0 copy-start.9
  10.2 0.7 copy-done.9
  10.9 4.8 %forward.1 = bf16[32,8,16,128]{3,2,1,0:T(8,128)(2,1)} custom-call(s32[1]{0:T(128)} %bitcast.index_ref, f32[480]{0:T(512)S(1)} %copy-done.9, bf16[15,32,1024]{2,1,0:T(8,128)(2,1)S(1)} %copy-done.3, f32[1,512]{1,0:T(1,128)S(1)} %reshape.37.order_ref), custom_call_target="tpu_custom_call" | custom-call | tf_op jit(solution)/shard_map/forward/pallas_call | solution.py:321
  15.7 8.6 %all-to-all-start = ((bf16[32,8,16,128]{3,2,1,0:T(8,128)(2,1)}), bf16[32,8,16,128]{3,2,1,0:T(8,128)(2,1)S(1)}, u32[]{:S(2)}, u32[]{:S(2)}) async-start(bf16[32,8,16,128]{3,2,1,0:T(8,128)(2,1)} %forward.1), calls=%async_computation | async-start | bytes 2097152 | tf_op jit(solution)/shard_map/all_to_all | solution.py:334
  24.3 0.2 dynamic-slice_reduce_fusion.order_ref
  24.5 0.1 broadcast_in_dim.6.order_ref
  24.6 0.0 copy-done.10
  24.6 0.0 copy-done.11
  24.6 0.0 copy-done.12
  24.6 14.3 %legendre.1 = bf16[16,32,16,512]{3,2,1,0:T(8,128)(2,1)S(1)} custom-call(f32[2,480]{1,0:T(2,128)S(1)} %copy-done.10, f32[16,128]{1,0:T(8,128)S(1)} %broadcast_in_dim.6.order_ref, f32[2,512]{1,0:T(2,128)S(1)} %copy-done.11, f32[1,512]{1,0:T(1,128)S(1)} %copy-done.12), custom_call_target="tpu_custom_call" | custom-call | flops 8000000000 | bytes 20000000 | tf_op jit(solution)/shard_map/legendre/pallas_call | solution.py:339
  38.9 0.0 copy-start
  38.9 3.2 %copy-done = bf16[16,32,16,512]{3,2,1,0:T(8,128)(2,1)} copy-done((bf16[16,32,16,512]{3,2,1,0:T(8,128)(2,1)}, bf16[16,32,16,512]{3,2,1,0:T(8,128)(2,1)S(1)}, u32[]{:S(2)}) %copy-start) | copy-done | bytes 8388632
  42.1 0.0 all-to-all-done.rows_ref
  42.1 0.0 copy-start.1
  42.1 3.5 %copy-done.1 = bf16[16,32,16,512]{3,2,1,0:T(8,128)(2,1)S(1)} copy-done((bf16[16,32,16,512]{3,2,1,0:T(8,128)(2,1)S(1)}, bf16[16,32,16,512]{3,2,1,0:T(8,128)(2,1)}, u32[]{:S(2)}) %copy-start.1) | copy-done | bytes 8388632
  45.6 3.8 %analysis.1 = bf16[32,8,16,128]{3,2,1,0:T(8,128)(2,1)S(1)} custom-call(bf16[32,8,16,128]{3,2,1,0:T(8,128)(2,1)S(1)} %all-to-all-done.rows_ref, bf16[16,512,512]{2,1,0:T(8,128)(2,1)S(1)} %bitcast.9), custom_call_target="tpu_custom_call" | custom-call | tf_op jit(solution)/shard_map/analysis/pallas_call | solution.py:369
  49.4 46.4 %all_to_all.20.coef_ref = bf16[256,16,128]{2,1,0:T(8,128)(2,1)S(1)} all-to-all(bf16[256,16,128]{2,1,0:T(8,128)(2,1)S(1)} %bitcast.12), channel_id=1, replica_groups=mesh['lat'=32,'ch'=8] {'lat','ch'}, dimensions={0} | all-to-all | bytes 2097152 | tf_op jit(solution)/shard_map/all_to_all | solution.py:379
  95.8 0.0 all-gather.3.cloned.1.call-done
  95.9 0.0 copy-start.5
  95.9 2.1 %copy-done.5 = bf16[16,15,32,256]{3,2,1,0:T(8,128)(2,1)S(1)} copy-done((bf16[16,15,32,256]{3,2,1,0:T(8,128)(2,1)S(1)}, bf16[16,15,32,256]{3,2,1,0:T(8,128)(2,1)}, u32[]{:S(2)}) %copy-start.5) | copy-done | bytes 3932184
  98.0 0.0 copy-start.8
  98.0 9.2 %mix.1 = bf16[256,16,128]{2,1,0:T(8,128)(2,1)S(1)} custom-call(bf16[256,16,128]{2,1,0:T(8,128)(2,1)S(1)} %all_to_all.20.coef_ref, bf16[8,2,15,32,256]{4,3,2,1,0:T(8,128)(2,1)S(1)} %bitcast.13), custom_call_target="tpu_custom_call" | custom-call | tf_op jit(solution)/shard_map/mix/pallas_call | solution.py:383
  107.2 37.9 %all_to_all.21 = bf16[256,16,128]{2,1,0:T(8,128)(2,1)S(1)} all-to-all(bf16[256,16,128]{2,1,0:T(8,128)(2,1)S(1)} %mix.1), channel_id=1, replica_groups=mesh['lat'=32,'ch'=8] {'lat','ch'}, dimensions={0} | all-to-all | bytes 2097152 | tf_op jit(solution)/shard_map/all_to_all | solution.py:396
  145.1 0.0 copy-done.8
  145.1 3.4 %copy-done.2 = bf16[16,32,16,512]{3,2,1,0:T(8,128)(2,1)S(1)} copy-done((bf16[16,32,16,512]{3,2,1,0:T(8,128)(2,1)S(1)}, bf16[16,32,16,512]{3,2,1,0:T(8,128)(2,1)}, u32[]{:S(2)}) %copy-start.2) | copy-done | bytes 8388632
  148.5 7.1 %synthesis.1 = (bf16[32,8,16,128]{3,2,1,0:T(8,128)(2,1)}, bf16[15,2,32,480]{3,2,1,0:T(8,128)(2,1)}) custom-call(s32[16]{0:T(128)S(1)} %dynamic-slice_reduce_fusion.order_ref, bf16[32,8,16,128]{3,2,1,0:T(8,128)(2,1)S(1)} %bitcast.11, bf16[16,512,512]{2,1,0:T(8,128)(2,1)S(1)} %bitcast.10, bf16[512,480]{1,0:T(8,128)(2,1)S(1)} %copy-done.8), custom_call_target="tpu_custom_call" | custom-call | tf_op jit(solution)/shard_map/synthesis/pallas_call | solution.py:398
  155.6 4.4 %all-to-all-start.3 = ((bf16[32,8,16,128]{3,2,1,0:T(8,128)(2,1)}), bf16[32,8,16,128]{3,2,1,0:T(8,128)(2,1)S(1)}, u32[]{:S(2)}, u32[]{:S(2)}) async-start(bf16[32,8,16,128]{3,2,1,0:T(8,128)(2,1)} %get-tuple-element.4), calls=%async_computation.3 | async-start | bytes 2097152 | tf_op jit(solution)/shard_map/all_to_all | solution.py:407
  160.0 0.0 copy-start.4
  160.0 0.1 broadcast_in_dim.14
  160.1 0.1 broadcast_in_dim.15.order_ref
  160.2 1.5 inverse_table.1.table_ref
  161.8 0.0 copy-start.6
  161.8 1.3 copy-done.6
  163.1 13.9 %all-to-all-done.3.rows_ref = bf16[32,8,16,128]{3,2,1,0:T(8,128)(2,1)S(1)} async-done(((bf16[32,8,16,128]{3,2,1,0:T(8,128)(2,1)}), bf16[32,8,16,128]{3,2,1,0:T(8,128)(2,1)S(1)}, u32[]{:S(2)}, u32[]{:S(2)}) %all-to-all-start.3) | async-done | bytes 1048608 | tf_op jit(solution)/shard_map/all_to_all | solution.py:407
  177.0 0.0 copy-done.4
  177.0 1.6 copy-done.7
  178.6 3.4 %backward.1 = bf16[15,32,1024]{2,1,0:T(8,128)(2,1)} custom-call(bf16[32,8,16,128]{3,2,1,0:T(8,128)(2,1)S(1)} %all-to-all-done.3.rows_ref, bf16[1024,1024]{1,0:T(8,128)(2,1)S(1)} %copy-done.7, bf16[15,32,1024]{2,1,0:T(8,128)(2,1)S(1)} %copy-done.4), custom_call_target="tpu_custom_call" | custom-call | tf_op jit(solution)/shard_map/backward/pallas_call | solution.py:409
  (4 shorter events, 0.0 us)
Async XLA Ops:
  7.2 17.4 %copy-start.10 = (f32[2,480]{1,0:T(2,128)S(1)}, f32[2,480]{1,0:T(2,128)}, u32[]{:S(2)}) copy-start(f32[2,480]{1,0:T(2,128)} %constant.24.clone.scale_ref) | copy-start | bytes 11524
  7.2 17.4 %copy-start.11 = (f32[2,512]{1,0:T(2,128)S(1)}, f32[2,512]{1,0:T(2,128)}, u32[]{:S(2)}) copy-start(f32[2,512]{1,0:T(2,128)} %constant.25.clone.geo_ref) | copy-start | bytes 12292
  7.2 17.4 %copy-start.12 = (f32[1,512]{1,0:T(1,128)S(1)}, f32[1,512]{1,0:T(1,128)}, u32[]{:S(2)}) copy-start(f32[1,512]{1,0:T(1,128)} %constant.26.clone.prod_ref) | copy-start | bytes 6148
  7.2 88.6 %all-gather.3.cloned.1.call-start = ((), (), s32[]{:S(2)}) async-start(), calls=%async_computation.4 | async-start | bytes 4423680 | tf_op jit(solution)/shard_map/all_gather | solution.py:319
  9.0 1.2 copy-start.3
  10.2 0.7 copy-start.9
  15.7 26.4 %all-to-all-start = ((bf16[32,8,16,128]{3,2,1,0:T(8,128)(2,1)}), bf16[32,8,16,128]{3,2,1,0:T(8,128)(2,1)S(1)}, u32[]{:S(2)}, u32[]{:S(2)}) async-start(bf16[32,8,16,128]{3,2,1,0:T(8,128)(2,1)} %forward.1), calls=%async_computation | async-start | bytes 2097152 | tf_op jit(solution)/shard_map/all_to_all | solution.py:334
  38.9 3.2 %copy-start = (bf16[16,32,16,512]{3,2,1,0:T(8,128)(2,1)}, bf16[16,32,16,512]{3,2,1,0:T(8,128)(2,1)S(1)}, u32[]{:S(2)}) copy-start(bf16[16,32,16,512]{3,2,1,0:T(8,128)(2,1)S(1)} %legendre.1) | copy-start | bytes 25165828
  42.1 3.5 %copy-start.1 = (bf16[16,32,16,512]{3,2,1,0:T(8,128)(2,1)S(1)}, bf16[16,32,16,512]{3,2,1,0:T(8,128)(2,1)}, u32[]{:S(2)}) copy-start(bf16[16,32,16,512]{3,2,1,0:T(8,128)(2,1)} %copy-done) | copy-start | bytes 25165828
  95.9 2.1 %copy-start.5 = (bf16[16,15,32,256]{3,2,1,0:T(8,128)(2,1)S(1)}, bf16[16,15,32,256]{3,2,1,0:T(8,128)(2,1)}, u32[]{:S(2)}) copy-start(bf16[16,15,32,256]{3,2,1,0:T(8,128)(2,1)} %all-gather.3.cloned.1.call-done) | copy-start | bytes 11796484
  98.0 47.1 %copy-start.8 = (bf16[512,480]{1,0:T(8,128)(2,1)S(1)}, bf16[512,480]{1,0:T(8,128)(2,1)}, u32[]{:S(2)}) copy-start(bf16[512,480]{1,0:T(8,128)(2,1)} %constant.22.clone.pick_ref) | copy-start | bytes 1474564
  145.1 3.4 %copy-start.2 = (bf16[16,32,16,512]{3,2,1,0:T(8,128)(2,1)S(1)}, bf16[16,32,16,512]{3,2,1,0:T(8,128)(2,1)}, u32[]{:S(2)}) copy-start(bf16[16,32,16,512]{3,2,1,0:T(8,128)(2,1)} %copy-done) | copy-start | bytes 25165828
  155.6 21.4 %all-to-all-start.3 = ((bf16[32,8,16,128]{3,2,1,0:T(8,128)(2,1)}), bf16[32,8,16,128]{3,2,1,0:T(8,128)(2,1)S(1)}, u32[]{:S(2)}, u32[]{:S(2)}) async-start(bf16[32,8,16,128]{3,2,1,0:T(8,128)(2,1)} %get-tuple-element.4), calls=%async_computation.3 | async-start | bytes 2097152 | tf_op jit(solution)/shard_map/all_to_all | solution.py:407
  160.0 17.0 %copy-start.4 = (bf16[15,32,1024]{2,1,0:T(8,128)(2,1)S(1)}, bf16[15,32,1024]{2,1,0:T(8,128)(2,1)}, u32[]{:S(2)}) copy-start(bf16[15,32,1024]{2,1,0:T(8,128)(2,1)} %field_ref.3) | copy-start | bytes 2949124
  161.8 1.3 copy-start.6
  177.0 1.6 copy-start.7
Sparse Core Ops, SparseCore 0:
  9.8 56.1 all-gather.2

commit v2 on v1

v2 whole, which is shorter than its diff:
```python
import functools
import math

import jax
import jax.numpy as jnp
import numpy as np
from jax import lax
from jax.experimental import pallas as pl
from jax.experimental.pallas import tpu as pltpu
from jax.sharding import PartitionSpec as P

PAD = 16
PAIRS = 8
LANES = 128
NO_ORDER = 1000
PITCH = 17
RESCALE_BITS = 60
f32 = jnp.float32
bf16 = jnp.bfloat16


VMEM_MIB = 57
TABLE_MIB = 63


def cos_turns(turns):
    part = turns - jnp.floor(turns + 0.5)
    y = part * math.pi
    z = y * y
    s = 1.0 / 362880 - z * (1.0 / 39916800)
    s = -1.0 / 5040 + z * s
    s = 1.0 / 120 + z * s
    s = -1.0 / 6 + z * s
    s = y * (1.0 + z * s)
    return 1.0 - 2.0 * s * s


def minus_sin_turns(turns):
    return cos_turns(turns + 0.25)


def chunk_transpose(rows):
    lane = lax.broadcasted_iota(jnp.int32, rows[0].shape, 1)
    low = lane < 64
    even = (lane // 32) % 2 == 0
    mid = [None] * 4
    for i in range(2):
        a, b = rows[i], rows[i + 2]
        mid[i] = jnp.where(low, a, pltpu.roll(b, 64, 1))
        mid[i + 2] = jnp.where(low, pltpu.roll(a, 64, 1), b)
    out = []
    for i in (0, 2):
        a, b = mid[i], mid[i + 1]
        out.append(jnp.where(even, a, pltpu.roll(b, 32, 1)))
        out.append(jnp.where(even, pltpu.roll(a, 96, 1), b))
    return out


def slot_of(j, lat_dev, index, lat_count):
    return jnp.where(index < lat_count // 2, j, lat_dev - 1 - j)


def forward_kernel(lat_dev, lat_count, index_ref, order_ref, field_hbm, out_ref, table, field_ref, rows, turned, sem):
    fetch = pltpu.make_async_copy(field_hbm, field_ref, sem)
    fetch.start()
    lon = table.shape[0]
    half = table.shape[1] // 4
    order = order_ref[...]
    step_cos = cos_turns(order * (LANES / lon))
    step_sin = -minus_sin_turns(order * (LANES / lon))

    @pl.loop(0, LANES // PAD)
    def _(r):
        n = (lax.broadcasted_iota(jnp.int32, (PAD, order.shape[1]), 0) + r * PAD).astype(f32)
        turns = order * n * (1.0 / lon)
        re, im = cos_turns(turns), minus_sin_turns(turns)
        for k in range(lon // LANES):
            at = pl.ds(pl.multiple_of(k * LANES + r * PAD, PAD), PAD)
            for m2 in range(2):
                cut = slice(m2 * half, (m2 + 1) * half)
                table[at, 2 * m2 * half : (2 * m2 + 1) * half] = re[:, cut].astype(bf16)
                table[at, (2 * m2 + 1) * half : (2 * m2 + 2) * half] = im[:, cut].astype(bf16)
            re, im = re * step_cos + im * step_sin, im * step_cos - re * step_sin

    fetch.wait()
    ch_dev = field_ref.shape[1]
    field = field_ref[...].reshape(lat_dev * ch_dev, lon)
    for q in range(4):
        part = jnp.dot(field, table[:, q * half : (q + 1) * half], preferred_element_type=f32)
        rows[:, q] = part.reshape(lat_dev, ch_dev, half)
    index = index_ref[0]
    lat_total = lat_dev * lat_count
    for j in range(lat_dev):
        place = jnp.full((1, half), index * lat_dev + j, jnp.int32).astype(f32)
        quad = cos_turns((place + 0.5) * (0.5 / lat_total) - 0.25) * (math.pi / lat_total)
        block = rows[j].reshape(4 * ch_dev, half) * quad
        turned[pl.ds(slot_of(j, lat_dev, index, lat_count), half, stride=PITCH), :] = block.T
    turned[pl.ds(lat_dev, half, stride=PITCH), :] = jnp.zeros((half, LANES), f32)
    for i in range(half):
        tile = turned[i * PITCH : i * PITCH + PAD, :]
        out_ref[i // PAIRS, i % PAIRS] = tile.astype(bf16)


def inverse_table_kernel(order_ref, out_hbm, out_ref, sem):
    lon = out_ref.shape[1]
    half = out_ref.shape[0] // 4
    steps = half // PAD

    @pl.loop(0, 2 * steps)
    def _(r):
        order = order_ref[pl.ds(pl.multiple_of(r * PAD, PAD), PAD), :]
        step_cos = cos_turns(order * (LANES / lon))
        step_sin = -minus_sin_turns(order * (LANES / lon))
        n = lax.broadcasted_iota(jnp.int32, (PAD, LANES), 1).astype(f32)
        turns = order * n * (1.0 / lon)
        re, im = cos_turns(turns), minus_sin_turns(turns)
        top = (r // steps) * (2 * half) + (r % steps) * PAD
        for k in range(lon // LANES):
            cut = slice(k * LANES, (k + 1) * LANES)
            out_ref[pl.ds(pl.multiple_of(top, PAD), PAD), cut] = re.astype(bf16)
            out_ref[pl.ds(pl.multiple_of(top + half, PAD), PAD), cut] = im.astype(bf16)
            re, im = re * step_cos + im * step_sin, im * step_cos - re * step_sin

    copy = pltpu.make_async_copy(out_ref, out_hbm, sem)
    copy.start()
    copy.wait()


def legendre_kernel(
    deg_dev, scale_ref, order_ref, geo_ref, prod_ref, out_hbm, cur, bef, resc, start, expo, root, buf, table, sems
):
    groups = cur.shape[0]
    log_step = RESCALE_BITS * math.log(2.0)
    shrink = 2.0 ** (-RESCALE_BITS)
    limit = 2.0**RESCALE_BITS
    order = order_ref[...]
    order_sq = order * order
    for state in (cur, bef, resc, root):
        state[...] = jnp.zeros_like(state)
    picked = jnp.zeros((PAD, 1), f32)
    for g in range(prod_ref.shape[1] // LANES):
        lane = lax.broadcasted_iota(jnp.int32, (PAD, LANES), 1) + g * LANES
        hit = order == lane.astype(f32)
        term = jnp.where(hit, prod_ref[:, g * LANES : (g + 1) * LANES], 0.0)
        picked = picked + jnp.sum(term, axis=1, keepdims=True)
    head = 0.5 * jnp.log(order + 0.5) + picked
    for g in range(groups):
        log_start = head + order * geo_ref[1:2, g * LANES : (g + 1) * LANES]
        start[g] = log_start
        expo[g] = jnp.exp(log_start)
        buf[g, pl.ds(deg_dev, PAD, stride=PITCH), :] = jnp.zeros((PAD, LANES), f32)

    def block(index):
        first = index * deg_dev
        now = [cur[g] for g in range(groups)]
        old = [bef[g] for g in range(groups)]
        factor = [expo[g] for g in range(groups)]
        cosine = [geo_ref[0:1, g * LANES : (g + 1) * LANES] for g in range(groups)]
        root_prev = root[...]
        for i in range(deg_dev):
            degree = first + i
            deg = degree.astype(f32)
            gap = deg * deg - order_sq
            gap_one = jnp.maximum(gap, 1.0)
            inv = lax.rsqrt(gap_one)
            inv = inv * (1.5 - 0.5 * gap_one * inv * inv)
            alpha = inv * scale_ref[0, degree]
            beta = root_prev * scale_ref[1, degree]
            root_prev = jnp.maximum(gap, 0.0) * inv
            begin = jnp.where(order == deg, 1.0, 0.0)
            for g in range(groups):
                new = alpha * (cosine[g] * now[g] - beta * old[g]) + begin
                old[g], now[g] = now[g], new
                buf[g, pl.ds(i, PAD, stride=PITCH), :] = new * factor[g]
            if i in (deg_dev // 2, deg_dev - 1):
                for g in range(groups):
                    large = jnp.abs(now[g]) > limit
                    ratio = jnp.where(large, shrink, 1.0)
                    now[g] = now[g] * ratio
                    old[g] = old[g] * ratio
                    count = resc[g] + jnp.where(large, 1.0, 0.0)
                    resc[g] = count
                    factor[g] = jnp.exp(start[g] + count * log_step)
        root[...] = root_prev
        for g in range(groups):
            cur[g] = now[g]
            bef[g] = old[g]
            expo[g] = factor[g]
            for m in range(PAD):
                tile = buf[g, m * PITCH : m * PITCH + PAD, :].astype(bf16)
                table[m, index, :, g * LANES : (g + 1) * LANES] = tile

    parts = sems.shape[0]
    count = table.shape[1] // parts
    copies = []
    for part in range(parts):
        pl.loop(part * count, (part + 1) * count)(block)
        cut = slice(part * count, (part + 1) * count)
        copies.append(pltpu.make_async_copy(table.at[:, cut], out_hbm.at[:, cut], sems.at[part]))
        copies[-1].start()
    for copy in copies:
        copy.wait()


def degree_parity(shape, dim, ord_dev):
    i = lax.broadcasted_iota(jnp.int32, shape, dim)
    return ((i // PAD) * ord_dev + i % PAD) & 1


def fetch_pairs(table_hbm, table, sems):
    def copy(p):
        cut = pl.ds(2 * p, 2)
        return pltpu.make_async_copy(table_hbm.at[cut], table.at[cut], sems.at[p])

    for p in range(PAIRS):
        copy(p).start()
    return copy


def analysis_kernel(ord_dev, order_ref, rows_ref, table_hbm, out_ref, table, sems):
    copy = fetch_pairs(table_hbm, table, sems)
    count = rows_ref.shape[0]
    parity = degree_parity((table.shape[1], LANES), 0, ord_dev)

    @pl.loop(0, PAIRS)
    def _(p):
        north = jnp.concatenate([rows_ref[s, p] for s in range(count // 2)], axis=0)
        south = jnp.concatenate([rows_ref[count - 1 - s, p] for s in range(count // 2)], axis=0)
        both = jnp.concatenate([north, south], axis=1)
        copy(p).wait()
        parts = []
        for m2 in range(2):
            order = order_ref[2 * p + m2]
            prod = jnp.dot(table[2 * p + m2], both, preferred_element_type=f32)
            mirror = prod[:, LANES:]
            parts.append(prod[:, :LANES] + jnp.where(parity == (order & 1), mirror, -mirror))
        lane = lax.broadcasted_iota(jnp.int32, parts[0].shape, 1)
        out = jnp.where(lane < LANES // 2, parts[0], parts[1]).astype(bf16)
        for d in range(count):
            out_ref[d, p] = out[d * PAD : (d + 1) * PAD]


def mix_kernel(blocks, ch_count, deg_dev, coef_ref, weight_hbm, out_ref, wide, mixed, weight, sems):
    jump = ch_count * PAD + 1
    ch_dev = LANES // 4
    channels = ch_count * ch_dev
    contract = (((1,), (1,)), ((), ()))

    def copy(degree):
        return pltpu.make_async_copy(weight_hbm.at[:, :, degree], weight.at[degree], sems.at[degree])

    for degree in range(deg_dev):
        copy(degree).start()
    for d in range(blocks):
        part = coef_ref[d * ch_count : (d + 1) * ch_count].reshape(jump - 1, LANES)
        wide[d * jump : (d + 1) * jump - 1, :] = part.astype(f32)
    for e in range(ch_count):
        mixed[pl.ds((e + 1) * PAD - 1, blocks, stride=jump), :] = jnp.zeros((blocks, LANES), f32)

    def one_degree(degree):
        groups = []
        for h in range(ch_count // 4):
            quads = [wide[pl.ds((4 * h + e) * PAD + degree, blocks, stride=jump), :] for e in range(4)]
            groups.append(chunk_transpose(quads))
        left = jnp.concatenate(
            [jnp.concatenate([g[q] for g in groups], axis=1) for q in range(4)], axis=0
        ).astype(bf16)
        prod = [
            lax.dot_general(
                left,
                weight[degree, :, w].reshape(channels, channels),
                contract,
                preferred_element_type=f32,
            )
            for w in range(2)
        ]

        def take(w, q):
            return prod[w][q * blocks : (q + 1) * blocks]

        results = []
        for m2 in range(2):
            results.append(take(0, 2 * m2) - take(1, 2 * m2 + 1))
            results.append(take(1, 2 * m2) + take(0, 2 * m2 + 1))
        for h in range(ch_count // 4):
            quads = chunk_transpose([r[:, h * LANES : (h + 1) * LANES] for r in results])
            for e in range(4):
                mixed[pl.ds((4 * h + e) * PAD + degree, blocks, stride=jump), :] = quads[e]

    group = MIX_GROUP

    @pl.loop(0, deg_dev // group)
    def _(step):
        for i in range(group):
            copy(step * group + i).wait()
        for i in range(group):
            one_degree(step * group + i)

    for d in range(blocks):
        part = mixed[d * jump : (d + 1) * jump - 1, :].astype(bf16)
        out_ref[d * ch_count : (d + 1) * ch_count] = part.reshape(ch_count, PAD, LANES)


def synthesis_kernel(
    ord_dev, lon, order_ref, mixed_ref, pick_ref, table_hbm, out_ref, spec_ref, table, sems
):
    copy = fetch_pairs(table_hbm, table, sems)
    count = out_ref.shape[0]
    half = LANES // 2
    shape = spec_ref.shape[1:]
    parity = degree_parity((half, table.shape[1]), 1, ord_dev)

    @pl.loop(0, PAIRS)
    def _(p):
        side = jnp.concatenate([mixed_ref[d, p] for d in range(count)], axis=0).astype(f32).T
        spec = jnp.dot(side.astype(bf16), pick_ref[...], preferred_element_type=f32).astype(bf16)
        spec_ref[2 * p] = spec[:half].reshape(shape)

        @pl.when(2 * p + 1 < ord_dev)
        def _():
            spec_ref[2 * p + 1] = spec[half:].reshape(shape)

        copy(p).wait()
        north, south = [], []
        for m2 in range(2):
            order = order_ref[2 * p + m2]
            weight = jnp.where(order == 0, 1.0 / lon, 2.0 / lon)
            part = side[m2 * half : (m2 + 1) * half]
            same = parity == (order & 1)
            split = jnp.concatenate([jnp.where(same, part, 0.0), jnp.where(same, 0.0, part)], axis=0)
            prod = jnp.dot(split.astype(bf16), table[2 * p + m2], preferred_element_type=f32)
            north.append((prod[:half] + prod[half:]) * weight)
            south.append((prod[:half] - prod[half:]) * weight)
        up = jnp.concatenate(north, axis=0).T.astype(bf16)
        down = jnp.concatenate(south, axis=0).T.astype(bf16)
        for s in range(count // 2):
            out_ref[s, p] = up[s * PAD : (s + 1) * PAD]
            out_ref[count - 1 - s, p] = down[s * PAD : (s + 1) * PAD]


def backward_kernel(
    lat_dev, lat_count, index_ref, rows_ref, table_hbm, field_hbm, out_ref, wide, left, table_ref, field_ref, sems
):
    copies = [
        pltpu.make_async_copy(table_hbm, table_ref, sems.at[0]),
        pltpu.make_async_copy(field_hbm, field_ref, sems.at[1]),
    ]
    for copy in copies:
        copy.start()
    half = rows_ref.shape[0] * rows_ref.shape[1]
    ch_dev = LANES // 4
    for i in range(half):
        wide[i * PITCH : i * PITCH + PAD, :] = rows_ref[i // PAIRS, i % PAIRS].astype(f32)
    for j in range(lat_dev):
        slot = slot_of(j, lat_dev, index_ref[0], lat_count)
        block = wide[pl.ds(slot, half, stride=PITCH), :].T.astype(bf16)
        for q in range(4):
            left[j * ch_dev : (j + 1) * ch_dev, q * half : (q + 1) * half] = block[
                q * ch_dev : (q + 1) * ch_dev
            ]
    lon = out_ref.shape[2]
    for copy in copies:
        copy.wait()
    for b in range(4):
        cut = slice(b * lon // 4, (b + 1) * lon // 4)
        wave = jnp.dot(left[...], table_ref[:, cut], preferred_element_type=f32)
        cubic = wave * wave * wave
        grown = 0.5 * wave * (1.0 + jnp.tanh(math.sqrt(2.0 / math.pi) * (wave + 0.044715 * cubic)))
        field = field_ref[:, :, cut].astype(f32)
        out_ref[:, :, cut] = (field + grown.reshape(field.shape)).astype(bf16)


def params(mib=VMEM_MIB):
    return pltpu.CompilerParams(vmem_limit_bytes=int(mib * 2**20))


def cost(flops, moved):
    return pl.CostEstimate(flops=int(flops), bytes_accessed=int(moved), transcendentals=0)


MIX_GROUP = 3
vmem = pl.BlockSpec(memory_space=pltpu.VMEM)
smem = pl.BlockSpec(memory_space=pltpu.SMEM)
hbm = pl.BlockSpec(memory_space=pltpu.HBM)


def buffer_of(lat_count):
    return jax.ShapeDtypeStruct((lat_count, PAIRS, PAD, LANES), bf16)


def call_forward(lat_count, index, order_lanes, field_in):
    lat_dev, ch_dev, lon = field_in.shape
    half = lat_count * PAIRS
    return pl.pallas_call(
        functools.partial(forward_kernel, lat_dev, lat_count),
        out_shape=buffer_of(lat_count),
        in_specs=[smem, vmem, hbm],
        out_specs=vmem,
        scratch_shapes=[
            pltpu.VMEM((lon, 4 * half), bf16),
            pltpu.VMEM(field_in.shape, bf16),
            pltpu.VMEM((lat_dev, 4, ch_dev, half), f32),
            pltpu.VMEM((half * PITCH, LANES), f32),
            pltpu.SemaphoreType.DMA,
        ],
        compiler_params=params(),
        name="forward",
    )(index, order_lanes, field_in)


def call_legendre(lat_count, lat_dev, modes, order_rows):
    lat_total = lat_count * lat_dev
    ord_dev = modes // lat_count
    full = lat_count * PAD
    near = full // 2
    angle = math.pi * (np.arange(lat_total) + 0.5) / lat_total
    geo = np.zeros((2, lat_count, PAD), np.float32)
    geo[0, :, :lat_dev] = np.cos(angle).reshape(lat_count, lat_dev)
    geo[1, :, :lat_dev] = np.log(np.sin(angle)).reshape(lat_count, lat_dev)
    geo = geo.reshape(2, full)[:, :near]
    k = np.arange(1, modes)
    prod = np.zeros((1, full), np.float32)
    prod[0, 1:modes] = np.cumsum(0.5 * np.log((2.0 * k - 1.0) / (2.0 * k)))
    deg = np.arange(modes, dtype=np.float64)
    scale = np.sqrt(np.maximum(4.0 * deg * deg - 1.0, 1.0))
    scales = np.ones((2, modes), np.float32)
    scales[0] = scale
    scales[1, 1:] = 1.0 / scale[:-1]
    groups = near // LANES
    parts = 4
    state = pltpu.VMEM((groups, PAD, LANES), f32)
    table = pl.pallas_call(
        functools.partial(legendre_kernel, ord_dev),
        out_shape=jax.ShapeDtypeStruct((PAD, lat_count, PAD, near), bf16),
        in_specs=[smem, vmem, vmem, vmem],
        out_specs=hbm,
        scratch_shapes=[state] * 5
        + [
            pltpu.VMEM((PAD, LANES), f32),
            pltpu.VMEM((groups, PAD * PITCH, LANES), f32),
            pltpu.VMEM((PAD, lat_count, PAD, near), bf16),
            pltpu.SemaphoreType.DMA((parts,)),
        ],
        compiler_params=params(TABLE_MIB),
        cost_estimate=cost(8e9, 2e7),
        name="legendre",
    )(jnp.asarray(scales), order_rows, jnp.asarray(geo), jnp.asarray(prod))
    return table.reshape(PAD, full, near)


def call_inverse_table(lon, order_rows):
    return pl.pallas_call(
        inverse_table_kernel,
        out_shape=jax.ShapeDtypeStruct((2 * order_rows.shape[0], lon), bf16),
        in_specs=[vmem],
        out_specs=hbm,
        scratch_shapes=[
            pltpu.VMEM((2 * order_rows.shape[0], lon), bf16),
            pltpu.SemaphoreType.DMA,
        ],
        compiler_params=params(TABLE_MIB),
        cost_estimate=cost(2e9, 4e6),
        name="inverse_table",
    )(order_rows)


def call_analysis(ord_dev, orders, rows, table):
    return pl.pallas_call(
        functools.partial(analysis_kernel, ord_dev),
        out_shape=jax.ShapeDtypeStruct(rows.shape, bf16),
        in_specs=[smem, vmem, hbm],
        out_specs=vmem,
        scratch_shapes=[pltpu.VMEM(table.shape, bf16), pltpu.SemaphoreType.DMA((PAIRS,))],
        compiler_params=params(),
        name="analysis",
    )(orders, rows, table)


def call_mix(lat_count, coeffs, weights):
    ch_count, _, ord_dev, ch_dev, channels = weights.shape
    return pl.pallas_call(
        functools.partial(mix_kernel, lat_count, ch_count, ord_dev),
        out_shape=jax.ShapeDtypeStruct(coeffs.shape, bf16),
        in_specs=[vmem, hbm],
        out_specs=vmem,
        scratch_shapes=[pltpu.VMEM((lat_count * (ch_count * PAD + 1), LANES), f32)] * 2
        + [
            pltpu.VMEM((ord_dev, ch_count, 2, ch_dev, channels), bf16),
            pltpu.SemaphoreType.DMA((ord_dev,)),
        ],
        compiler_params=params(),
        name="mix",
    )(coeffs, weights)


def call_synthesis(ord_dev, lon, orders, mixed, table):
    lat_count = mixed.shape[0]
    modes = ord_dev * lat_count
    full = lat_count * PAD
    ch_dev = LANES // 4
    pick = np.zeros((lat_count, PAD, modes), np.float32)
    pick[:, :ord_dev] = np.eye(modes, dtype=np.float32).reshape(lat_count, ord_dev, modes)
    pick = jnp.asarray(pick.reshape(full, modes), bf16)
    return pl.pallas_call(
        functools.partial(synthesis_kernel, ord_dev, lon),
        out_shape=(
            buffer_of(lat_count),
            jax.ShapeDtypeStruct((ord_dev, 2, ch_dev, modes), bf16),
        ),
        in_specs=[smem, vmem, vmem, hbm],
        out_specs=(vmem, vmem),
        scratch_shapes=[pltpu.VMEM(table.shape, bf16), pltpu.SemaphoreType.DMA((PAIRS,))],
        compiler_params=params(),
        name="synthesis",
    )(orders, mixed, pick, table)


def call_backward(index, rows, table, field_in):
    lat_dev, ch_dev, _ = field_in.shape
    lat_count = rows.shape[0]
    half = lat_count * PAIRS
    return pl.pallas_call(
        functools.partial(backward_kernel, lat_dev, lat_count),
        out_shape=jax.ShapeDtypeStruct(field_in.shape, bf16),
        in_specs=[smem, vmem, hbm, hbm],
        out_specs=vmem,
        scratch_shapes=[
            pltpu.VMEM((half * PITCH, LANES), f32),
            pltpu.VMEM((lat_dev * ch_dev, 4 * half), bf16),
            pltpu.VMEM(table.shape, bf16),
            pltpu.VMEM(field_in.shape, bf16),
            pltpu.SemaphoreType.DMA((2,)),
        ],
        compiler_params=params(),
        name="backward",
    )(index, rows, table, field_in)


def on_device(field_in, mix_weight, order_slots):
    lat_dev, _, lon = field_in.shape
    lat_count = lax.axis_size("lat")
    modes = order_slots.shape[0]
    ord_dev = modes // lat_count
    half = lat_count * PAIRS
    index = lax.axis_index("lat")
    padded = jnp.pad(
        order_slots.reshape(lat_count, ord_dev), ((0, 0), (0, PAD - ord_dev)), constant_values=NO_ORDER
    )
    mine = lax.dynamic_slice_in_dim(padded, index, 1, 0).reshape(PAD)
    by_pair = padded.reshape(lat_count, PAIRS, 2).transpose(2, 0, 1).astype(f32)
    index = index.reshape(1)

    weights = lax.all_gather(jnp.transpose(mix_weight, (0, 3, 2, 1)), "ch", axis=0)
    rows = call_forward(lat_count, index, by_pair.reshape(1, 2 * half), field_in)
    rows = lax.all_to_all(rows, "lat", 0, 0, tiled=True)
    order_rows = jnp.broadcast_to(mine.astype(f32)[:, None], (PAD, LANES))
    legendre = call_legendre(lat_count, lat_dev, modes, order_rows)
    order_rows = jnp.broadcast_to(by_pair.reshape(2 * half, 1), (2 * half, LANES))
    inverse_table = call_inverse_table(lon, order_rows)
    coeffs = call_analysis(ord_dev, mine, rows, legendre)
    coeffs = lax.all_to_all(coeffs.reshape(-1, PAD, LANES), ("lat", "ch"), 0, 0, tiled=True)
    mixed = call_mix(lat_count, coeffs, weights)
    mixed = lax.all_to_all(mixed, ("lat", "ch"), 0, 0, tiled=True)
    synth, spectrum = call_synthesis(ord_dev, lon, mine, mixed.reshape(rows.shape), legendre)
    synth = lax.all_to_all(synth, "lat", 0, 0, tiled=True)
    field_out = call_backward(index, synth, inverse_table, field_in)
    return (field_out, spectrum)


def solution(mesh):
    placed = (P("lat", "ch", None), P(None, None, "ch", "lat"), P())
    return jax.shard_map(
        on_device,
        mesh=mesh,
        in_specs=placed,
        out_specs=(P("lat", "ch", None), P("lat", None, "ch", None)),
        check_vma=False,
    )
```

time: 189 us -> 184 us (0.974)
  local copies, waits for them, and re-layouts: 18.6 us -> 3.43 us
  waiting for transfers between devices: 14.6 us -> 22 us
  blocking collectives: 84.3 us -> 88.1 us
  Pallas kernels: 44.1 us -> 42 us
    unnamed x26 -> x2, local copies, waits for them, and re-layouts: 17 us -> 0.01 us
    all_to_all x1, waiting for transfers between devices: 0.01 us -> 9.06 us  [on_device(): rows = lax.all_to_all(rows, 'lat', 0, 0, tiled=True)]
    pallas_call x7, Pallas kernels: 44.1 us -> 42 us  [the longest x1 8.09 us: call_synthesis(): pl.pallas_call(functools.partial(synthesis_kernel, ord_dev, lon), out_sha...]
    all_to_all x1, blocking collectives: 37.9 us -> 39.9 us  [on_device(): mixed = lax.all_to_all(mixed, ('lat', 'ch'), 0, 0, tiled=True)]
  transfers between devices with their start and end apart: 3 -> 3, of which waited for: 1 -> 2; matrix products, arithmetic and copies ran while one was open for 1% -> 2% of each run, Pallas kernels for 13% -> 12%
where the time goes in v2:
time: 184 us
  blocking collectives  88.1 us (48%)
  Pallas kernels  42 us (23%)
  waiting for transfers between devices  22 us (12%)
  between operations  14.1 us (8%)
  starting transfers between devices  13.8 us (8%)
  local copies, waits for them, and re-layouts  3.43 us (2%)
    all_to_all x1, blocking collectives, on_device(): lax.all_to_all(coeffs.reshape(-1, PAD, LANES), ('lat', 'ch'), 0, 0, tiled...  48.2 us
    all_to_all x1, blocking collectives, on_device(): mixed = lax.all_to_all(mixed, ('lat', 'ch'), 0, 0, tiled=True)  39.9 us
    all_to_all x1, waiting for transfers between devices, on_device(): synth = lax.all_to_all(synth, 'lat', 0, 0, tiled=True)  12.3 us
    all_to_all x1, waiting for transfers between devices, on_device(): rows = lax.all_to_all(rows, 'lat', 0, 0, tiled=True)  9.06 us
    all_to_all x1, starting transfers between devices, on_device(): rows = lax.all_to_all(rows, 'lat', 0, 0, tiled=True)  8.66 us
    pallas_call x1, Pallas kernels, call_synthesis(): pl.pallas_call(functools.partial(synthesis_kernel, ord_dev, lon), out_sha...  8.09 us
    pallas_call x1, Pallas kernels, call_legendre(): pl.pallas_call(functools.partial(legendre_kernel, ord_dev), out_shape=jax...  7.01 us
    pallas_call x1, Pallas kernels, call_mix(): pl.pallas_call(functools.partial(mix_kernel, lat_count, ch_count, ord_dev...  6.93 us
  transfers between devices with their start and end apart: 3, of which 2 were waited for; matrix products, arithmetic and copies ran while one was open for 2% of the time, Pallas kernels for 12%

profile of v2, /device:TPU:1, one launch (start us, length us, event | category | flops | bytes accessed | tf_op | source)
XLA Modules:
  0.0 183.5 jit_solution(6800106454903031501)
XLA Ops:
  7.2 0.0 all-gather.3.cloned.1.call-start
  7.2 0.7 all-gather.3.cloned.1.call-update
  7.9 0.8 reshape.35
  8.7 0.1 copy.19
  8.8 0.1 copy.20
  8.9 0.7 reshape.37.order_ref
  9.6 4.6 %forward.1 = bf16[32,8,16,128]{3,2,1,0:T(8,128)(2,1)} custom-call(s32[1]{0:T(128)} %bitcast.index_ref, f32[1,512]{1,0:T(1,128)} %reshape.37.order_ref, bf16[15,32,1024]{2,1,0:T(8,128)(2,1)} %field_hbm.3), custom_call_target="tpu_custom_call" | custom-call | tf_op jit(solution)/shard_map/forward/pallas_call | solution.py:394
  14.2 8.7 %all-to-all-start = ((bf16[32,8,16,128]{3,2,1,0:T(8,128)(2,1)}), bf16[32,8,16,128]{3,2,1,0:T(8,128)(2,1)}, u32[]{:S(2)}, u32[]{:S(2)}) async-start(bf16[32,8,16,128]{3,2,1,0:T(8,128)(2,1)} %forward.1), calls=%async_computation | async-start | bytes 2097152 | tf_op jit(solution)/shard_map/all_to_all | solution.py:555
  22.8 0.2 dynamic-slice_reduce_fusion.order_ref
  23.0 0.0 copy-start
  23.0 0.7 broadcast_in_dim.6.order_ref
  23.7 7.0 %legendre.1 = bf16[16,32,16,256]{3,2,1,0:T(8,128)(2,1)} custom-call(f32[2,480]{1,0:T(2,128)} %constant.20.clone.scale_ref, f32[16,128]{1,0:T(8,128)} %broadcast_in_dim.6.order_ref, f32[2,256]{1,0:T(2,128)} %constant.21.clone.geo_ref, f32[1,512]{1,0:T(1,128)} %constant.22.clone.prod_ref), custom_call_target="tpu_custom_call" | custom-call | flops 8000000000 | bytes 20000000 | tf_op jit(solution)/shard_map/legendre/pallas_call | solution.py:432
  30.7 0.0 copy-done
  30.7 9.1 %all-to-all-done.rows_ref = bf16[32,8,16,128]{3,2,1,0:T(8,128)(2,1)} async-done(((bf16[32,8,16,128]{3,2,1,0:T(8,128)(2,1)}), bf16[32,8,16,128]{3,2,1,0:T(8,128)(2,1)}, u32[]{:S(2)}, u32[]{:S(2)}) %all-to-all-start) | async-done | bytes 1048608 | tf_op jit(solution)/shard_map/all_to_all | solution.py:555
  39.8 5.8 %analysis.1 = bf16[32,8,16,128]{3,2,1,0:T(8,128)(2,1)} custom-call(s32[16]{0:T(128)} %copy-done, bf16[32,8,16,128]{3,2,1,0:T(8,128)(2,1)} %all-to-all-done.rows_ref, bf16[16,512,256]{2,1,0:T(8,128)(2,1)} %bitcast.9), custom_call_target="tpu_custom_call" | custom-call | tf_op jit(solution)/shard_map/analysis/pallas_call | solution.py:468
  45.6 48.2 %all_to_all.20.coef_ref = bf16[256,16,128]{2,1,0:T(8,128)(2,1)} all-to-all(bf16[256,16,128]{2,1,0:T(8,128)(2,1)} %bitcast.11), channel_id=1, replica_groups=mesh['lat'=32,'ch'=8] {'lat','ch'}, dimensions={0} | all-to-all | bytes 2097152 | tf_op jit(solution)/shard_map/all_to_all | solution.py:561
  93.8 0.0 all-gather.3.cloned.1.call-done
  93.8 6.9 %mix.1 = bf16[256,16,128]{2,1,0:T(8,128)(2,1)} custom-call(bf16[256,16,128]{2,1,0:T(8,128)(2,1)} %all_to_all.20.coef_ref, bf16[8,2,15,32,256]{4,3,2,1,0:T(8,128)(2,1)} %bitcast.13), custom_call_target="tpu_custom_call" | custom-call | tf_op jit(solution)/shard_map/mix/pallas_call | solution.py:481
  100.7 39.9 %all_to_all.21 = bf16[256,16,128]{2,1,0:T(8,128)(2,1)} all-to-all(bf16[256,16,128]{2,1,0:T(8,128)(2,1)} %mix.1), channel_id=1, replica_groups=mesh['lat'=32,'ch'=8] {'lat','ch'}, dimensions={0} | all-to-all | bytes 2097152 | tf_op jit(solution)/shard_map/all_to_all | solution.py:563
  140.6 8.1 %synthesis.1 = (bf16[32,8,16,128]{3,2,1,0:T(8,128)(2,1)}, bf16[15,2,32,480]{3,2,1,0:T(8,128)(2,1)}) custom-call(s32[16]{0:T(128)} %copy-done, bf16[32,8,16,128]{3,2,1,0:T(8,128)(2,1)} %bitcast.12, bf16[512,480]{1,0:T(8,128)(2,1)} %constant.23.clone.pick_ref, bf16[16,512,256]{2,1,0:T(8,128)(2,1)} %bitcast.10), custom_call_target="tpu_custom_call" | custom-call | tf_op jit(solution)/shard_map/synthesis/pallas_call | solution.py:504
  148.7 5.1 %all-to-all-start.3 = ((bf16[32,8,16,128]{3,2,1,0:T(8,128)(2,1)}), bf16[32,8,16,128]{3,2,1,0:T(8,128)(2,1)}, u32[]{:S(2)}, u32[]{:S(2)}) async-start(bf16[32,8,16,128]{3,2,1,0:T(8,128)(2,1)} %get-tuple-element.4), calls=%async_computation.3 | async-start | bytes 2097152 | tf_op jit(solution)/shard_map/all_to_all | solution.py:565
  153.8 0.1 broadcast_in_dim.14
  153.9 0.8 broadcast_in_dim.15.order_ref
  154.8 3.8 %inverse_table.1.table_hbm = bf16[1024,1024]{1,0:T(8,128)(2,1)} custom-call(f32[512,128]{1,0:T(8,128)} %broadcast_in_dim.15.order_ref), custom_call_target="tpu_custom_call" | custom-call | flops 2000000000 | bytes 4000000 | tf_op jit(solution)/shard_map/inverse_table/pallas_call | solution.py:452
  158.6 12.3 %all-to-all-done.3.rows_ref = bf16[32,8,16,128]{3,2,1,0:T(8,128)(2,1)} async-done(((bf16[32,8,16,128]{3,2,1,0:T(8,128)(2,1)}), bf16[32,8,16,128]{3,2,1,0:T(8,128)(2,1)}, u32[]{:S(2)}, u32[]{:S(2)}) %all-to-all-start.3) | async-done | bytes 1048608 | tf_op jit(solution)/shard_map/all_to_all | solution.py:565
  170.9 5.8 %backward.1 = bf16[15,32,1024]{2,1,0:T(8,128)(2,1)} custom-call(s32[1]{0:T(128)} %bitcast.index_ref, bf16[32,8,16,128]{3,2,1,0:T(8,128)(2,1)} %all-to-all-done.3.rows_ref, bf16[1024,1024]{1,0:T(8,128)(2,1)} %inverse_table.1.table_hbm, bf16[15,32,1024]{2,1,0:T(8,128)(2,1)} %field_hbm.3), custom_call_target="tpu_custom_call" | custom-call | tf_op jit(solution)/shard_map/backward/pallas_call | solution.py:522
  (2 shorter events, 0.0 us)
Async XLA Ops:
  7.2 86.6 %all-gather.3.cloned.1.call-start = ((), (), s32[]{:S(2)}) async-start(), calls=%async_computation.4 | async-start | bytes 4423680 | tf_op jit(solution)/shard_map/all_gather | solution.py:553
  14.2 25.6 %all-to-all-start = ((bf16[32,8,16,128]{3,2,1,0:T(8,128)(2,1)}), bf16[32,8,16,128]{3,2,1,0:T(8,128)(2,1)}, u32[]{:S(2)}, u32[]{:S(2)}) async-start(bf16[32,8,16,128]{3,2,1,0:T(8,128)(2,1)} %forward.1), calls=%async_computation | async-start | bytes 2097152 | tf_op jit(solution)/shard_map/all_to_all | solution.py:555
  23.0 7.7 %copy-start = (s32[16]{0:T(128)}, s32[16]{0:T(128)S(1)}, u32[]{:S(2)}) copy-start(s32[16]{0:T(128)S(1)} %dynamic-slice_reduce_fusion.order_ref) | copy-start | bytes 196
  148.7 22.2 %all-to-all-start.3 = ((bf16[32,8,16,128]{3,2,1,0:T(8,128)(2,1)}), bf16[32,8,16,128]{3,2,1,0:T(8,128)(2,1)}, u32[]{:S(2)}, u32[]{:S(2)}) async-start(bf16[32,8,16,128]{3,2,1,0:T(8,128)(2,1)} %get-tuple-element.4), calls=%async_computation.3 | async-start | bytes 2097152 | tf_op jit(solution)/shard_map/all_to_all | solution.py:565
Sparse Core Ops, SparseCore 0:
  9.8 67.3 all-gather.2

commit v3 on v2

--- a/solution.py
+++ b/solution.py
@@ -19,8 +19,8 @@
 bf16 = jnp.bfloat16
 
 
-VMEM_MIB = 57
-TABLE_MIB = 63
+VMEM_MIB = 50
+TABLE_MIB = 57
 
 
 def cos_turns(turns):
@@ -56,16 +56,66 @@
     return out
 
 
+def digits_of(slots_ref):
+    slots = slots_ref[...].astype(f32)
+    high = jnp.floor(slots * (1.0 / PAD))
+    return high.astype(bf16), (slots - PAD * high).astype(bf16)
+
+
+def one_hot(hit):
+    return jnp.where(hit, 1.0, 0.0).astype(bf16)
+
+
+def slot_wanted(place, ord_dev, half):
+    within = 2 * (place % PAIRS) + place // half
+    return jnp.where(within < ord_dev, (place % half) // PAIRS * ord_dev + within, -1)
+
+
+def order_lanes(slots_ref, ord_dev, lat_count):
+    modes = slots_ref.shape[1]
+    half = lat_count * PAIRS
+    wanted = slot_wanted(lax.broadcasted_iota(jnp.int32, (1, 2 * half), 1), ord_dev, half)
+    pick = one_hot(lax.broadcasted_iota(jnp.int32, (modes, 2 * half), 0) == wanted)
+    digits = [jnp.broadcast_to(d.astype(f32), (8, modes)).astype(bf16) for d in digits_of(slots_ref)]
+    high, low = [jnp.dot(d, pick, preferred_element_type=f32) for d in digits]
+    return high[0:1] * PAD + low[0:1]
+
+
+def order_rows(slots_ref, ord_dev, lat_count):
+    modes = slots_ref.shape[1]
+    half = lat_count * PAIRS
+    wanted = slot_wanted(lax.broadcasted_iota(jnp.int32, (2 * half, 1), 0), ord_dev, half)
+    pick = one_hot(lax.broadcasted_iota(jnp.int32, (2 * half, modes), 1) == wanted)
+    contract = (((1,), (1,)), ((), ()))
+    high, low = [
+        lax.dot_general(
+            pick,
+            jnp.broadcast_to(d.astype(f32), (LANES, modes)).astype(bf16),
+            contract,
+            preferred_element_type=f32,
+        )
+        for d in digits_of(slots_ref)
+    ]
+    return high * PAD + low
+
+
+def order_column(slots, wanted):
+    place = lax.broadcasted_iota(jnp.int32, (wanted.shape[0], slots.shape[1]), 1)
+    return jnp.sum(jnp.where(place == wanted, slots, 0.0), axis=1, keepdims=True)
+
+
 def slot_of(j, lat_dev, index, lat_count):
     return jnp.where(index < lat_count // 2, j, lat_dev - 1 - j)
 
 
-def forward_kernel(lat_dev, lat_count, index_ref, order_ref, field_hbm, out_ref, table, field_ref, rows, turned, sem):
+def forward_kernel(
+    lat_dev, lat_count, ord_dev, index_ref, slots_ref, field_hbm, out_hbm, table, field_ref, rows, turned, out_ref, sem, sems
+):
     fetch = pltpu.make_async_copy(field_hbm, field_ref, sem)
     fetch.start()
     lon = table.shape[0]
     half = table.shape[1] // 4
-    order = order_ref[...]
+    order = order_lanes(slots_ref, ord_dev, lat_count)
     step_cos = cos_turns(order * (LANES / lon))
     step_sin = -minus_sin_turns(order * (LANES / lon))
 
@@ -96,19 +146,29 @@
         block = rows[j].reshape(4 * ch_dev, half) * quad
         turned[pl.ds(slot_of(j, lat_dev, index, lat_count), half, stride=PITCH), :] = block.T
     turned[pl.ds(lat_dev, half, stride=PITCH), :] = jnp.zeros((half, LANES), f32)
-    for i in range(half):
-        tile = turned[i * PITCH : i * PITCH + PAD, :]
-        out_ref[i // PAIRS, i % PAIRS] = tile.astype(bf16)
-
-
-def inverse_table_kernel(order_ref, out_hbm, out_ref, sem):
+    copies = []
+    part = lat_count // sems.shape[0]
+    for d in range(lat_count):
+        for p in range(PAIRS):
+            i = d * PAIRS + p
+            out_ref[d, p] = turned[i * PITCH : i * PITCH + PAD, :].astype(bf16)
+        if d % part == part - 1:
+            cut = slice(d + 1 - part, d + 1)
+            copies.append(pltpu.make_async_copy(out_ref.at[cut], out_hbm.at[cut], sems.at[d // part]))
+            copies[-1].start()
+    for copy in copies:
+        copy.wait()
+
+
+def inverse_table_kernel(ord_dev, lat_count, slots_ref, out_hbm, out_ref, orders, sem):
     lon = out_ref.shape[1]
     half = out_ref.shape[0] // 4
     steps = half // PAD
+    orders[...] = order_rows(slots_ref, ord_dev, lat_count)
 
     @pl.loop(0, 2 * steps)
     def _(r):
-        order = order_ref[pl.ds(pl.multiple_of(r * PAD, PAD), PAD), :]
+        order = orders[pl.ds(pl.multiple_of(r * PAD, PAD), PAD), :]
         step_cos = cos_turns(order * (LANES / lon))
         step_sin = -minus_sin_turns(order * (LANES / lon))
         n = lax.broadcasted_iota(jnp.int32, (PAD, LANES), 1).astype(f32)
@@ -127,13 +187,15 @@
 
 
 def legendre_kernel(
-    deg_dev, scale_ref, order_ref, geo_ref, prod_ref, out_hbm, cur, bef, resc, start, expo, root, buf, table, sems
+    deg_dev, index_ref, scale_ref, slots_ref, geo_ref, prod_ref, out_hbm, cur, bef, resc, start, expo, root, buf, table, sems
 ):
     groups = cur.shape[0]
     log_step = RESCALE_BITS * math.log(2.0)
     shrink = 2.0 ** (-RESCALE_BITS)
     limit = 2.0**RESCALE_BITS
-    order = order_ref[...]
+    row = lax.broadcasted_iota(jnp.int32, (PAD, 1), 0)
+    order = order_column(slots_ref[...].astype(f32), jnp.where(row < deg_dev, index_ref[0] * deg_dev + row, -1))
+    order = jnp.broadcast_to(jnp.where(row < deg_dev, order, 1.0 * NO_ORDER), (PAD, LANES))
     order_sq = order * order
     for state in (cur, bef, resc, root):
         state[...] = jnp.zeros_like(state)
@@ -207,6 +269,10 @@
     return ((i // PAD) * ord_dev + i % PAD) & 1
 
 
+def order_of(slots_ref, index_ref, ord_dev, m):
+    return slots_ref[index_ref[0] * ord_dev + jnp.minimum(m, ord_dev - 1)]
+
+
 def fetch_pairs(table_hbm, table, sems):
     def copy(p):
         cut = pl.ds(2 * p, 2)
@@ -217,7 +283,7 @@
     return copy
 
 
-def analysis_kernel(ord_dev, order_ref, rows_ref, table_hbm, out_ref, table, sems):
+def analysis_kernel(ord_dev, index_ref, slots_ref, rows_ref, table_hbm, out_ref, table, sems):
     copy = fetch_pairs(table_hbm, table, sems)
     count = rows_ref.shape[0]
     parity = degree_parity((table.shape[1], LANES), 0, ord_dev)
@@ -230,7 +296,7 @@
         copy(p).wait()
         parts = []
         for m2 in range(2):
-            order = order_ref[2 * p + m2]
+            order = order_of(slots_ref, index_ref, ord_dev, 2 * p + m2)
             prod = jnp.dot(table[2 * p + m2], both, preferred_element_type=f32)
             mirror = prod[:, LANES:]
             parts.append(prod[:, :LANES] + jnp.where(parity == (order & 1), mirror, -mirror))
@@ -301,29 +367,19 @@
         out_ref[d * ch_count : (d + 1) * ch_count] = part.reshape(ch_count, PAD, LANES)
 
 
-def synthesis_kernel(
-    ord_dev, lon, order_ref, mixed_ref, pick_ref, table_hbm, out_ref, spec_ref, table, sems
-):
+def synthesis_kernel(ord_dev, lon, index_ref, slots_ref, mixed_ref, table_hbm, out_ref, table, sems):
     copy = fetch_pairs(table_hbm, table, sems)
     count = out_ref.shape[0]
     half = LANES // 2
-    shape = spec_ref.shape[1:]
     parity = degree_parity((half, table.shape[1]), 1, ord_dev)
 
     @pl.loop(0, PAIRS)
     def _(p):
         side = jnp.concatenate([mixed_ref[d, p] for d in range(count)], axis=0).astype(f32).T
-        spec = jnp.dot(side.astype(bf16), pick_ref[...], preferred_element_type=f32).astype(bf16)
-        spec_ref[2 * p] = spec[:half].reshape(shape)
-
-        @pl.when(2 * p + 1 < ord_dev)
-        def _():
-            spec_ref[2 * p + 1] = spec[half:].reshape(shape)
-
         copy(p).wait()
         north, south = [], []
         for m2 in range(2):
-            order = order_ref[2 * p + m2]
+            order = order_of(slots_ref, index_ref, ord_dev, 2 * p + m2)
             weight = jnp.where(order == 0, 1.0 / lon, 2.0 / lon)
             part = side[m2 * half : (m2 + 1) * half]
             same = parity == (order & 1)
@@ -336,6 +392,23 @@
         for s in range(count // 2):
             out_ref[s, p] = up[s * PAD : (s + 1) * PAD]
             out_ref[count - 1 - s, p] = down[s * PAD : (s + 1) * PAD]
+
+
+def spectrum_kernel(ord_dev, mixed_ref, pick_ref, out_ref):
+    count = mixed_ref.shape[0]
+    half = LANES // 2
+    shape = out_ref.shape[1:]
+
+    @pl.loop(0, PAIRS)
+    def _(p):
+        rows = jnp.concatenate([mixed_ref[d, p] for d in range(count)], axis=0)
+        side = rows.astype(f32).T.astype(bf16)
+        spec = jnp.dot(side, pick_ref[...], preferred_element_type=f32).astype(bf16)
+        out_ref[2 * p] = spec[:half].reshape(shape)
+
+        @pl.when(2 * p + 1 < ord_dev)
+        def _():
+            out_ref[2 * p + 1] = spec[half:].reshape(shape)
 
 
 def backward_kernel(
@@ -388,28 +461,31 @@
     return jax.ShapeDtypeStruct((lat_count, PAIRS, PAD, LANES), bf16)
 
 
-def call_forward(lat_count, index, order_lanes, field_in):
+def call_forward(lat_count, index, slots, field_in):
     lat_dev, ch_dev, lon = field_in.shape
     half = lat_count * PAIRS
     return pl.pallas_call(
-        functools.partial(forward_kernel, lat_dev, lat_count),
+        functools.partial(forward_kernel, lat_dev, lat_count, slots.shape[1] // lat_count),
         out_shape=buffer_of(lat_count),
         in_specs=[smem, vmem, hbm],
-        out_specs=vmem,
+        out_specs=hbm,
         scratch_shapes=[
             pltpu.VMEM((lon, 4 * half), bf16),
             pltpu.VMEM(field_in.shape, bf16),
             pltpu.VMEM((lat_dev, 4, ch_dev, half), f32),
             pltpu.VMEM((half * PITCH, LANES), f32),
+            pltpu.VMEM((lat_count, PAIRS, PAD, LANES), bf16),
             pltpu.SemaphoreType.DMA,
+            pltpu.SemaphoreType.DMA((4,)),
         ],
-        compiler_params=params(),
+        compiler_params=params(TABLE_MIB),
         name="forward",
-    )(index, order_lanes, field_in)
-
-
-def call_legendre(lat_count, lat_dev, modes, order_rows):
+    )(index, slots, field_in)
+
+
+def call_legendre(lat_count, lat_dev, index, slots):
     lat_total = lat_count * lat_dev
+    modes = slots.shape[1]
     ord_dev = modes // lat_count
     full = lat_count * PAD
     near = full // 2
@@ -432,7 +508,7 @@
     table = pl.pallas_call(
         functools.partial(legendre_kernel, ord_dev),
         out_shape=jax.ShapeDtypeStruct((PAD, lat_count, PAD, near), bf16),
-        in_specs=[smem, vmem, vmem, vmem],
+        in_specs=[smem, smem, vmem, vmem, vmem],
         out_specs=hbm,
         scratch_shapes=[state] * 5
         + [
@@ -444,36 +520,38 @@
         compiler_params=params(TABLE_MIB),
         cost_estimate=cost(8e9, 2e7),
         name="legendre",
-    )(jnp.asarray(scales), order_rows, jnp.asarray(geo), jnp.asarray(prod))
+    )(index, jnp.asarray(scales), slots, jnp.asarray(geo), jnp.asarray(prod))
     return table.reshape(PAD, full, near)
 
 
-def call_inverse_table(lon, order_rows):
+def call_inverse_table(lat_count, lon, slots):
+    half = lat_count * PAIRS
     return pl.pallas_call(
-        inverse_table_kernel,
-        out_shape=jax.ShapeDtypeStruct((2 * order_rows.shape[0], lon), bf16),
+        functools.partial(inverse_table_kernel, slots.shape[1] // lat_count, lat_count),
+        out_shape=jax.ShapeDtypeStruct((4 * half, lon), bf16),
         in_specs=[vmem],
         out_specs=hbm,
         scratch_shapes=[
-            pltpu.VMEM((2 * order_rows.shape[0], lon), bf16),
+            pltpu.VMEM((4 * half, lon), bf16),
+            pltpu.VMEM((2 * half, LANES), f32),
             pltpu.SemaphoreType.DMA,
         ],
         compiler_params=params(TABLE_MIB),
         cost_estimate=cost(2e9, 4e6),
         name="inverse_table",
-    )(order_rows)
-
-
-def call_analysis(ord_dev, orders, rows, table):
+    )(slots)
+
+
+def call_analysis(ord_dev, index, orders, rows, table):
     return pl.pallas_call(
         functools.partial(analysis_kernel, ord_dev),
         out_shape=jax.ShapeDtypeStruct(rows.shape, bf16),
-        in_specs=[smem, vmem, hbm],
+        in_specs=[smem, smem, vmem, hbm],
         out_specs=vmem,
         scratch_shapes=[pltpu.VMEM(table.shape, bf16), pltpu.SemaphoreType.DMA((PAIRS,))],
         compiler_params=params(),
         name="analysis",
-    )(orders, rows, table)
+    )(index, orders, rows, table)
 
 
 def call_mix(lat_count, coeffs, weights):
@@ -493,26 +571,33 @@
     )(coeffs, weights)
 
 
-def call_synthesis(ord_dev, lon, orders, mixed, table):
-    lat_count = mixed.shape[0]
-    modes = ord_dev * lat_count
-    full = lat_count * PAD
-    ch_dev = LANES // 4
-    pick = np.zeros((lat_count, PAD, modes), np.float32)
-    pick[:, :ord_dev] = np.eye(modes, dtype=np.float32).reshape(lat_count, ord_dev, modes)
-    pick = jnp.asarray(pick.reshape(full, modes), bf16)
+def call_synthesis(ord_dev, lon, index, orders, mixed, table):
     return pl.pallas_call(
         functools.partial(synthesis_kernel, ord_dev, lon),
-        out_shape=(
-            buffer_of(lat_count),
-            jax.ShapeDtypeStruct((ord_dev, 2, ch_dev, modes), bf16),
-        ),
-        in_specs=[smem, vmem, vmem, hbm],
-        out_specs=(vmem, vmem),
+        out_shape=buffer_of(mixed.shape[0]),
+        in_specs=[smem, smem, vmem, hbm],
+        out_specs=vmem,
         scratch_shapes=[pltpu.VMEM(table.shape, bf16), pltpu.SemaphoreType.DMA((PAIRS,))],
         compiler_params=params(),
         name="synthesis",
-    )(orders, mixed, pick, table)
+    )(index, orders, mixed, table)
+
+
+def call_spectrum(ord_dev, mixed):
+    lat_count = mixed.shape[0]
+    modes = ord_dev * lat_count
+    pick = np.zeros((lat_count, PAD, modes), np.float32)
+    pick[:, :ord_dev] = np.eye(modes, dtype=np.float32).reshape(lat_count, ord_dev, modes)
+    pick = jnp.asarray(pick.reshape(lat_count * PAD, modes), bf16)
+    return pl.pallas_call(
+        functools.partial(spectrum_kernel, ord_dev),
+        out_shape=jax.ShapeDtypeStruct((ord_dev, 2, LANES // 4, modes), bf16),
+        in_specs=[vmem, vmem],
+        out_specs=vmem,
+        compiler_params=params(),
+        cost_estimate=cost(3e9, 4e6),
+        name="spectrum",
+    )(mixed, pick)
 
 
 def call_backward(index, rows, table, field_in):
@@ -541,28 +626,22 @@
     lat_count = lax.axis_size("lat")
     modes = order_slots.shape[0]
     ord_dev = modes // lat_count
-    half = lat_count * PAIRS
     index = lax.axis_index("lat")
-    padded = jnp.pad(
-        order_slots.reshape(lat_count, ord_dev), ((0, 0), (0, PAD - ord_dev)), constant_values=NO_ORDER
-    )
-    mine = lax.dynamic_slice_in_dim(padded, index, 1, 0).reshape(PAD)
-    by_pair = padded.reshape(lat_count, PAIRS, 2).transpose(2, 0, 1).astype(f32)
     index = index.reshape(1)
+    slots = order_slots.reshape(1, modes)
 
     weights = lax.all_gather(jnp.transpose(mix_weight, (0, 3, 2, 1)), "ch", axis=0)
-    rows = call_forward(lat_count, index, by_pair.reshape(1, 2 * half), field_in)
+    rows = call_forward(lat_count, index, slots, field_in)
     rows = lax.all_to_all(rows, "lat", 0, 0, tiled=True)
-    order_rows = jnp.broadcast_to(mine.astype(f32)[:, None], (PAD, LANES))
-    legendre = call_legendre(lat_count, lat_dev, modes, order_rows)
-    order_rows = jnp.broadcast_to(by_pair.reshape(2 * half, 1), (2 * half, LANES))
-    inverse_table = call_inverse_table(lon, order_rows)
-    coeffs = call_analysis(ord_dev, mine, rows, legendre)
+    legendre = call_legendre(lat_count, lat_dev, index, slots)
+    coeffs = call_analysis(ord_dev, index, order_slots, rows, legendre)
     coeffs = lax.all_to_all(coeffs.reshape(-1, PAD, LANES), ("lat", "ch"), 0, 0, tiled=True)
     mixed = call_mix(lat_count, coeffs, weights)
-    mixed = lax.all_to_all(mixed, ("lat", "ch"), 0, 0, tiled=True)
-    synth, spectrum = call_synthesis(ord_dev, lon, mine, mixed.reshape(rows.shape), legendre)
+    mixed = lax.all_to_all(mixed, ("lat", "ch"), 0, 0, tiled=True).reshape(rows.shape)
+    synth = call_synthesis(ord_dev, lon, index, order_slots, mixed, legendre)
     synth = lax.all_to_all(synth, "lat", 0, 0, tiled=True)
+    spectrum = call_spectrum(ord_dev, mixed)
+    inverse_table = call_inverse_table(lat_count, lon, slots)
     field_out = call_backward(index, synth, inverse_table, field_in)
     return (field_out, spectrum)
 

time: 184 us -> 176 us (0.957)
  Pallas kernels: 42 us -> 38.2 us
  local copies, waits for them, and re-layouts: 3.43 us -> 0.02 us
    all_to_all x1, blocking collectives: 48.2 us -> 51.9 us  [on_device(): lax.all_to_all(coeffs.reshape(-1, PAD, LANES), ('lat', 'ch'), 0, 0, tiled...]
    pallas_call x2 -> x3, Pallas kernels: 8.41 us -> 11.9 us  [the longest x1 4.64 us: call_forward(): pl.pallas_call(functools.partial(forward_kernel, lat_dev, lat_count, slot...]
    all_to_all x1, waiting for transfers between devices: 12.3 us -> 9.66 us  [on_device(): synth = lax.all_to_all(synth, 'lat', 0, 0, tiled=True)]
    pallas_call x1, Pallas kernels: 6.93 us -> 4.74 us  [call_mix(): pl.pallas_call(functools.partial(mix_kernel, lat_count, ch_count, ord_dev...]
    pallas_call x1, Pallas kernels: 8.09 us -> 6 us  [call_synthesis(): pl.pallas_call(functools.partial(synthesis_kernel, ord_dev, lon), out_sha...]
    all_to_all x1, blocking collectives: 39.9 us -> 38 us  [on_device(): lax.all_to_all(mixed, ('lat', 'ch'), 0, 0, tiled=True).reshape(rows.shape)]
  transfers between devices with their start and end apart: 3 -> 3, of which waited for: 2 -> 2; matrix products, arithmetic and copies ran while one was open for 2% -> 0% of each run, Pallas kernels for 12% -> 13%
where the time goes in v3:
time: 176 us
  blocking collectives  89.9 us (51%)
  Pallas kernels  38.2 us (22%)
  waiting for transfers between devices  20.2 us (11%)
  between operations  14.1 us (8%)
  starting transfers between devices  13.1 us (7%)
    all_to_all x1, blocking collectives, on_device(): lax.all_to_all(coeffs.reshape(-1, PAD, LANES), ('lat', 'ch'), 0, 0, tiled...  51.9 us
    all_to_all x1, blocking collectives, on_device(): lax.all_to_all(mixed, ('lat', 'ch'), 0, 0, tiled=True).reshape(rows.shape)  38 us
    all_to_all x1, waiting for transfers between devices, on_device(): rows = lax.all_to_all(rows, 'lat', 0, 0, tiled=True)  9.82 us
    all_to_all x1, waiting for transfers between devices, on_device(): synth = lax.all_to_all(synth, 'lat', 0, 0, tiled=True)  9.66 us
    all_to_all x1, starting transfers between devices, on_device(): rows = lax.all_to_all(rows, 'lat', 0, 0, tiled=True)  8.6 us
    pallas_call x1, Pallas kernels, call_legendre(): pl.pallas_call(functools.partial(legendre_kernel, ord_dev), out_shape=jax...  7.07 us
    pallas_call x1, Pallas kernels, call_synthesis(): pl.pallas_call(functools.partial(synthesis_kernel, ord_dev, lon), out_sha...  6 us
    pallas_call x1, Pallas kernels, call_mix(): pl.pallas_call(functools.partial(mix_kernel, lat_count, ch_count, ord_dev...  4.74 us
  transfers between devices with their start and end apart: 3, of which 2 were waited for; matrix products, arithmetic and copies ran while one was open for 0% of the time, Pallas kernels for 13%

profile of v3, /device:TPU:1, one launch (start us, length us, event | category | flops | bytes accessed | tf_op | source)
XLA Modules:
  0.0 175.5 jit_solution(1834967406916380843)
XLA Ops:
  7.2 0.0 all-gather.3.cloned.1.call-start
  7.2 0.7 all-gather.3.cloned.1.call-update
  7.9 4.6 %forward.1 = bf16[32,8,16,128]{3,2,1,0:T(8,128)(2,1)} custom-call(s32[1]{0:T(128)} %bitcast.index_ref, s32[1,480]{1,0:T(1,128)} %bitcast.10, bf16[15,32,1024]{2,1,0:T(8,128)(2,1)} %field_hbm.3), custom_call_target="tpu_custom_call" | custom-call | tf_op jit(solution)/shard_map/forward/pallas_call | solution.py:467
  12.5 8.6 %all-to-all-start = ((bf16[32,8,16,128]{3,2,1,0:T(8,128)(2,1)}), bf16[32,8,16,128]{3,2,1,0:T(8,128)(2,1)S(1)}, u32[]{:S(2)}, u32[]{:S(2)}) async-start(bf16[32,8,16,128]{3,2,1,0:T(8,128)(2,1)} %forward.1), calls=%async_computation | async-start | bytes 2097152 | tf_op jit(solution)/shard_map/all_to_all | solution.py:635
  21.2 0.0 copy-start.1
  21.2 7.1 %legendre.1 = bf16[16,32,16,256]{3,2,1,0:T(8,128)(2,1)} custom-call(s32[1]{0:T(128)} %bitcast.index_ref, f32[2,480]{1,0:T(2,128)} %constant.14.clone.scale_ref, s32[1,480]{1,0:T(1,128)} %bitcast.11, f32[2,256]{1,0:T(2,128)} %constant.15.clone.geo_ref, f32[1,512]{1,0:T(1,128)} %constant.16.clone.prod_ref), custom_call_target="tpu_custom_call" | custom-call | flops 8000000000 | bytes 20000000 | tf_op jit(solution)/shard_map/legendre/pallas_call | solution.py:508
  28.2 9.8 %all-to-all-done.rows_ref = bf16[32,8,16,128]{3,2,1,0:T(8,128)(2,1)S(1)} async-done(((bf16[32,8,16,128]{3,2,1,0:T(8,128)(2,1)}), bf16[32,8,16,128]{3,2,1,0:T(8,128)(2,1)S(1)}, u32[]{:S(2)}, u32[]{:S(2)}) %all-to-all-start) | async-done | bytes 1048608 | tf_op jit(solution)/shard_map/all_to_all | solution.py:635
  38.1 0.0 copy-done.1
  38.1 4.2 %analysis.1 = bf16[32,8,16,128]{3,2,1,0:T(8,128)(2,1)S(1)} custom-call(s32[1]{0:T(128)} %bitcast.index_ref, s32[480]{0:T(512)S(1)} %copy-done.1, bf16[32,8,16,128]{3,2,1,0:T(8,128)(2,1)S(1)} %all-to-all-done.rows_ref, bf16[16,512,256]{2,1,0:T(8,128)(2,1)} %bitcast.13), custom_call_target="tpu_custom_call" | custom-call | tf_op jit(solution)/shard_map/analysis/pallas_call | solution.py:546
  42.3 51.9 %all_to_all.20.coef_ref = bf16[256,16,128]{2,1,0:T(8,128)(2,1)S(1)} all-to-all(bf16[256,16,128]{2,1,0:T(8,128)(2,1)S(1)} %bitcast.9), channel_id=1, replica_groups=mesh['lat'=32,'ch'=8] {'lat','ch'}, dimensions={0} | all-to-all | bytes 2097152 | tf_op jit(solution)/shard_map/all_to_all | solution.py:638
  94.2 0.0 all-gather.3.cloned.1.call-done
  94.2 4.7 %mix.1 = bf16[256,16,128]{2,1,0:T(8,128)(2,1)S(1)} custom-call(bf16[256,16,128]{2,1,0:T(8,128)(2,1)S(1)} %all_to_all.20.coef_ref, bf16[8,2,15,32,256]{4,3,2,1,0:T(8,128)(2,1)} %bitcast.15), custom_call_target="tpu_custom_call" | custom-call | tf_op jit(solution)/shard_map/mix/pallas_call | solution.py:559
  98.9 38.0 %all_to_all.21 = bf16[256,16,128]{2,1,0:T(8,128)(2,1)S(1)} all-to-all(bf16[256,16,128]{2,1,0:T(8,128)(2,1)S(1)} %mix.1), channel_id=1, replica_groups=mesh['lat'=32,'ch'=8] {'lat','ch'}, dimensions={0} | all-to-all | bytes 2097152 | tf_op jit(solution)/shard_map/all_to_all | solution.py:640
  137.0 6.0 %synthesis.1 = bf16[32,8,16,128]{3,2,1,0:T(8,128)(2,1)} custom-call(s32[1]{0:T(128)} %bitcast.index_ref, s32[480]{0:T(512)S(1)} %copy-done.1, bf16[32,8,16,128]{3,2,1,0:T(8,128)(2,1)S(1)} %bitcast.7, bf16[16,512,256]{2,1,0:T(8,128)(2,1)} %bitcast.14), custom_call_target="tpu_custom_call" | custom-call | tf_op jit(solution)/shard_map/synthesis/pallas_call | solution.py:575
  143.0 4.4 %all-to-all-start.3 = ((bf16[32,8,16,128]{3,2,1,0:T(8,128)(2,1)}), bf16[32,8,16,128]{3,2,1,0:T(8,128)(2,1)S(1)}, u32[]{:S(2)}, u32[]{:S(2)}) async-start(bf16[32,8,16,128]{3,2,1,0:T(8,128)(2,1)} %synthesis.1), calls=%async_computation.3 | async-start | bytes 2097152 | tf_op jit(solution)/shard_map/all_to_all | solution.py:642
  147.4 0.0 copy-start.2
  147.4 4.1 %inverse_table.1.table_hbm = bf16[1024,1024]{1,0:T(8,128)(2,1)} custom-call(s32[1,480]{1,0:T(1,128)} %bitcast.12), custom_call_target="tpu_custom_call" | custom-call | flops 2000000000 | bytes 4000000 | tf_op jit(solution)/shard_map/inverse_table/pallas_call | solution.py:529
  151.5 0.0 copy-done.2
  151.5 0.0 copy-start
  151.5 3.2 %spectrum.1 = bf16[15,2,32,480]{3,2,1,0:T(8,128)(2,1)} custom-call(bf16[32,8,16,128]{3,2,1,0:T(8,128)(2,1)S(1)} %bitcast.8, bf16[512,480]{1,0:T(8,128)(2,1)S(1)} %copy-done.2), custom_call_target="tpu_custom_call" | custom-call | flops 3000000000 | bytes 4000000 | tf_op jit(solution)/shard_map/spectrum/pallas_call | solution.py:592
  154.7 9.7 %all-to-all-done.3.rows_ref = bf16[32,8,16,128]{3,2,1,0:T(8,128)(2,1)S(1)} async-done(((bf16[32,8,16,128]{3,2,1,0:T(8,128)(2,1)}), bf16[32,8,16,128]{3,2,1,0:T(8,128)(2,1)S(1)}, u32[]{:S(2)}, u32[]{:S(2)}) %all-to-all-start.3) | async-done | bytes 1048608 | tf_op jit(solution)/shard_map/all_to_all | solution.py:642
  164.4 0.0 copy-done
  164.4 4.2 %backward.1 = bf16[15,32,1024]{2,1,0:T(8,128)(2,1)} custom-call(s32[1]{0:T(128)} %bitcast.index_ref, bf16[32,8,16,128]{3,2,1,0:T(8,128)(2,1)S(1)} %all-to-all-done.3.rows_ref, bf16[1024,1024]{1,0:T(8,128)(2,1)} %inverse_table.1.table_hbm, bf16[15,32,1024]{2,1,0:T(8,128)(2,1)S(1)} %copy-done), custom_call_target="tpu_custom_call" | custom-call | tf_op jit(solution)/shard_map/backward/pallas_call | solution.py:607
Async XLA Ops:
  7.2 87.0 %all-gather.3.cloned.1.call-start = ((), (), s32[]{:S(2)}) async-start(), calls=%async_computation.4 | async-start | bytes 4423680 | tf_op jit(solution)/shard_map/all_gather | solution.py:633
  12.5 25.5 %all-to-all-start = ((bf16[32,8,16,128]{3,2,1,0:T(8,128)(2,1)}), bf16[32,8,16,128]{3,2,1,0:T(8,128)(2,1)S(1)}, u32[]{:S(2)}, u32[]{:S(2)}) async-start(bf16[32,8,16,128]{3,2,1,0:T(8,128)(2,1)} %forward.1), calls=%async_computation | async-start | bytes 2097152 | tf_op jit(solution)/shard_map/all_to_all | solution.py:635
  21.2 16.9 %copy-start.1 = (s32[480]{0:T(512)S(1)}, s32[480]{0:T(512)}, u32[]{:S(2)}) copy-start(s32[480]{0:T(512)} %slots_ref.3) | copy-start | bytes 5764
  143.0 21.4 %all-to-all-start.3 = ((bf16[32,8,16,128]{3,2,1,0:T(8,128)(2,1)}), bf16[32,8,16,128]{3,2,1,0:T(8,128)(2,1)S(1)}, u32[]{:S(2)}, u32[]{:S(2)}) async-start(bf16[32,8,16,128]{3,2,1,0:T(8,128)(2,1)} %synthesis.1), calls=%async_computation.3 | async-start | bytes 2097152 | tf_op jit(solution)/shard_map/all_to_all | solution.py:642
  147.4 4.1 %copy-start.2 = (bf16[512,480]{1,0:T(8,128)(2,1)S(1)}, bf16[512,480]{1,0:T(8,128)(2,1)}, u32[]{:S(2)}) copy-start(bf16[512,480]{1,0:T(8,128)(2,1)} %constant.17.clone.pick_ref) | copy-start | bytes 1474564
  151.5 12.9 %copy-start = (bf16[15,32,1024]{2,1,0:T(8,128)(2,1)S(1)}, bf16[15,32,1024]{2,1,0:T(8,128)(2,1)}, u32[]{:S(2)}) copy-start(bf16[15,32,1024]{2,1,0:T(8,128)(2,1)} %field_hbm.3) | copy-start | bytes 2949124
Sparse Core Ops, SparseCore 0:
  9.8 76.4 all-gather.2

commit v4 on v3

--- a/solution.py
+++ b/solution.py
@@ -190,6 +190,7 @@
     deg_dev, index_ref, scale_ref, slots_ref, geo_ref, prod_ref, out_hbm, cur, bef, resc, start, expo, root, buf, table, sems
 ):
     groups = cur.shape[0]
+    pitch = 2 * PAD + 1
     log_step = RESCALE_BITS * math.log(2.0)
     shrink = 2.0 ** (-RESCALE_BITS)
     limit = 2.0**RESCALE_BITS
@@ -210,17 +211,17 @@
         log_start = head + order * geo_ref[1:2, g * LANES : (g + 1) * LANES]
         start[g] = log_start
         expo[g] = jnp.exp(log_start)
-        buf[g, pl.ds(deg_dev, PAD, stride=PITCH), :] = jnp.zeros((PAD, LANES), f32)
+        for twin in range(2):
+            buf[g, pl.ds(PAD + twin * PAIRS + PAIRS - 1, PAD, stride=pitch), :] = jnp.zeros((PAD, LANES), f32)
 
     def block(index):
-        first = index * deg_dev
         now = [cur[g] for g in range(groups)]
         old = [bef[g] for g in range(groups)]
         factor = [expo[g] for g in range(groups)]
         cosine = [geo_ref[0:1, g * LANES : (g + 1) * LANES] for g in range(groups)]
         root_prev = root[...]
-        for i in range(deg_dev):
-            degree = first + i
+        for twin, i in [(t, k) for t in range(2) for k in range(deg_dev)]:
+            degree = (2 * index + twin) * deg_dev + i
             deg = degree.astype(f32)
             gap = deg * deg - order_sq
             gap_one = jnp.maximum(gap, 1.0)
@@ -233,7 +234,8 @@
             for g in range(groups):
                 new = alpha * (cosine[g] * now[g] - beta * old[g]) + begin
                 old[g], now[g] = now[g], new
-                buf[g, pl.ds(i, PAD, stride=PITCH), :] = new * factor[g]
+                row = i % 2 * PAD + twin * PAIRS + i // 2
+                buf[g, pl.ds(row, PAD, stride=pitch), :] = new * factor[g]
             if i in (deg_dev // 2, deg_dev - 1):
                 for g in range(groups):
                     large = jnp.abs(now[g]) > limit
@@ -249,24 +251,27 @@
             bef[g] = old[g]
             expo[g] = factor[g]
             for m in range(PAD):
-                tile = buf[g, m * PITCH : m * PITCH + PAD, :].astype(bf16)
-                table[m, index, :, g * LANES : (g + 1) * LANES] = tile
+                for side in range(2):
+                    row = m * pitch + side * PAD
+                    tile = buf[g, row : row + PAD, :].astype(bf16)
+                    table[m, side, index, :, g * LANES : (g + 1) * LANES] = tile
 
     parts = sems.shape[0]
-    count = table.shape[1] // parts
+    count = table.shape[2] // parts
     copies = []
     for part in range(parts):
         pl.loop(part * count, (part + 1) * count)(block)
         cut = slice(part * count, (part + 1) * count)
-        copies.append(pltpu.make_async_copy(table.at[:, cut], out_hbm.at[:, cut], sems.at[part]))
+        copies.append(pltpu.make_async_copy(table.at[:, :, cut], out_hbm.at[:, :, cut], sems.at[part]))
         copies[-1].start()
     for copy in copies:
         copy.wait()
 
 
-def degree_parity(shape, dim, ord_dev):
+def degree_parity(shape, dim, deg_dev):
+    half = shape[dim] // 2
     i = lax.broadcasted_iota(jnp.int32, shape, dim)
-    return ((i // PAD) * ord_dev + i % PAD) & 1
+    return ((i % half) // PAIRS * deg_dev + i // half) & 1
 
 
 def order_of(slots_ref, index_ref, ord_dev, m):
@@ -283,9 +288,10 @@
     return copy
 
 
-def analysis_kernel(ord_dev, index_ref, slots_ref, rows_ref, table_hbm, out_ref, table, sems):
+def analysis_kernel(ord_dev, index_ref, slots_ref, rows_ref, table_hbm, out_ref, table, wide, sems):
     copy = fetch_pairs(table_hbm, table, sems)
     count = rows_ref.shape[0]
+    half = count * PAIRS
     parity = degree_parity((table.shape[1], LANES), 0, ord_dev)
 
     @pl.loop(0, PAIRS)
@@ -294,94 +300,88 @@
         south = jnp.concatenate([rows_ref[count - 1 - s, p] for s in range(count // 2)], axis=0)
         both = jnp.concatenate([north, south], axis=1)
         copy(p).wait()
-        parts = []
         for m2 in range(2):
             order = order_of(slots_ref, index_ref, ord_dev, 2 * p + m2)
             prod = jnp.dot(table[2 * p + m2], both, preferred_element_type=f32)
             mirror = prod[:, LANES:]
-            parts.append(prod[:, :LANES] + jnp.where(parity == (order & 1), mirror, -mirror))
-        lane = lax.broadcasted_iota(jnp.int32, parts[0].shape, 1)
-        out = jnp.where(lane < LANES // 2, parts[0], parts[1]).astype(bf16)
-        for d in range(count):
-            out_ref[d, p] = out[d * PAD : (d + 1) * PAD]
-
-
-def mix_kernel(blocks, ch_count, deg_dev, coef_ref, weight_hbm, out_ref, wide, mixed, weight, sems):
-    jump = ch_count * PAD + 1
+            coefs = prod[:, :LANES] + jnp.where(parity == (order & 1), mirror, -mirror)
+            low, high = coefs[:half], coefs[half:]
+            if m2 == 0:
+                high = pltpu.roll(high, LANES // 2, 1)
+            else:
+                low = pltpu.roll(low, LANES // 2, 1)
+            lane = lax.broadcasted_iota(jnp.int32, low.shape, 1)
+            wide[pl.ds(2 * p + m2, half, stride=PITCH), :] = jnp.where(lane < LANES // 2, low, high)
+
+    for i in range(half):
+        out_ref[i // PAIRS, i % PAIRS] = wide[i * PITCH : i * PITCH + PAD, :].astype(bf16)
+
+
+def mix_kernel(coef_ref, weight_hbm, out_ref, weight, sem):
+    copy = pltpu.make_async_copy(weight_hbm, weight, sem)
+    copy.start()
+    copy.wait()
+    bands, ch_count = coef_ref.shape[:2]
     ch_dev = LANES // 4
     channels = ch_count * ch_dev
     contract = (((1,), (1,)), ((), ()))
-
-    def copy(degree):
-        return pltpu.make_async_copy(weight_hbm.at[:, :, degree], weight.at[degree], sems.at[degree])
-
-    for degree in range(deg_dev):
-        copy(degree).start()
-    for d in range(blocks):
-        part = coef_ref[d * ch_count : (d + 1) * ch_count].reshape(jump - 1, LANES)
-        wide[d * jump : (d + 1) * jump - 1, :] = part.astype(f32)
-    for e in range(ch_count):
-        mixed[pl.ds((e + 1) * PAD - 1, blocks, stride=jump), :] = jnp.zeros((blocks, LANES), f32)
-
-    def one_degree(degree):
+    step = MIX_BANDS
+    count = step * PAD
+
+    @pl.loop(0, bands // step)
+    def _(chunk):
+        here = pl.ds(chunk * step, step)
         groups = []
         for h in range(ch_count // 4):
-            quads = [wide[pl.ds((4 * h + e) * PAD + degree, blocks, stride=jump), :] for e in range(4)]
+            quads = [coef_ref[here, 4 * h + e].reshape(count, LANES).astype(f32) for e in range(4)]
             groups.append(chunk_transpose(quads))
-        left = jnp.concatenate(
-            [jnp.concatenate([g[q] for g in groups], axis=1) for q in range(4)], axis=0
-        ).astype(bf16)
-        prod = [
-            lax.dot_general(
-                left,
-                weight[degree, :, w].reshape(channels, channels),
-                contract,
-                preferred_element_type=f32,
-            )
-            for w in range(2)
-        ]
-
-        def take(w, q):
-            return prod[w][q * blocks : (q + 1) * blocks]
-
         results = []
-        for m2 in range(2):
-            results.append(take(0, 2 * m2) - take(1, 2 * m2 + 1))
-            results.append(take(1, 2 * m2) + take(0, 2 * m2 + 1))
+        for l2 in range(2):
+            left = jnp.concatenate(
+                [jnp.concatenate([g[2 * l2 + x] for g in groups], axis=1) for x in range(2)], axis=0
+            ).astype(bf16)
+            prod = [
+                lax.dot_general(
+                    left,
+                    weight[:, w, l2].reshape(channels, channels),
+                    contract,
+                    preferred_element_type=f32,
+                )
+                for w in range(2)
+            ]
+            results.append(prod[0][:count] - prod[1][count:])
+            results.append(prod[1][:count] + prod[0][count:])
         for h in range(ch_count // 4):
             quads = chunk_transpose([r[:, h * LANES : (h + 1) * LANES] for r in results])
             for e in range(4):
-                mixed[pl.ds((4 * h + e) * PAD + degree, blocks, stride=jump), :] = quads[e]
-
-    group = MIX_GROUP
-
-    @pl.loop(0, deg_dev // group)
-    def _(step):
-        for i in range(group):
-            copy(step * group + i).wait()
-        for i in range(group):
-            one_degree(step * group + i)
-
-    for d in range(blocks):
-        part = mixed[d * jump : (d + 1) * jump - 1, :].astype(bf16)
-        out_ref[d * ch_count : (d + 1) * ch_count] = part.reshape(ch_count, PAD, LANES)
-
-
-def synthesis_kernel(ord_dev, lon, index_ref, slots_ref, mixed_ref, table_hbm, out_ref, table, sems):
+                out_ref[here, 4 * h + e] = quads[e].astype(bf16).reshape(step, PAD, LANES)
+
+
+def widen(mixed_ref, wide):
+    for i in range(mixed_ref.shape[0] * PAIRS):
+        wide[i * PITCH : i * PITCH + PAD, :] = mixed_ref[i // PAIRS, i % PAIRS].astype(f32)
+
+
+def side_of(wide, count, m):
+    turned = wide[pl.ds(m, count * PAIRS, stride=PITCH), :].T
+    return jnp.concatenate([turned[: LANES // 2], turned[LANES // 2 :]], axis=1)
+
+
+def synthesis_kernel(ord_dev, lon, index_ref, slots_ref, mixed_ref, table_hbm, out_ref, table, wide, sems):
     copy = fetch_pairs(table_hbm, table, sems)
+    widen(mixed_ref, wide)
     count = out_ref.shape[0]
     half = LANES // 2
     parity = degree_parity((half, table.shape[1]), 1, ord_dev)
 
     @pl.loop(0, PAIRS)
     def _(p):
-        side = jnp.concatenate([mixed_ref[d, p] for d in range(count)], axis=0).astype(f32).T
         copy(p).wait()
         north, south = [], []
         for m2 in range(2):
             order = order_of(slots_ref, index_ref, ord_dev, 2 * p + m2)
             weight = jnp.where(order == 0, 1.0 / lon, 2.0 / lon)
-            part = side[m2 * half : (m2 + 1) * half]
+            part = side_of(wide, count, 2 * p + m2)
             same = parity == (order & 1)
             split = jnp.concatenate([jnp.where(same, part, 0.0), jnp.where(same, 0.0, part)], axis=0)
             prod = jnp.dot(split.astype(bf16), table[2 * p + m2], preferred_element_type=f32)
@@ -394,21 +394,15 @@
             out_ref[count - 1 - s, p] = down[s * PAD : (s + 1) * PAD]
 
 
-def spectrum_kernel(ord_dev, mixed_ref, pick_ref, out_ref):
+def spectrum_kernel(ord_dev, mixed_ref, pick_ref, out_ref, wide):
     count = mixed_ref.shape[0]
-    half = LANES // 2
-    shape = out_ref.shape[1:]
-
-    @pl.loop(0, PAIRS)
-    def _(p):
-        rows = jnp.concatenate([mixed_ref[d, p] for d in range(count)], axis=0)
-        side = rows.astype(f32).T.astype(bf16)
+    widen(mixed_ref, wide)
+
+    @pl.loop(0, ord_dev)
+    def _(m):
+        side = side_of(wide, count, m).astype(bf16)
         spec = jnp.dot(side, pick_ref[...], preferred_element_type=f32).astype(bf16)
-        out_ref[2 * p] = spec[:half].reshape(shape)
-
-        @pl.when(2 * p + 1 < ord_dev)
-        def _():
-            out_ref[2 * p + 1] = spec[half:].reshape(shape)
+        out_ref[m] = spec.reshape(out_ref.shape[1:])
 
 
 def backward_kernel(
@@ -451,7 +445,7 @@
     return pl.CostEstimate(flops=int(flops), bytes_accessed=int(moved), transcendentals=0)
 
 
-MIX_GROUP = 3
+MIX_BANDS = 8
 vmem = pl.BlockSpec(memory_space=pltpu.VMEM)
 smem = pl.BlockSpec(memory_space=pltpu.SMEM)
 hbm = pl.BlockSpec(memory_space=pltpu.HBM)
@@ -507,14 +501,14 @@
     state = pltpu.VMEM((groups, PAD, LANES), f32)
     table = pl.pallas_call(
         functools.partial(legendre_kernel, ord_dev),
-        out_shape=jax.ShapeDtypeStruct((PAD, lat_count, PAD, near), bf16),
+        out_shape=jax.ShapeDtypeStruct((PAD, 2, lat_count // 2, PAD, near), bf16),
         in_specs=[smem, smem, vmem, vmem, vmem],
         out_specs=hbm,
         scratch_shapes=[state] * 5
         + [
             pltpu.VMEM((PAD, LANES), f32),
-            pltpu.VMEM((groups, PAD * PITCH, LANES), f32),
-            pltpu.VMEM((PAD, lat_count, PAD, near), bf16),
+            pltpu.VMEM((groups, PAD * (2 * PAD + 1), LANES), f32),
+            pltpu.VMEM((PAD, 2, lat_count // 2, PAD, near), bf16),
             pltpu.SemaphoreType.DMA((parts,)),
         ],
         compiler_params=params(TABLE_MIB),
@@ -543,41 +537,46 @@
 
 
 def call_analysis(ord_dev, index, orders, rows, table):
+    lat_count = rows.shape[0]
     return pl.pallas_call(
         functools.partial(analysis_kernel, ord_dev),
         out_shape=jax.ShapeDtypeStruct(rows.shape, bf16),
         in_specs=[smem, smem, vmem, hbm],
         out_specs=vmem,
-        scratch_shapes=[pltpu.VMEM(table.shape, bf16), pltpu.SemaphoreType.DMA((PAIRS,))],
+        scratch_shapes=[
+            pltpu.VMEM(table.shape, bf16),
+            pltpu.VMEM((lat_count * PAIRS * PITCH, LANES), f32),
+            pltpu.SemaphoreType.DMA((PAIRS,)),
+        ],
         compiler_params=params(),
         name="analysis",
     )(index, orders, rows, table)
 
 
-def call_mix(lat_count, coeffs, weights):
-    ch_count, _, ord_dev, ch_dev, channels = weights.shape
+def call_mix(coeffs, weights):
     return pl.pallas_call(
-        functools.partial(mix_kernel, lat_count, ch_count, ord_dev),
+        mix_kernel,
         out_shape=jax.ShapeDtypeStruct(coeffs.shape, bf16),
         in_specs=[vmem, hbm],
         out_specs=vmem,
-        scratch_shapes=[pltpu.VMEM((lat_count * (ch_count * PAD + 1), LANES), f32)] * 2
-        + [
-            pltpu.VMEM((ord_dev, ch_count, 2, ch_dev, channels), bf16),
-            pltpu.SemaphoreType.DMA((ord_dev,)),
-        ],
+        scratch_shapes=[pltpu.VMEM(weights.shape, bf16), pltpu.SemaphoreType.DMA],
         compiler_params=params(),
         name="mix",
     )(coeffs, weights)
 
 
 def call_synthesis(ord_dev, lon, index, orders, mixed, table):
+    lat_count = mixed.shape[0]
     return pl.pallas_call(
         functools.partial(synthesis_kernel, ord_dev, lon),
         out_shape=buffer_of(mixed.shape[0]),
         in_specs=[smem, smem, vmem, hbm],
         out_specs=vmem,
-        scratch_shapes=[pltpu.VMEM(table.shape, bf16), pltpu.SemaphoreType.DMA((PAIRS,))],
+        scratch_shapes=[
+            pltpu.VMEM(table.shape, bf16),
+            pltpu.VMEM((lat_count * PAIRS * PITCH, LANES), f32),
+            pltpu.SemaphoreType.DMA((PAIRS,)),
+        ],
         compiler_params=params(),
         name="synthesis",
     )(index, orders, mixed, table)
@@ -588,12 +587,14 @@
     modes = ord_dev * lat_count
     pick = np.zeros((lat_count, PAD, modes), np.float32)
     pick[:, :ord_dev] = np.eye(modes, dtype=np.float32).reshape(lat_count, ord_dev, modes)
+    pick = pick.reshape(lat_count * PAIRS, 2, modes).transpose(1, 0, 2)
     pick = jnp.asarray(pick.reshape(lat_count * PAD, modes), bf16)
     return pl.pallas_call(
         functools.partial(spectrum_kernel, ord_dev),
         out_shape=jax.ShapeDtypeStruct((ord_dev, 2, LANES // 4, modes), bf16),
         in_specs=[vmem, vmem],
         out_specs=vmem,
+        scratch_shapes=[pltpu.VMEM((lat_count * PAIRS * PITCH, LANES), f32)],
         compiler_params=params(),
         cost_estimate=cost(3e9, 4e6),
         name="spectrum",
@@ -630,14 +631,18 @@
     index = index.reshape(1)
     slots = order_slots.reshape(1, modes)
 
-    weights = lax.all_gather(jnp.transpose(mix_weight, (0, 3, 2, 1)), "ch", axis=0)
     rows = call_forward(lat_count, index, slots, field_in)
     rows = lax.all_to_all(rows, "lat", 0, 0, tiled=True)
     legendre = call_legendre(lat_count, lat_dev, index, slots)
+    weights = jnp.transpose(mix_weight, (0, 3, 2, 1))
+    weights, legendre = lax.optimization_barrier((weights, legendre))
+    weights = jnp.pad(weights, ((0, 0), (0, PAD - ord_dev), (0, 0), (0, 0)))
+    weights = weights.reshape((2, PAIRS, 2) + weights.shape[2:]).swapaxes(0, 1)
+    weights = lax.all_to_all(weights, "ch", 0, 0, tiled=True)
     coeffs = call_analysis(ord_dev, index, order_slots, rows, legendre)
     coeffs = lax.all_to_all(coeffs.reshape(-1, PAD, LANES), ("lat", "ch"), 0, 0, tiled=True)
-    mixed = call_mix(lat_count, coeffs, weights)
-    mixed = lax.all_to_all(mixed, ("lat", "ch"), 0, 0, tiled=True).reshape(rows.shape)
+    mixed = call_mix(coeffs.reshape(rows.shape), weights)
+    mixed = lax.all_to_all(mixed.reshape(-1, PAD, LANES), ("lat", "ch"), 0, 0, tiled=True).reshape(rows.shape)
     synth = call_synthesis(ord_dev, lon, index, order_slots, mixed, legendre)
     synth = lax.all_to_all(synth, "lat", 0, 0, tiled=True)
     spectrum = call_spectrum(ord_dev, mixed)

time: 176 us -> 167 us (0.949)
  blocking collectives: 89.9 us -> 75.4 us
  between operations: 14.1 us -> 0.76 us
  waiting for transfers between devices: 20.2 us -> 30.1 us
  starting transfers between devices: 13.1 us -> 21.2 us
    all_to_all x1, blocking collectives: 51.9 us -> 37.5 us  [on_device(): lax.all_to_all(coeffs.reshape(-1, PAD, LANES), ('lat', 'ch'), 0, 0, tiled...]
    all_to_all x0 -> x1, waiting for transfers between devices: none -> 13.1 us  [on_device(): weights = lax.all_to_all(weights, 'ch', 0, 0, tiled=True)]
    all_to_all x0 -> x1, starting transfers between devices: none -> 8.19 us  [on_device(): weights = lax.all_to_all(weights, 'ch', 0, 0, tiled=True)]
    pallas_call x1, Pallas kernels: 4.74 us -> 2.93 us  [call_mix(): pl.pallas_call(mix_kernel, out_shape=jax.ShapeDtypeStruct(coeffs.shape, b...]
  transfers between devices with their start and end apart: 3 -> 3, of which waited for: 2 -> 3; matrix products, arithmetic and copies ran while one was open for 0% -> 1% of each run, Pallas kernels for 13% -> 13%
where the time goes in v4:
time: 167 us
  blocking collectives  75.4 us (45%)
  Pallas kernels  38.1 us (23%)
  waiting for transfers between devices  30.1 us (18%)
  starting transfers between devices  21.2 us (13%)
    all_to_all x1, blocking collectives, on_device(): lax.all_to_all(mixed.reshape(-1, PAD, LANES), ('lat', 'ch'), 0, 0, tiled=...  37.9 us
    all_to_all x1, blocking collectives, on_device(): lax.all_to_all(coeffs.reshape(-1, PAD, LANES), ('lat', 'ch'), 0, 0, tiled...  37.5 us
    all_to_all x1, waiting for transfers between devices, on_device(): weights = lax.all_to_all(weights, 'ch', 0, 0, tiled=True)  13.1 us
    all_to_all x1, waiting for transfers between devices, on_device(): rows = lax.all_to_all(rows, 'lat', 0, 0, tiled=True)  9.09 us
    all_to_all x1, starting transfers between devices, on_device(): rows = lax.all_to_all(rows, 'lat', 0, 0, tiled=True)  8.6 us
    all_to_all x1, starting transfers between devices, on_device(): weights = lax.all_to_all(weights, 'ch', 0, 0, tiled=True)  8.19 us
    all_to_all x1, waiting for transfers between devices, on_device(): synth = lax.all_to_all(synth, 'lat', 0, 0, tiled=True)  7.94 us
    pallas_call x1, Pallas kernels, call_legendre(): pl.pallas_call(functools.partial(legendre_kernel, ord_dev), out_shape=jax...  6.9 us
  transfers between devices with their start and end apart: 3, of which 3 were waited for; matrix products, arithmetic and copies ran while one was open for 1% of the time, Pallas kernels for 13%

profile of v4, /device:TPU:1, one launch (start us, length us, event | category | flops | bytes accessed | tf_op | source)
XLA Modules:
  0.0 166.5 jit_solution(10597105790439693788)
XLA Ops:
  0.6 4.5 %forward.1 = bf16[32,8,16,128]{3,2,1,0:T(8,128)(2,1)} custom-call(s32[1]{0:T(128)} %bitcast.index_ref, s32[1,480]{1,0:T(1,128)} %bitcast.17, bf16[15,32,1024]{2,1,0:T(8,128)(2,1)} %field_hbm.3), custom_call_target="tpu_custom_call" | custom-call | tf_op jit(solution)/shard_map/forward/pallas_call | solution.py:461
  5.2 8.6 %all-to-all-start = ((bf16[32,8,16,128]{3,2,1,0:T(8,128)(2,1)}), bf16[32,8,16,128]{3,2,1,0:T(8,128)(2,1)S(1)}, u32[]{:S(2)}, u32[]{:S(2)}) async-start(bf16[32,8,16,128]{3,2,1,0:T(8,128)(2,1)} %forward.1), calls=%async_computation | async-start | bytes 2097152 | tf_op jit(solution)/shard_map/all_to_all | solution.py:635
  13.8 0.0 copy-start.3
  13.8 0.0 copy-start.1
  13.8 6.9 %legendre.1 = bf16[16,2,16,16,256]{4,3,2,1,0:T(8,128)(2,1)} custom-call(s32[1]{0:T(128)} %bitcast.index_ref, f32[2,480]{1,0:T(2,128)} %constant.17.clone.scale_ref, s32[1,480]{1,0:T(1,128)} %bitcast.18, f32[2,256]{1,0:T(2,128)} %constant.18.clone.geo_ref, f32[1,512]{1,0:T(1,128)} %constant.19.clone.prod_ref), custom_call_target="tpu_custom_call" | custom-call | flops 8000000000 | bytes 20000000 | tf_op jit(solution)/shard_map/legendre/pallas_call | solution.py:502
  20.7 0.0 copy-done.3
  20.8 0.8 copy.11
  21.6 9.1 %all-to-all-done.rows_ref = bf16[32,8,16,128]{3,2,1,0:T(8,128)(2,1)S(1)} async-done(((bf16[32,8,16,128]{3,2,1,0:T(8,128)(2,1)}), bf16[32,8,16,128]{3,2,1,0:T(8,128)(2,1)S(1)}, u32[]{:S(2)}, u32[]{:S(2)}) %all-to-all-start) | async-done | bytes 1048608 | tf_op jit(solution)/shard_map/all_to_all | solution.py:635
  30.7 8.2 %all-to-all-start.2 = ((bf16[8,2,2,32,256]{4,3,2,1,0:T(8,128)(2,1)}), bf16[8,2,2,32,256]{4,3,2,1,0:T(8,128)(2,1)S(1)}, u32[]{:S(2)}, u32[]{:S(2)}) async-start(bf16[8,2,2,32,256]{4,3,2,1,0:T(8,128)(2,1)} %bitcast.11), calls=%async_computation.2 | async-start | bytes 1048576 | tf_op jit(solution)/shard_map/all_to_all | solution.py:641
  38.9 0.0 copy-done.1
  38.9 4.9 %analysis.1 = bf16[32,8,16,128]{3,2,1,0:T(8,128)(2,1)S(1)} custom-call(s32[1]{0:T(128)} %bitcast.index_ref, s32[480]{0:T(512)S(1)} %copy-done.1, bf16[32,8,16,128]{3,2,1,0:T(8,128)(2,1)S(1)} %all-to-all-done.rows_ref, bf16[16,512,256]{2,1,0:T(8,128)(2,1)} %bitcast.20), custom_call_target="tpu_custom_call" | custom-call | tf_op jit(solution)/shard_map/analysis/pallas_call | solution.py:541
  43.8 13.1 %all-to-all-done.2.weight_hbm = bf16[8,2,2,32,256]{4,3,2,1,0:T(8,128)(2,1)S(1)} async-done(((bf16[8,2,2,32,256]{4,3,2,1,0:T(8,128)(2,1)}), bf16[8,2,2,32,256]{4,3,2,1,0:T(8,128)(2,1)S(1)}, u32[]{:S(2)}, u32[]{:S(2)}) %all-to-all-start.2) | async-done | bytes 524320 | tf_op jit(solution)/shard_map/all_to_all | solution.py:641
  56.9 37.5 %all_to_all.25 = bf16[256,16,128]{2,1,0:T(8,128)(2,1)S(1)} all-to-all(bf16[256,16,128]{2,1,0:T(8,128)(2,1)S(1)} %bitcast.16), channel_id=1, replica_groups=mesh['lat'=32,'ch'=8] {'lat','ch'}, dimensions={0} | all-to-all | bytes 2097152 | tf_op jit(solution)/shard_map/all_to_all | solution.py:643
  94.4 2.9 %mix.1 = bf16[32,8,16,128]{3,2,1,0:T(8,128)(2,1)S(1)} custom-call(bf16[32,8,16,128]{3,2,1,0:T(8,128)(2,1)S(1)} %bitcast.12, bf16[8,2,2,32,256]{4,3,2,1,0:T(8,128)(2,1)S(1)} %all-to-all-done.2.weight_hbm), custom_call_target="tpu_custom_call" | custom-call | tf_op jit(solution)/shard_map/mix/pallas_call | solution.py:557
  97.3 37.9 %all_to_all.26 = bf16[256,16,128]{2,1,0:T(8,128)(2,1)S(1)} all-to-all(bf16[256,16,128]{2,1,0:T(8,128)(2,1)S(1)} %bitcast.13), channel_id=1, replica_groups=mesh['lat'=32,'ch'=8] {'lat','ch'}, dimensions={0} | all-to-all | bytes 2097152 | tf_op jit(solution)/shard_map/all_to_all | solution.py:645
  135.2 5.6 %synthesis.1 = bf16[32,8,16,128]{3,2,1,0:T(8,128)(2,1)} custom-call(s32[1]{0:T(128)} %bitcast.index_ref, s32[480]{0:T(512)S(1)} %copy-done.1, bf16[32,8,16,128]{3,2,1,0:T(8,128)(2,1)S(1)} %bitcast.14, bf16[16,512,256]{2,1,0:T(8,128)(2,1)} %bitcast.21), custom_call_target="tpu_custom_call" | custom-call | tf_op jit(solution)/shard_map/synthesis/pallas_call | solution.py:570
  140.8 4.4 %all-to-all-start.4 = ((bf16[32,8,16,128]{3,2,1,0:T(8,128)(2,1)}), bf16[32,8,16,128]{3,2,1,0:T(8,128)(2,1)S(1)}, u32[]{:S(2)}, u32[]{:S(2)}) async-start(bf16[32,8,16,128]{3,2,1,0:T(8,128)(2,1)} %synthesis.1), calls=%async_computation.4 | async-start | bytes 2097152 | tf_op jit(solution)/shard_map/all_to_all | solution.py:647
  145.3 0.0 copy-start.2
  145.3 4.1 %inverse_table.1.table_hbm = bf16[1024,1024]{1,0:T(8,128)(2,1)} custom-call(s32[1,480]{1,0:T(1,128)} %bitcast.19), custom_call_target="tpu_custom_call" | custom-call | flops 2000000000 | bytes 4000000 | tf_op jit(solution)/shard_map/inverse_table/pallas_call | solution.py:523
  149.4 0.0 copy-done.2
  149.4 0.0 copy-start
  149.4 4.9 %spectrum.1 = bf16[15,2,32,480]{3,2,1,0:T(8,128)(2,1)} custom-call(bf16[32,8,16,128]{3,2,1,0:T(8,128)(2,1)S(1)} %bitcast.15, bf16[512,480]{1,0:T(8,128)(2,1)S(1)} %copy-done.2), custom_call_target="tpu_custom_call" | custom-call | flops 3000000000 | bytes 4000000 | tf_op jit(solution)/shard_map/spectrum/pallas_call | solution.py:592
  154.3 7.9 %all-to-all-done.4.rows_ref = bf16[32,8,16,128]{3,2,1,0:T(8,128)(2,1)S(1)} async-done(((bf16[32,8,16,128]{3,2,1,0:T(8,128)(2,1)}), bf16[32,8,16,128]{3,2,1,0:T(8,128)(2,1)S(1)}, u32[]{:S(2)}, u32[]{:S(2)}) %all-to-all-start.4) | async-done | bytes 1048608 | tf_op jit(solution)/shard_map/all_to_all | solution.py:647
  162.3 0.0 copy-done
  162.3 4.2 %backward.1 = bf16[15,32,1024]{2,1,0:T(8,128)(2,1)} custom-call(s32[1]{0:T(128)} %bitcast.index_ref, bf16[32,8,16,128]{3,2,1,0:T(8,128)(2,1)S(1)} %all-to-all-done.4.rows_ref, bf16[1024,1024]{1,0:T(8,128)(2,1)} %inverse_table.1.table_hbm, bf16[15,32,1024]{2,1,0:T(8,128)(2,1)S(1)} %copy-done), custom_call_target="tpu_custom_call" | custom-call | tf_op jit(solution)/shard_map/backward/pallas_call | solution.py:608
  (1 shorter events, 0.0 us)
Async XLA Ops:
  5.2 25.5 %all-to-all-start = ((bf16[32,8,16,128]{3,2,1,0:T(8,128)(2,1)}), bf16[32,8,16,128]{3,2,1,0:T(8,128)(2,1)S(1)}, u32[]{:S(2)}, u32[]{:S(2)}) async-start(bf16[32,8,16,128]{3,2,1,0:T(8,128)(2,1)} %forward.1), calls=%async_computation | async-start | bytes 2097152 | tf_op jit(solution)/shard_map/all_to_all | solution.py:635
  13.8 6.9 %copy-start.3 = (bf16[2,256,32,15]{1,2,3,0:T(8,128)(2,1)S(1)}, bf16[2,256,32,15]{1,2,3,0:T(8,128)(2,1)}, u32[]{:S(2)}) copy-start(bf16[2,256,32,15]{1,2,3,0:T(8,128)(2,1)} %param.8) | copy-start | bytes 1474564
  13.8 25.1 %copy-start.1 = (s32[480]{0:T(512)S(1)}, s32[480]{0:T(512)}, u32[]{:S(2)}) copy-start(s32[480]{0:T(512)} %slots_ref.3) | copy-start | bytes 5764
  30.7 26.2 %all-to-all-start.2 = ((bf16[8,2,2,32,256]{4,3,2,1,0:T(8,128)(2,1)}), bf16[8,2,2,32,256]{4,3,2,1,0:T(8,128)(2,1)S(1)}, u32[]{:S(2)}, u32[]{:S(2)}) async-start(bf16[8,2,2,32,256]{4,3,2,1,0:T(8,128)(2,1)} %bitcast.11), calls=%async_computation.2 | async-start | bytes 1048576 | tf_op jit(solution)/shard_map/all_to_all | solution.py:641
  140.8 21.4 %all-to-all-start.4 = ((bf16[32,8,16,128]{3,2,1,0:T(8,128)(2,1)}), bf16[32,8,16,128]{3,2,1,0:T(8,128)(2,1)S(1)}, u32[]{:S(2)}, u32[]{:S(2)}) async-start(bf16[32,8,16,128]{3,2,1,0:T(8,128)(2,1)} %synthesis.1), calls=%async_computation.4 | async-start | bytes 2097152 | tf_op jit(solution)/shard_map/all_to_all | solution.py:647
  145.3 4.1 %copy-start.2 = (bf16[512,480]{1,0:T(8,128)(2,1)S(1)}, bf16[512,480]{1,0:T(8,128)(2,1)}, u32[]{:S(2)}) copy-start(bf16[512,480]{1,0:T(8,128)(2,1)} %constant.20.clone.pick_ref) | copy-start | bytes 1474564
  149.4 12.9 %copy-start = (bf16[15,32,1024]{2,1,0:T(8,128)(2,1)S(1)}, bf16[15,32,1024]{2,1,0:T(8,128)(2,1)}, u32[]{:S(2)}) copy-start(bf16[15,32,1024]{2,1,0:T(8,128)(2,1)} %field_hbm.3) | copy-start | bytes 2949124

commit v5 on v4

--- a/solution.py
+++ b/solution.py
@@ -317,11 +317,27 @@
         out_ref[i // PAIRS, i % PAIRS] = wide[i * PITCH : i * PITCH + PAD, :].astype(bf16)
 
 
-def mix_kernel(coef_ref, weight_hbm, out_ref, weight, sem):
-    copy = pltpu.make_async_copy(weight_hbm, weight, sem)
-    copy.start()
-    copy.wait()
-    bands, ch_count = coef_ref.shape[:2]
+def weights_kernel(index_ref, weight_ref, *out_refs):
+    ch_count = len(out_refs)
+    last = weight_ref.shape[1] - 1
+    for k, out_ref in enumerate(out_refs):
+        there = lax.rem(index_ref[0] + k, ch_count)
+        for w in range(2):
+            for l2 in range(2):
+                out_ref[w, l2] = weight_ref[w, jnp.minimum(2 * there + l2, last)]
+
+
+def mix_kernel(index_ref, coef_ref, *refs):
+    ch_count = len(refs) - 3
+    out_ref, weight, sems = refs[ch_count:]
+    copies = []
+    for k in range(ch_count):
+        source = lax.rem(index_ref[0] + ch_count - k, ch_count)
+        copies.append(pltpu.make_async_copy(refs[k], weight.at[source], sems.at[k]))
+        copies[-1].start()
+    for copy in copies:
+        copy.wait()
+    bands = coef_ref.shape[0]
     ch_dev = LANES // 4
     channels = ch_count * ch_dev
     contract = (((1,), (1,)), ((), ()))
@@ -553,16 +569,38 @@
     )(index, orders, rows, table)
 
 
-def call_mix(coeffs, weights):
+def exchange_weights(index, weights):
+    ch_count = lax.axis_size("ch")
+    piece = jax.ShapeDtypeStruct((2, 2) + weights.shape[2:], bf16)
+    pieces = pl.pallas_call(
+        weights_kernel,
+        out_shape=(piece,) * ch_count,
+        in_specs=[smem, vmem],
+        out_specs=(vmem,) * ch_count,
+        compiler_params=params(),
+        name="weights",
+    )(index, weights)
+    moved = [pieces[0]]
+    for k in range(1, ch_count):
+        ring = [(e, (e + k) % ch_count) for e in range(ch_count)]
+        moved.append(lax.ppermute(pieces[k], "ch", ring))
+    return moved
+
+
+def call_mix(index, coeffs, weights):
+    ch_count = len(weights)
     return pl.pallas_call(
         mix_kernel,
         out_shape=jax.ShapeDtypeStruct(coeffs.shape, bf16),
-        in_specs=[vmem, hbm],
+        in_specs=[smem, vmem] + [hbm] * ch_count,
         out_specs=vmem,
-        scratch_shapes=[pltpu.VMEM(weights.shape, bf16), pltpu.SemaphoreType.DMA],
+        scratch_shapes=[
+            pltpu.VMEM((ch_count,) + weights[0].shape, bf16),
+            pltpu.SemaphoreType.DMA((ch_count,)),
+        ],
         compiler_params=params(),
         name="mix",
-    )(coeffs, weights)
+    )(index, coeffs, *weights)
 
 
 def call_synthesis(ord_dev, lon, index, orders, mixed, table):
@@ -636,12 +674,12 @@
     legendre = call_legendre(lat_count, lat_dev, index, slots)
     weights = jnp.transpose(mix_weight, (0, 3, 2, 1))
     weights, legendre = lax.optimization_barrier((weights, legendre))
-    weights = jnp.pad(weights, ((0, 0), (0, PAD - ord_dev), (0, 0), (0, 0)))
-    weights = weights.reshape((2, PAIRS, 2) + weights.shape[2:]).swapaxes(0, 1)
-    weights = lax.all_to_all(weights, "ch", 0, 0, tiled=True)
+    ch_index = lax.axis_index("ch").reshape(1)
+    weights = exchange_weights(ch_index, weights)
     coeffs = call_analysis(ord_dev, index, order_slots, rows, legendre)
+    coeffs, weights = lax.optimization_barrier((coeffs, weights))
     coeffs = lax.all_to_all(coeffs.reshape(-1, PAD, LANES), ("lat", "ch"), 0, 0, tiled=True)
-    mixed = call_mix(coeffs.reshape(rows.shape), weights)
+    mixed = call_mix(ch_index, coeffs.reshape(rows.shape), weights)
     mixed = lax.all_to_all(mixed.reshape(-1, PAD, LANES), ("lat", "ch"), 0, 0, tiled=True).reshape(rows.shape)
     synth = call_synthesis(ord_dev, lon, index, order_slots, mixed, legendre)
     synth = lax.all_to_all(synth, "lat", 0, 0, tiled=True)

time: 167 us -> 161 us (0.964)
  waiting for transfers between devices: 30.1 us -> 9.88 us
  starting transfers between devices: 21.2 us -> 29.5 us
  blocking collectives: 75.4 us -> 81.5 us
    ppermute x0 -> x7, starting transfers between devices: none -> 16.5 us  [exchange_weights(): moved.append(lax.ppermute(pieces[k], 'ch', ring))]
    all_to_all x1 -> x0, waiting for transfers between devices: 13.1 us -> none  [on_device(): weights = lax.all_to_all(weights, 'ch', 0, 0, tiled=True)]
    all_to_all x1, waiting for transfers between devices: 9.09 us -> 0.01 us  [on_device(): rows = lax.all_to_all(rows, 'lat', 0, 0, tiled=True)]
    all_to_all x1 -> x0, starting transfers between devices: 8.19 us -> none  [on_device(): weights = lax.all_to_all(weights, 'ch', 0, 0, tiled=True)]
    all_to_all x1, blocking collectives: 37.5 us -> 43.4 us  [on_device(): lax.all_to_all(coeffs.reshape(-1, PAD, LANES), ('lat', 'ch'), 0, 0, tiled...]
    ppermute x0 -> x7, waiting for transfers between devices: none -> 1.94 us  [exchange_weights(): moved.append(lax.ppermute(pieces[k], 'ch', ring))]
  transfers between devices with their start and end apart: 3 -> 9, of which waited for: 3 -> 2; matrix products, arithmetic and copies ran while one was open for 1% -> 0% of each run, Pallas kernels for 13% -> 13%
where the time goes in v5:
time: 161 us
  blocking collectives  81.5 us (51%)
  Pallas kernels  38.9 us (24%)
  starting transfers between devices  29.5 us (18%)
  waiting for transfers between devices  9.88 us (6%)
    all_to_all x1, blocking collectives, on_device(): lax.all_to_all(coeffs.reshape(-1, PAD, LANES), ('lat', 'ch'), 0, 0, tiled...  43.4 us
    all_to_all x1, blocking collectives, on_device(): lax.all_to_all(mixed.reshape(-1, PAD, LANES), ('lat', 'ch'), 0, 0, tiled=...  38.1 us
    ppermute x7, starting transfers between devices, exchange_weights(): moved.append(lax.ppermute(pieces[k], 'ch', ring))  16.5 us
    all_to_all x1, starting transfers between devices, on_device(): rows = lax.all_to_all(rows, 'lat', 0, 0, tiled=True)  8.6 us
    all_to_all x1, waiting for transfers between devices, on_device(): synth = lax.all_to_all(synth, 'lat', 0, 0, tiled=True)  7.94 us
    pallas_call x1, Pallas kernels, call_legendre(): pl.pallas_call(functools.partial(legendre_kernel, ord_dev), out_shape=jax...  6.9 us
    pallas_call x1, Pallas kernels, call_synthesis(): pl.pallas_call(functools.partial(synthesis_kernel, ord_dev, lon), out_sha...  5.62 us
    pallas_call x1, Pallas kernels, call_spectrum(): pl.pallas_call(functools.partial(spectrum_kernel, ord_dev), out_shape=jax...  4.93 us
  transfers between devices with their start and end apart: 9, of which 2 were waited for; matrix products, arithmetic and copies ran while one was open for 0% of the time, Pallas kernels for 13%

profile of v5, /device:TPU:1, one launch (start us, length us, event | category | flops | bytes accessed | tf_op | source)
XLA Modules:
  0.0 160.8 jit_solution(2359604193569615589)
XLA Ops:
  0.6 4.6 %forward.1 = bf16[32,8,16,128]{3,2,1,0:T(8,128)(2,1)} custom-call(s32[1]{0:T(128)} %bitcast.index_ref, s32[1,480]{1,0:T(1,128)} %bitcast.15, bf16[15,32,1024]{2,1,0:T(8,128)(2,1)} %field_hbm.3), custom_call_target="tpu_custom_call" | custom-call | tf_op jit(solution)/shard_map/forward/pallas_call | solution.py:477
  5.2 8.6 %all-to-all-start = ((bf16[32,8,16,128]{3,2,1,0:T(8,128)(2,1)}), bf16[32,8,16,128]{3,2,1,0:T(8,128)(2,1)S(1)}, u32[]{:S(2)}, u32[]{:S(2)}) async-start(bf16[32,8,16,128]{3,2,1,0:T(8,128)(2,1)} %forward.1), calls=%async_computation | async-start | bytes 2097152 | tf_op jit(solution)/shard_map/all_to_all | solution.py:673
  13.8 0.0 copy-start.1
  13.8 0.0 copy-start.2
  13.8 6.9 %legendre.1 = bf16[16,2,16,16,256]{4,3,2,1,0:T(8,128)(2,1)} custom-call(s32[1]{0:T(128)} %bitcast.index_ref, f32[2,480]{1,0:T(2,128)} %constant.17.clone.scale_ref, s32[1,480]{1,0:T(1,128)} %bitcast.16, f32[2,256]{1,0:T(2,128)} %constant.18.clone.geo_ref, f32[1,512]{1,0:T(1,128)} %constant.19.clone.prod_ref), custom_call_target="tpu_custom_call" | custom-call | flops 8000000000 | bytes 20000000 | tf_op jit(solution)/shard_map/legendre/pallas_call | solution.py:518
  20.7 0.0 copy-done.1
  20.8 1.7 %collective-permute-start = (bf16[2,2,32,256]{3,2,1,0:T(8,128)(2,1)S(1)}, bf16[2,2,32,256]{3,2,1,0:T(8,128)(2,1)S(1)}, u32[]{:S(2)}, u32[]{:S(2)}) collective-permute-start(bf16[2,2,32,256]{3,2,1,0:T(8,128)(2,1)S(1)} %get-tuple-element.24), channel_id=1, source_target_pairs={{0,1},{1,2},{2,3},{3,4},{4,5},{5,6},{6,7},{7,0},{8,9},{9,10},{10,1... | collective-permute-start | bytes 196616 | tf_op jit(solution)/shard_map/ppermute | solution.py:586
  22.5 3.0 %collective-permute-start.1 = (bf16[2,2,32,256]{3,2,1,0:T(8,128)(2,1)S(1)}, bf16[2,2,32,256]{3,2,1,0:T(8,128)(2,1)S(1)}, u32[]{:S(2)}, u32[]{:S(2)}) collective-permute-start(bf16[2,2,32,256]{3,2,1,0:T(8,128)(2,1)S(1)} %get-tuple-element.25), channel_id=1, source_target_pairs={{0,2},{1,3},{2,4},{3,5},{4,6},{5,7},{6,0},{7,1},{8,10},{9,11},{10,... | collective-permute-start | bytes 196616 | tf_op jit(solution)/shard_map/ppermute | solution.py:586
  25.5 3.8 %collective-permute-start.2 = (bf16[2,2,32,256]{3,2,1,0:T(8,128)(2,1)S(1)}, bf16[2,2,32,256]{3,2,1,0:T(8,128)(2,1)S(1)}, u32[]{:S(2)}, u32[]{:S(2)}) collective-permute-start(bf16[2,2,32,256]{3,2,1,0:T(8,128)(2,1)S(1)} %get-tuple-element.26), channel_id=1, source_target_pairs={{0,3},{1,4},{2,5},{3,6},{4,7},{5,0},{6,1},{7,2},{8,11},{9,12},{10,... | collective-permute-start | bytes 196616 | tf_op jit(solution)/shard_map/ppermute | solution.py:586
  29.3 0.5 collective-permute-start.3
  29.7 4.5 %collective-permute-start.4 = (bf16[2,2,32,256]{3,2,1,0:T(8,128)(2,1)S(1)}, bf16[2,2,32,256]{3,2,1,0:T(8,128)(2,1)S(1)}, u32[]{:S(2)}, u32[]{:S(2)}) collective-permute-start(bf16[2,2,32,256]{3,2,1,0:T(8,128)(2,1)S(1)} %get-tuple-element.28), channel_id=1, source_target_pairs={{0,5},{1,6},{2,7},{3,0},{4,1},{5,2},{6,3},{7,4},{8,13},{9,14},{10,... | collective-permute-start | bytes 196616 | tf_op jit(solution)/shard_map/ppermute | solution.py:586
  34.2 0.0 collective-permute-done.refs_1_
  34.2 2.4 %collective-permute-start.5 = (bf16[2,2,32,256]{3,2,1,0:T(8,128)(2,1)S(1)}, bf16[2,2,32,256]{3,2,1,0:T(8,128)(2,1)S(1)}, u32[]{:S(2)}, u32[]{:S(2)}) collective-permute-start(bf16[2,2,32,256]{3,2,1,0:T(8,128)(2,1)S(1)} %get-tuple-element.29), channel_id=1, source_target_pairs={{0,6},{1,7},{2,0},{3,1},{4,2},{5,3},{6,4},{7,5},{8,14},{9,15},{10,... | collective-permute-start | bytes 196616 | tf_op jit(solution)/shard_map/ppermute | solution.py:586
  36.6 0.0 collective-permute-done.1.refs_2_
  36.6 0.7 collective-permute-start.6
  37.3 0.0 all-to-all-done.rows_ref
  37.3 0.0 copy-done.2
  37.3 4.9 %analysis.1 = bf16[32,8,16,128]{3,2,1,0:T(8,128)(2,1)S(1)} custom-call(s32[1]{0:T(128)} %bitcast.index_ref, s32[480]{0:T(512)S(1)} %copy-done.2, bf16[32,8,16,128]{3,2,1,0:T(8,128)(2,1)S(1)} %all-to-all-done.rows_ref, bf16[16,512,256]{2,1,0:T(8,128)(2,1)} %bitcast.18), custom_call_target="tpu_custom_call" | custom-call | tf_op jit(solution)/shard_map/analysis/pallas_call | solution.py:557
  42.2 0.0 collective-permute-done.2.refs_3_
  42.2 0.0 collective-permute-done.3.refs_4_
  42.2 0.0 collective-permute-done.4.refs_5_
  42.3 1.9 %collective-permute-done.5.refs_6_ = bf16[2,2,32,256]{3,2,1,0:T(8,128)(2,1)S(1)} collective-permute-done((bf16[2,2,32,256]{3,2,1,0:T(8,128)(2,1)S(1)}, bf16[2,2,32,256]{3,2,1,0:T(8,128)(2,1)S(1)}, u32[]{:S(2)}, u32[]{:S(2)}) %collective-permute-start.5) | collective-permute-done | bytes 65568 | tf_op jit(solution)/shard_map/ppermute | solution.py:586
  44.2 0.0 collective-permute-done.6.refs_7_
  44.2 43.4 %all_to_all.20 = bf16[256,16,128]{2,1,0:T(8,128)(2,1)S(1)} all-to-all(bf16[256,16,128]{2,1,0:T(8,128)(2,1)S(1)} %bitcast.11), channel_id=1, replica_groups=mesh['lat'=32,'ch'=8] {'lat','ch'}, dimensions={0} | all-to-all | bytes 2097152 | tf_op jit(solution)/shard_map/all_to_all | solution.py:681
  87.6 3.7 %mix.1 = bf16[32,8,16,128]{3,2,1,0:T(8,128)(2,1)S(1)} custom-call(s32[1]{0:T(128)} %bitcast.1.index_ref, bf16[32,8,16,128]{3,2,1,0:T(8,128)(2,1)S(1)} %bitcast.9, bf16[2,2,32,256]{3,2,1,0:T(8,128)(2,1)S(1)} %get-tuple-element.32.refs_0_, bf16[2,2,32,256]{3,2,1,0:T(8,128)(2,1)S(1)} %collective-permute-done.refs_1_, ...), custom_call_target="tpu_custom_call" | custom-call | tf_op jit(solution)/shard_map/mix/pallas_call | solution.py:592
  91.3 38.1 %all_to_all.21 = bf16[256,16,128]{2,1,0:T(8,128)(2,1)S(1)} all-to-all(bf16[256,16,128]{2,1,0:T(8,128)(2,1)S(1)} %bitcast.10), channel_id=1, replica_groups=mesh['lat'=32,'ch'=8] {'lat','ch'}, dimensions={0} | all-to-all | bytes 2097152 | tf_op jit(solution)/shard_map/all_to_all | solution.py:683
  129.3 5.6 %synthesis.1 = bf16[32,8,16,128]{3,2,1,0:T(8,128)(2,1)} custom-call(s32[1]{0:T(128)} %bitcast.index_ref, s32[480]{0:T(512)S(1)} %copy-done.2, bf16[32,8,16,128]{3,2,1,0:T(8,128)(2,1)S(1)} %bitcast.12, bf16[16,512,256]{2,1,0:T(8,128)(2,1)} %bitcast.19), custom_call_target="tpu_custom_call" | custom-call | tf_op jit(solution)/shard_map/synthesis/pallas_call | solution.py:608
  135.0 4.4 %all-to-all-start.3 = ((bf16[32,8,16,128]{3,2,1,0:T(8,128)(2,1)}), bf16[32,8,16,128]{3,2,1,0:T(8,128)(2,1)S(1)}, u32[]{:S(2)}, u32[]{:S(2)}) async-start(bf16[32,8,16,128]{3,2,1,0:T(8,128)(2,1)} %synthesis.1), calls=%async_computation.3 | async-start | bytes 2097152 | tf_op jit(solution)/shard_map/all_to_all | solution.py:685
  139.4 0.0 copy-start.3
  139.4 4.1 %inverse_table.1.table_hbm = bf16[1024,1024]{1,0:T(8,128)(2,1)} custom-call(s32[1,480]{1,0:T(1,128)} %bitcast.17), custom_call_target="tpu_custom_call" | custom-call | flops 2000000000 | bytes 4000000 | tf_op jit(solution)/shard_map/inverse_table/pallas_call | solution.py:539
  143.5 0.0 copy-done.3
  143.5 0.0 copy-start
  143.5 4.9 %spectrum.1 = bf16[15,2,32,480]{3,2,1,0:T(8,128)(2,1)} custom-call(bf16[32,8,16,128]{3,2,1,0:T(8,128)(2,1)S(1)} %bitcast.13, bf16[512,480]{1,0:T(8,128)(2,1)S(1)} %copy-done.3), custom_call_target="tpu_custom_call" | custom-call | flops 3000000000 | bytes 4000000 | tf_op jit(solution)/shard_map/spectrum/pallas_call | solution.py:630
  148.5 7.9 %all-to-all-done.3.rows_ref = bf16[32,8,16,128]{3,2,1,0:T(8,128)(2,1)S(1)} async-done(((bf16[32,8,16,128]{3,2,1,0:T(8,128)(2,1)}), bf16[32,8,16,128]{3,2,1,0:T(8,128)(2,1)S(1)}, u32[]{:S(2)}, u32[]{:S(2)}) %all-to-all-start.3) | async-done | bytes 1048608 | tf_op jit(solution)/shard_map/all_to_all | solution.py:685
  156.4 0.0 copy-done
  156.4 4.2 %backward.1 = bf16[15,32,1024]{2,1,0:T(8,128)(2,1)} custom-call(s32[1]{0:T(128)} %bitcast.index_ref, bf16[32,8,16,128]{3,2,1,0:T(8,128)(2,1)S(1)} %all-to-all-done.3.rows_ref, bf16[1024,1024]{1,0:T(8,128)(2,1)} %inverse_table.1.table_hbm, bf16[15,32,1024]{2,1,0:T(8,128)(2,1)S(1)} %copy-done), custom_call_target="tpu_custom_call" | custom-call | tf_op jit(solution)/shard_map/backward/pallas_call | solution.py:646
  (1 shorter events, 0.0 us)
Async XLA Ops:
  5.2 32.1 %all-to-all-start = ((bf16[32,8,16,128]{3,2,1,0:T(8,128)(2,1)}), bf16[32,8,16,128]{3,2,1,0:T(8,128)(2,1)S(1)}, u32[]{:S(2)}, u32[]{:S(2)}) async-start(bf16[32,8,16,128]{3,2,1,0:T(8,128)(2,1)} %forward.1), calls=%async_computation | async-start | bytes 2097152 | tf_op jit(solution)/shard_map/all_to_all | solution.py:673
  13.8 6.9 %copy-start.1 = (bf16[2,256,32,15]{1,2,3,0:T(8,128)(2,1)S(1)}, bf16[2,256,32,15]{1,2,3,0:T(8,128)(2,1)}, u32[]{:S(2)}) copy-start(bf16[2,256,32,15]{1,2,3,0:T(8,128)(2,1)} %param.8) | copy-start | bytes 1474564
  13.8 23.5 %copy-start.2 = (s32[480]{0:T(512)S(1)}, s32[480]{0:T(512)}, u32[]{:S(2)}) copy-start(s32[480]{0:T(512)} %slots_ref.3) | copy-start | bytes 5764
  20.8 13.4 %collective-permute-start = (bf16[2,2,32,256]{3,2,1,0:T(8,128)(2,1)S(1)}, bf16[2,2,32,256]{3,2,1,0:T(8,128)(2,1)S(1)}, u32[]{:S(2)}, u32[]{:S(2)}) collective-permute-start(bf16[2,2,32,256]{3,2,1,0:T(8,128)(2,1)S(1)} %get-tuple-element.24), channel_id=1, source_target_pairs={{0,1},{1,2},{2,3},{3,4},{4,5},{5,6},{6,7},{7,0},{8,9},{9,10},{10,1... | collective-permute-start | bytes 196616 | tf_op jit(solution)/shard_map/ppermute | solution.py:586
  22.5 14.1 %collective-permute-start.1 = (bf16[2,2,32,256]{3,2,1,0:T(8,128)(2,1)S(1)}, bf16[2,2,32,256]{3,2,1,0:T(8,128)(2,1)S(1)}, u32[]{:S(2)}, u32[]{:S(2)}) collective-permute-start(bf16[2,2,32,256]{3,2,1,0:T(8,128)(2,1)S(1)} %get-tuple-element.25), channel_id=1, source_target_pairs={{0,2},{1,3},{2,4},{3,5},{4,6},{5,7},{6,0},{7,1},{8,10},{9,11},{10,... | collective-permute-start | bytes 196616 | tf_op jit(solution)/shard_map/ppermute | solution.py:586
  25.5 16.7 %collective-permute-start.2 = (bf16[2,2,32,256]{3,2,1,0:T(8,128)(2,1)S(1)}, bf16[2,2,32,256]{3,2,1,0:T(8,128)(2,1)S(1)}, u32[]{:S(2)}, u32[]{:S(2)}) collective-permute-start(bf16[2,2,32,256]{3,2,1,0:T(8,128)(2,1)S(1)} %get-tuple-element.26), channel_id=1, source_target_pairs={{0,3},{1,4},{2,5},{3,6},{4,7},{5,0},{6,1},{7,2},{8,11},{9,12},{10,... | collective-permute-start | bytes 196616 | tf_op jit(solution)/shard_map/ppermute | solution.py:586
  29.3 13.0 %collective-permute-start.3 = (bf16[2,2,32,256]{3,2,1,0:T(8,128)(2,1)S(1)}, bf16[2,2,32,256]{3,2,1,0:T(8,128)(2,1)S(1)}, u32[]{:S(2)}, u32[]{:S(2)}) collective-permute-start(bf16[2,2,32,256]{3,2,1,0:T(8,128)(2,1)S(1)} %get-tuple-element.27), channel_id=1, source_target_pairs={{0,4},{1,5},{2,6},{3,7},{4,0},{5,1},{6,2},{7,3},{8,12},{9,13},{10,... | collective-permute-start | bytes 196616 | tf_op jit(solution)/shard_map/ppermute | solution.py:586
  29.7 12.5 %collective-permute-start.4 = (bf16[2,2,32,256]{3,2,1,0:T(8,128)(2,1)S(1)}, bf16[2,2,32,256]{3,2,1,0:T(8,128)(2,1)S(1)}, u32[]{:S(2)}, u32[]{:S(2)}) collective-permute-start(bf16[2,2,32,256]{3,2,1,0:T(8,128)(2,1)S(1)} %get-tuple-element.28), channel_id=1, source_target_pairs={{0,5},{1,6},{2,7},{3,0},{4,1},{5,2},{6,3},{7,4},{8,13},{9,14},{10,... | collective-permute-start | bytes 196616 | tf_op jit(solution)/shard_map/ppermute | solution.py:586
  34.2 10.0 %collective-permute-start.5 = (bf16[2,2,32,256]{3,2,1,0:T(8,128)(2,1)S(1)}, bf16[2,2,32,256]{3,2,1,0:T(8,128)(2,1)S(1)}, u32[]{:S(2)}, u32[]{:S(2)}) collective-permute-start(bf16[2,2,32,256]{3,2,1,0:T(8,128)(2,1)S(1)} %get-tuple-element.29), channel_id=1, source_target_pairs={{0,6},{1,7},{2,0},{3,1},{4,2},{5,3},{6,4},{7,5},{8,14},{9,15},{10,... | collective-permute-start | bytes 196616 | tf_op jit(solution)/shard_map/ppermute | solution.py:586
  36.6 7.6 %collective-permute-start.6 = (bf16[2,2,32,256]{3,2,1,0:T(8,128)(2,1)S(1)}, bf16[2,2,32,256]{3,2,1,0:T(8,128)(2,1)S(1)}, u32[]{:S(2)}, u32[]{:S(2)}) collective-permute-start(bf16[2,2,32,256]{3,2,1,0:T(8,128)(2,1)S(1)} %get-tuple-element.30), channel_id=1, source_target_pairs={{0,7},{1,0},{2,1},{3,2},{4,3},{5,4},{6,5},{7,6},{8,15},{9,8},{10,9... | collective-permute-start | bytes 196616 | tf_op jit(solution)/shard_map/ppermute | solution.py:586
  135.0 21.4 %all-to-all-start.3 = ((bf16[32,8,16,128]{3,2,1,0:T(8,128)(2,1)}), bf16[32,8,16,128]{3,2,1,0:T(8,128)(2,1)S(1)}, u32[]{:S(2)}, u32[]{:S(2)}) async-start(bf16[32,8,16,128]{3,2,1,0:T(8,128)(2,1)} %synthesis.1), calls=%async_computation.3 | async-start | bytes 2097152 | tf_op jit(solution)/shard_map/all_to_all | solution.py:685
  139.4 4.1 %copy-start.3 = (bf16[512,480]{1,0:T(8,128)(2,1)S(1)}, bf16[512,480]{1,0:T(8,128)(2,1)}, u32[]{:S(2)}) copy-start(bf16[512,480]{1,0:T(8,128)(2,1)} %constant.20.clone.pick_ref) | copy-start | bytes 1474564
  143.5 12.9 %copy-start = (bf16[15,32,1024]{2,1,0:T(8,128)(2,1)S(1)}, bf16[15,32,1024]{2,1,0:T(8,128)(2,1)}, u32[]{:S(2)}) copy-start(bf16[15,32,1024]{2,1,0:T(8,128)(2,1)} %field_hbm.3) | copy-start | bytes 2949124

commit v6 on v5

--- a/solution.py
+++ b/solution.py
@@ -379,7 +379,7 @@
 
 
 def side_of(wide, count, m):
-    turned = wide[pl.ds(m, count * PAIRS, stride=PITCH), :].T
+    turned = wide[pl.ds(m, count * PAIRS, stride=PITCH), :].astype(bf16).T
     return jnp.concatenate([turned[: LANES // 2], turned[LANES // 2 :]], axis=1)
 
 
@@ -397,14 +397,14 @@
         for m2 in range(2):
             order = order_of(slots_ref, index_ref, ord_dev, 2 * p + m2)
             weight = jnp.where(order == 0, 1.0 / lon, 2.0 / lon)
-            part = side_of(wide, count, 2 * p + m2)
+            part = side_of(wide, count, 2 * p + m2).astype(f32)
             same = parity == (order & 1)
             split = jnp.concatenate([jnp.where(same, part, 0.0), jnp.where(same, 0.0, part)], axis=0)
             prod = jnp.dot(split.astype(bf16), table[2 * p + m2], preferred_element_type=f32)
             north.append((prod[:half] + prod[half:]) * weight)
             south.append((prod[:half] - prod[half:]) * weight)
-        up = jnp.concatenate(north, axis=0).T.astype(bf16)
-        down = jnp.concatenate(south, axis=0).T.astype(bf16)
+        up = jnp.concatenate(north, axis=0).astype(bf16).T
+        down = jnp.concatenate(south, axis=0).astype(bf16).T
         for s in range(count // 2):
             out_ref[s, p] = up[s * PAD : (s + 1) * PAD]
             out_ref[count - 1 - s, p] = down[s * PAD : (s + 1) * PAD]
@@ -416,7 +416,7 @@
 
     @pl.loop(0, ord_dev)
     def _(m):
-        side = side_of(wide, count, m).astype(bf16)
+        side = side_of(wide, count, m)
         spec = jnp.dot(side, pick_ref[...], preferred_element_type=f32).astype(bf16)
         out_ref[m] = spec.reshape(out_ref.shape[1:])
 
@@ -436,7 +436,7 @@
         wide[i * PITCH : i * PITCH + PAD, :] = rows_ref[i // PAIRS, i % PAIRS].astype(f32)
     for j in range(lat_dev):
         slot = slot_of(j, lat_dev, index_ref[0], lat_count)
-        block = wide[pl.ds(slot, half, stride=PITCH), :].T.astype(bf16)
+        block = wide[pl.ds(slot, half, stride=PITCH), :].astype(bf16).T
         for q in range(4):
             left[j * ch_dev : (j + 1) * ch_dev, q * half : (q + 1) * half] = block[
                 q * ch_dev : (q + 1) * ch_dev
@@ -569,10 +569,9 @@
     )(index, orders, rows, table)
 
 
-def exchange_weights(index, weights):
-    ch_count = lax.axis_size("ch")
+def weight_pieces(index, weights, ch_count):
     piece = jax.ShapeDtypeStruct((2, 2) + weights.shape[2:], bf16)
-    pieces = pl.pallas_call(
+    return pl.pallas_call(
         weights_kernel,
         out_shape=(piece,) * ch_count,
         in_specs=[smem, vmem],
@@ -580,11 +579,14 @@
         compiler_params=params(),
         name="weights",
     )(index, weights)
-    moved = [pieces[0]]
-    for k in range(1, ch_count):
-        ring = [(e, (e + k) % ch_count) for e in range(ch_count)]
-        moved.append(lax.ppermute(pieces[k], "ch", ring))
-    return moved
+
+
+def move_along(pieces, steps):
+    count = len(pieces)
+    pieces = list(pieces)
+    for k in steps:
+        pieces[k] = lax.ppermute(pieces[k], "ch", [(e, (e + k) % count) for e in range(count)])
+    return tuple(pieces)
 
 
 def call_mix(index, coeffs, weights):
@@ -675,9 +677,13 @@
     weights = jnp.transpose(mix_weight, (0, 3, 2, 1))
     weights, legendre = lax.optimization_barrier((weights, legendre))
     ch_index = lax.axis_index("ch").reshape(1)
-    weights = exchange_weights(ch_index, weights)
+    ch_count = lax.axis_size("ch")
+    far = sorted(range(1, ch_count), key=lambda k: -min(k, ch_count - k))[: ch_count // 2]
+    near = [k for k in range(1, ch_count) if k not in far]
+    weights = move_along(weight_pieces(ch_index, weights, ch_count), far)
     coeffs = call_analysis(ord_dev, index, order_slots, rows, legendre)
     coeffs, weights = lax.optimization_barrier((coeffs, weights))
+    weights = move_along(weights, near)
     coeffs = lax.all_to_all(coeffs.reshape(-1, PAD, LANES), ("lat", "ch"), 0, 0, tiled=True)
     mixed = call_mix(ch_index, coeffs.reshape(rows.shape), weights)
     mixed = lax.all_to_all(mixed.reshape(-1, PAD, LANES), ("lat", "ch"), 0, 0, tiled=True).reshape(rows.shape)

time: 161 us -> 160 us (level)
  blocking collectives: 81.5 us -> 40.4 us
  waiting for transfers between devices: 9.88 us -> 33.9 us
  starting transfers between devices: 29.5 us -> 44.5 us
    all_to_all x1 -> x0, blocking collectives: 43.4 us -> none  [on_device(): lax.all_to_all(coeffs.reshape(-1, PAD, LANES), ('lat', 'ch'), 0, 0, tiled...]
    ppermute x7, waiting for transfers between devices: 1.94 us -> 20.6 us  [move_along(): lax.ppermute(pieces[k], 'ch', [(e, (e + k) % count) for e in range(count)])]
    all_to_all x0 -> x1, starting transfers between devices: none -> 12.3 us  [on_device(): lax.all_to_all(coeffs.reshape(-1, PAD, LANES), ('lat', 'ch'), 0, 0, tiled...]
    all_to_all x0 -> x1, waiting for transfers between devices: none -> 5.06 us  [on_device(): lax.all_to_all(coeffs.reshape(-1, PAD, LANES), ('lat', 'ch'), 0, 0, tiled...]
    ppermute x7, starting transfers between devices: 16.5 us -> 19.2 us  [move_along(): lax.ppermute(pieces[k], 'ch', [(e, (e + k) % count) for e in range(count)])]
    all_to_all x1, blocking collectives: 38.1 us -> 40.4 us  [on_device(): lax.all_to_all(mixed.reshape(-1, PAD, LANES), ('lat', 'ch'), 0, 0, tiled=...]
  transfers between devices with their start and end apart: 9 -> 10, of which waited for: 2 -> 3; matrix products, arithmetic and copies ran while one was open for 0% -> 0% of each run, Pallas kernels for 13% -> 14%
where the time goes in v6:
time: 160 us; the launch traced here: 159 us
  starting transfers between devices  44.5 us (28%)
  blocking collectives  40.4 us (25%)
  Pallas kernels  39.4 us (25%)
  waiting for transfers between devices  33.9 us (21%)
    all_to_all x1, blocking collectives, on_device(): lax.all_to_all(mixed.reshape(-1, PAD, LANES), ('lat', 'ch'), 0, 0, tiled=...  40.4 us
    ppermute x7, waiting for transfers between devices, move_along(): lax.ppermute(pieces[k], 'ch', [(e, (e + k) % count) for e in range(count)])  20.6 us
    ppermute x7, starting transfers between devices, move_along(): lax.ppermute(pieces[k], 'ch', [(e, (e + k) % count) for e in range(count)])  19.2 us
    all_to_all x1, starting transfers between devices, on_device(): lax.all_to_all(coeffs.reshape(-1, PAD, LANES), ('lat', 'ch'), 0, 0, tiled...  12.3 us
    all_to_all x1, starting transfers between devices, on_device(): rows = lax.all_to_all(rows, 'lat', 0, 0, tiled=True)  8.6 us
    all_to_all x1, waiting for transfers between devices, on_device(): synth = lax.all_to_all(synth, 'lat', 0, 0, tiled=True)  8.25 us
    pallas_call x1, Pallas kernels, call_legendre(): pl.pallas_call(functools.partial(legendre_kernel, ord_dev), out_shape=jax...  6.91 us
    pallas_call x1, Pallas kernels, call_analysis(): pl.pallas_call(functools.partial(analysis_kernel, ord_dev), out_shape=jax...  5.87 us
  transfers between devices with their start and end apart: 10, of which 3 were waited for; matrix products, arithmetic and copies ran while one was open for 0% of the time, Pallas kernels for 14%

profile of v6, /device:TPU:1, one launch (start us, length us, event | category | flops | bytes accessed | tf_op | source)
XLA Modules:
  0.0 159.2 jit_solution(5698522945312390440)
XLA Ops:
  0.6 4.6 %forward.1 = bf16[32,8,16,128]{3,2,1,0:T(8,128)(2,1)} custom-call(s32[1]{0:T(128)} %bitcast.index_ref, s32[1,480]{1,0:T(1,128)} %bitcast.14, bf16[15,32,1024]{2,1,0:T(8,128)(2,1)} %field_hbm.3), custom_call_target="tpu_custom_call" | custom-call | tf_op jit(solution)/shard_map/forward/pallas_call | solution.py:477
  5.2 8.6 %all-to-all-start = ((bf16[32,8,16,128]{3,2,1,0:T(8,128)(2,1)}), bf16[32,8,16,128]{3,2,1,0:T(8,128)(2,1)S(1)}, u32[]{:S(2)}, u32[]{:S(2)}) async-start(bf16[32,8,16,128]{3,2,1,0:T(8,128)(2,1)} %forward.1), calls=%async_computation | async-start | bytes 2097152 | tf_op jit(solution)/shard_map/all_to_all | solution.py:675
  13.8 0.0 copy-start.1
  13.8 0.0 copy-start.2
  13.8 6.9 %legendre.1 = bf16[16,2,16,16,256]{4,3,2,1,0:T(8,128)(2,1)} custom-call(s32[1]{0:T(128)} %bitcast.index_ref, f32[2,480]{1,0:T(2,128)} %constant.17.clone.scale_ref, s32[1,480]{1,0:T(1,128)} %bitcast.15, f32[2,256]{1,0:T(2,128)} %constant.18.clone.geo_ref, f32[1,512]{1,0:T(1,128)} %constant.19.clone.prod_ref), custom_call_target="tpu_custom_call" | custom-call | flops 8000000000 | bytes 20000000 | tf_op jit(solution)/shard_map/legendre/pallas_call | solution.py:518
  20.8 0.0 copy-done.1
  20.8 3.1 %collective-permute-start = (bf16[2,2,32,256]{3,2,1,0:T(8,128)(2,1)S(1)}, bf16[2,2,32,256]{3,2,1,0:T(8,128)(2,1)S(1)}, u32[]{:S(2)}, u32[]{:S(2)}) collective-permute-start(bf16[2,2,32,256]{3,2,1,0:T(8,128)(2,1)S(1)} %get-tuple-element.25), channel_id=1, source_target_pairs={{0,2},{1,3},{2,4},{3,5},{4,6},{5,7},{6,0},{7,1},{8,10},{9,11},{10,... | collective-permute-start | bytes 196616 | tf_op jit(solution)/shard_map/ppermute | solution.py:588
  23.9 4.7 %collective-permute-start.1 = (bf16[2,2,32,256]{3,2,1,0:T(8,128)(2,1)S(1)}, bf16[2,2,32,256]{3,2,1,0:T(8,128)(2,1)S(1)}, u32[]{:S(2)}, u32[]{:S(2)}) collective-permute-start(bf16[2,2,32,256]{3,2,1,0:T(8,128)(2,1)S(1)} %get-tuple-element.26), channel_id=1, source_target_pairs={{0,3},{1,4},{2,5},{3,6},{4,7},{5,0},{6,1},{7,2},{8,11},{9,12},{10,... | collective-permute-start | bytes 196616 | tf_op jit(solution)/shard_map/ppermute | solution.py:588
  28.5 1.0 collective-permute-start.2
  29.5 3.9 %collective-permute-start.3 = (bf16[2,2,32,256]{3,2,1,0:T(8,128)(2,1)S(1)}, bf16[2,2,32,256]{3,2,1,0:T(8,128)(2,1)S(1)}, u32[]{:S(2)}, u32[]{:S(2)}) collective-permute-start(bf16[2,2,32,256]{3,2,1,0:T(8,128)(2,1)S(1)} %get-tuple-element.28), channel_id=1, source_target_pairs={{0,5},{1,6},{2,7},{3,0},{4,1},{5,2},{6,3},{7,4},{8,13},{9,14},{10,... | collective-permute-start | bytes 196616 | tf_op jit(solution)/shard_map/ppermute | solution.py:588
  33.5 0.0 all-to-all-done.rows_ref
  33.5 0.0 copy-done.2
  33.5 5.9 %analysis.1 = bf16[32,8,16,128]{3,2,1,0:T(8,128)(2,1)} custom-call(s32[1]{0:T(128)} %bitcast.index_ref, s32[480]{0:T(512)S(1)} %copy-done.2, bf16[32,8,16,128]{3,2,1,0:T(8,128)(2,1)S(1)} %all-to-all-done.rows_ref, bf16[16,512,256]{2,1,0:T(8,128)(2,1)} %bitcast.17), custom_call_target="tpu_custom_call" | custom-call | tf_op jit(solution)/shard_map/analysis/pallas_call | solution.py:557
  39.4 0.0 collective-permute-done.refs_2_
  39.4 0.0 collective-permute-done.1.refs_3_
  39.4 0.0 collective-permute-done.2.refs_4_
  39.4 0.0 collective-permute-done.3.refs_5_
  39.4 12.3 %all-to-all-start.1 = ((bf16[256,16,128]{2,1,0:T(8,128)(2,1)}), bf16[256,16,128]{2,1,0:T(8,128)(2,1)S(1)}, u32[]{:S(2)}, u32[]{:S(2)}) async-start(bf16[256,16,128]{2,1,0:T(8,128)(2,1)} %bitcast.5), calls=%async_computation.1 | async-start | bytes 2097152 | tf_op jit(solution)/shard_map/all_to_all | solution.py:687
  51.7 1.6 collective-permute-start.4
  53.3 4.0 %collective-permute-start.5 = (bf16[2,2,32,256]{3,2,1,0:T(8,128)(2,1)S(1)}, bf16[2,2,32,256]{3,2,1,0:T(8,128)(2,1)S(1)}, u32[]{:S(2)}, u32[]{:S(2)}) collective-permute-start(bf16[2,2,32,256]{3,2,1,0:T(8,128)(2,1)S(1)} %get-tuple-element.38), channel_id=1, source_target_pairs={{0,6},{1,7},{2,0},{3,1},{4,2},{5,3},{6,4},{7,5},{8,14},{9,15},{10,... | collective-permute-start | bytes 196616 | tf_op jit(solution)/shard_map/ppermute | solution.py:588
  57.3 0.9 collective-permute-start.6
  58.2 20.6 %collective-permute-done.4.refs_1_ = bf16[2,2,32,256]{3,2,1,0:T(8,128)(2,1)S(1)} collective-permute-done((bf16[2,2,32,256]{3,2,1,0:T(8,128)(2,1)S(1)}, bf16[2,2,32,256]{3,2,1,0:T(8,128)(2,1)S(1)}, u32[]{:S(2)}, u32[]{:S(2)}) %collective-permute-start.4) | collective-permute-done | bytes 65568 | tf_op jit(solution)/shard_map/ppermute | solution.py:588
  78.8 0.0 collective-permute-done.5.refs_6_
  78.8 0.0 collective-permute-done.6.refs_7_
  78.8 5.1 %all-to-all-done.1 = bf16[256,16,128]{2,1,0:T(8,128)(2,1)S(1)} async-done(((bf16[256,16,128]{2,1,0:T(8,128)(2,1)}), bf16[256,16,128]{2,1,0:T(8,128)(2,1)S(1)}, u32[]{:S(2)}, u32[]{:S(2)}) %all-to-all-start.1) | async-done | bytes 1048608 | tf_op jit(solution)/shard_map/all_to_all | solution.py:687
  83.9 3.6 %mix.1 = bf16[32,8,16,128]{3,2,1,0:T(8,128)(2,1)S(1)} custom-call(s32[1]{0:T(128)} %bitcast.1.index_ref, bf16[32,8,16,128]{3,2,1,0:T(8,128)(2,1)S(1)} %bitcast.9, bf16[2,2,32,256]{3,2,1,0:T(8,128)(2,1)S(1)} %get-tuple-element.32.refs_0_, bf16[2,2,32,256]{3,2,1,0:T(8,128)(2,1)S(1)} %collective-permute-done.4.refs_1_, ...), custom_call_target="tpu_custom_call" | custom-call | tf_op jit(solution)/shard_map/mix/pallas_call | solution.py:594
  87.5 40.4 %all_to_all.20 = bf16[256,16,128]{2,1,0:T(8,128)(2,1)S(1)} all-to-all(bf16[256,16,128]{2,1,0:T(8,128)(2,1)S(1)} %bitcast.10), channel_id=1, replica_groups=mesh['lat'=32,'ch'=8] {'lat','ch'}, dimensions={0} | all-to-all | bytes 2097152 | tf_op jit(solution)/shard_map/all_to_all | solution.py:689
  127.9 5.4 %synthesis.1 = bf16[32,8,16,128]{3,2,1,0:T(8,128)(2,1)} custom-call(s32[1]{0:T(128)} %bitcast.index_ref, s32[480]{0:T(512)S(1)} %copy-done.2, bf16[32,8,16,128]{3,2,1,0:T(8,128)(2,1)S(1)} %bitcast.11, bf16[16,512,256]{2,1,0:T(8,128)(2,1)} %bitcast.18), custom_call_target="tpu_custom_call" | custom-call | tf_op jit(solution)/shard_map/synthesis/pallas_call | solution.py:610
  133.4 4.4 %all-to-all-start.3 = ((bf16[32,8,16,128]{3,2,1,0:T(8,128)(2,1)}), bf16[32,8,16,128]{3,2,1,0:T(8,128)(2,1)S(1)}, u32[]{:S(2)}, u32[]{:S(2)}) async-start(bf16[32,8,16,128]{3,2,1,0:T(8,128)(2,1)} %synthesis.1), calls=%async_computation.3 | async-start | bytes 2097152 | tf_op jit(solution)/shard_map/all_to_all | solution.py:691
  137.8 0.0 copy-start.3
  137.8 4.1 %inverse_table.1.table_hbm = bf16[1024,1024]{1,0:T(8,128)(2,1)} custom-call(s32[1,480]{1,0:T(1,128)} %bitcast.16), custom_call_target="tpu_custom_call" | custom-call | flops 2000000000 | bytes 4000000 | tf_op jit(solution)/shard_map/inverse_table/pallas_call | solution.py:539
  141.9 0.0 copy-done.3
  141.9 0.0 copy-start
  141.9 4.6 %spectrum.1 = bf16[15,2,32,480]{3,2,1,0:T(8,128)(2,1)} custom-call(bf16[32,8,16,128]{3,2,1,0:T(8,128)(2,1)S(1)} %bitcast.12, bf16[512,480]{1,0:T(8,128)(2,1)S(1)} %copy-done.3), custom_call_target="tpu_custom_call" | custom-call | flops 3000000000 | bytes 4000000 | tf_op jit(solution)/shard_map/spectrum/pallas_call | solution.py:632
  146.6 8.2 %all-to-all-done.3.rows_ref = bf16[32,8,16,128]{3,2,1,0:T(8,128)(2,1)S(1)} async-done(((bf16[32,8,16,128]{3,2,1,0:T(8,128)(2,1)}), bf16[32,8,16,128]{3,2,1,0:T(8,128)(2,1)S(1)}, u32[]{:S(2)}, u32[]{:S(2)}) %all-to-all-start.3) | async-done | bytes 1048608 | tf_op jit(solution)/shard_map/all_to_all | solution.py:691
  154.8 0.0 copy-done
  154.8 4.2 %backward.1 = bf16[15,32,1024]{2,1,0:T(8,128)(2,1)} custom-call(s32[1]{0:T(128)} %bitcast.index_ref, bf16[32,8,16,128]{3,2,1,0:T(8,128)(2,1)S(1)} %all-to-all-done.3.rows_ref, bf16[1024,1024]{1,0:T(8,128)(2,1)} %inverse_table.1.table_hbm, bf16[15,32,1024]{2,1,0:T(8,128)(2,1)S(1)} %copy-done), custom_call_target="tpu_custom_call" | custom-call | tf_op jit(solution)/shard_map/backward/pallas_call | solution.py:648
  (1 shorter events, 0.0 us)
Async XLA Ops:
  5.2 28.3 %all-to-all-start = ((bf16[32,8,16,128]{3,2,1,0:T(8,128)(2,1)}), bf16[32,8,16,128]{3,2,1,0:T(8,128)(2,1)S(1)}, u32[]{:S(2)}, u32[]{:S(2)}) async-start(bf16[32,8,16,128]{3,2,1,0:T(8,128)(2,1)} %forward.1), calls=%async_computation | async-start | bytes 2097152 | tf_op jit(solution)/shard_map/all_to_all | solution.py:675
  13.8 6.9 %copy-start.1 = (bf16[2,256,32,15]{1,2,3,0:T(8,128)(2,1)S(1)}, bf16[2,256,32,15]{1,2,3,0:T(8,128)(2,1)}, u32[]{:S(2)}) copy-start(bf16[2,256,32,15]{1,2,3,0:T(8,128)(2,1)} %param.8) | copy-start | bytes 1474564
  13.8 19.7 %copy-start.2 = (s32[480]{0:T(512)S(1)}, s32[480]{0:T(512)}, u32[]{:S(2)}) copy-start(s32[480]{0:T(512)} %slots_ref.3) | copy-start | bytes 5764
  20.8 18.5 %collective-permute-start = (bf16[2,2,32,256]{3,2,1,0:T(8,128)(2,1)S(1)}, bf16[2,2,32,256]{3,2,1,0:T(8,128)(2,1)S(1)}, u32[]{:S(2)}, u32[]{:S(2)}) collective-permute-start(bf16[2,2,32,256]{3,2,1,0:T(8,128)(2,1)S(1)} %get-tuple-element.25), channel_id=1, source_target_pairs={{0,2},{1,3},{2,4},{3,5},{4,6},{5,7},{6,0},{7,1},{8,10},{9,11},{10,... | collective-permute-start | bytes 196616 | tf_op jit(solution)/shard_map/ppermute | solution.py:588
  23.9 15.5 %collective-permute-start.1 = (bf16[2,2,32,256]{3,2,1,0:T(8,128)(2,1)S(1)}, bf16[2,2,32,256]{3,2,1,0:T(8,128)(2,1)S(1)}, u32[]{:S(2)}, u32[]{:S(2)}) collective-permute-start(bf16[2,2,32,256]{3,2,1,0:T(8,128)(2,1)S(1)} %get-tuple-element.26), channel_id=1, source_target_pairs={{0,3},{1,4},{2,5},{3,6},{4,7},{5,0},{6,1},{7,2},{8,11},{9,12},{10,... | collective-permute-start | bytes 196616 | tf_op jit(solution)/shard_map/ppermute | solution.py:588
  28.5 10.8 %collective-permute-start.2 = (bf16[2,2,32,256]{3,2,1,0:T(8,128)(2,1)S(1)}, bf16[2,2,32,256]{3,2,1,0:T(8,128)(2,1)S(1)}, u32[]{:S(2)}, u32[]{:S(2)}) collective-permute-start(bf16[2,2,32,256]{3,2,1,0:T(8,128)(2,1)S(1)} %get-tuple-element.27), channel_id=1, source_target_pairs={{0,4},{1,5},{2,6},{3,7},{4,0},{5,1},{6,2},{7,3},{8,12},{9,13},{10,... | collective-permute-start | bytes 196616 | tf_op jit(solution)/shard_map/ppermute | solution.py:588
  29.5 9.8 %collective-permute-start.3 = (bf16[2,2,32,256]{3,2,1,0:T(8,128)(2,1)S(1)}, bf16[2,2,32,256]{3,2,1,0:T(8,128)(2,1)S(1)}, u32[]{:S(2)}, u32[]{:S(2)}) collective-permute-start(bf16[2,2,32,256]{3,2,1,0:T(8,128)(2,1)S(1)} %get-tuple-element.28), channel_id=1, source_target_pairs={{0,5},{1,6},{2,7},{3,0},{4,1},{5,2},{6,3},{7,4},{8,13},{9,14},{10,... | collective-permute-start | bytes 196616 | tf_op jit(solution)/shard_map/ppermute | solution.py:588
  39.4 44.5 %all-to-all-start.1 = ((bf16[256,16,128]{2,1,0:T(8,128)(2,1)}), bf16[256,16,128]{2,1,0:T(8,128)(2,1)S(1)}, u32[]{:S(2)}, u32[]{:S(2)}) async-start(bf16[256,16,128]{2,1,0:T(8,128)(2,1)} %bitcast.5), calls=%async_computation.1 | async-start | bytes 2097152 | tf_op jit(solution)/shard_map/all_to_all | solution.py:687
  51.7 27.1 %collective-permute-start.4 = (bf16[2,2,32,256]{3,2,1,0:T(8,128)(2,1)S(1)}, bf16[2,2,32,256]{3,2,1,0:T(8,128)(2,1)S(1)}, u32[]{:S(2)}, u32[]{:S(2)}) collective-permute-start(bf16[2,2,32,256]{3,2,1,0:T(8,128)(2,1)S(1)} %get-tuple-element.33), channel_id=1, source_target_pairs={{0,1},{1,2},{2,3},{3,4},{4,5},{5,6},{6,7},{7,0},{8,9},{9,10},{10,1... | collective-permute-start | bytes 196616 | tf_op jit(solution)/shard_map/ppermute | solution.py:588
  53.3 25.5 %collective-permute-start.5 = (bf16[2,2,32,256]{3,2,1,0:T(8,128)(2,1)S(1)}, bf16[2,2,32,256]{3,2,1,0:T(8,128)(2,1)S(1)}, u32[]{:S(2)}, u32[]{:S(2)}) collective-permute-start(bf16[2,2,32,256]{3,2,1,0:T(8,128)(2,1)S(1)} %get-tuple-element.38), channel_id=1, source_target_pairs={{0,6},{1,7},{2,0},{3,1},{4,2},{5,3},{6,4},{7,5},{8,14},{9,15},{10,... | collective-permute-start | bytes 196616 | tf_op jit(solution)/shard_map/ppermute | solution.py:588
  57.3 21.5 %collective-permute-start.6 = (bf16[2,2,32,256]{3,2,1,0:T(8,128)(2,1)S(1)}, bf16[2,2,32,256]{3,2,1,0:T(8,128)(2,1)S(1)}, u32[]{:S(2)}, u32[]{:S(2)}) collective-permute-start(bf16[2,2,32,256]{3,2,1,0:T(8,128)(2,1)S(1)} %get-tuple-element.39), channel_id=1, source_target_pairs={{0,7},{1,0},{2,1},{3,2},{4,3},{5,4},{6,5},{7,6},{8,15},{9,8},{10,9... | collective-permute-start | bytes 196616 | tf_op jit(solution)/shard_map/ppermute | solution.py:588
  133.4 21.4 %all-to-all-start.3 = ((bf16[32,8,16,128]{3,2,1,0:T(8,128)(2,1)}), bf16[32,8,16,128]{3,2,1,0:T(8,128)(2,1)S(1)}, u32[]{:S(2)}, u32[]{:S(2)}) async-start(bf16[32,8,16,128]{3,2,1,0:T(8,128)(2,1)} %synthesis.1), calls=%async_computation.3 | async-start | bytes 2097152 | tf_op jit(solution)/shard_map/all_to_all | solution.py:691
  137.8 4.1 %copy-start.3 = (bf16[512,480]{1,0:T(8,128)(2,1)S(1)}, bf16[512,480]{1,0:T(8,128)(2,1)}, u32[]{:S(2)}) copy-start(bf16[512,480]{1,0:T(8,128)(2,1)} %constant.20.clone.pick_ref) | copy-start | bytes 1474564
  141.9 12.9 %copy-start = (bf16[15,32,1024]{2,1,0:T(8,128)(2,1)S(1)}, bf16[15,32,1024]{2,1,0:T(8,128)(2,1)}, u32[]{:S(2)}) copy-start(bf16[15,32,1024]{2,1,0:T(8,128)(2,1)} %field_hbm.3) | copy-start | bytes 2949124

commit v7 on v6

--- a/solution.py
+++ b/solution.py
@@ -108,6 +108,22 @@
     return jnp.where(index < lat_count // 2, j, lat_dev - 1 - j)
 
 
+def narrow(wide, out_ref, out_hbm, sems):
+    count = out_ref.shape[0]
+    part = count // sems.shape[0]
+    copies = []
+    for d in range(count):
+        for p in range(PAIRS):
+            i = d * PAIRS + p
+            out_ref[d, p] = wide[i * PITCH : i * PITCH + PAD, :].astype(bf16)
+        if d % part == part - 1:
+            cut = slice(d + 1 - part, d + 1)
+            copies.append(pltpu.make_async_copy(out_ref.at[cut], out_hbm.at[cut], sems.at[d // part]))
+            copies[-1].start()
+    for copy in copies:
+        copy.wait()
+
+
 def forward_kernel(
     lat_dev, lat_count, ord_dev, index_ref, slots_ref, field_hbm, out_hbm, table, field_ref, rows, turned, out_ref, sem, sems
 ):
@@ -144,20 +160,9 @@
         place = jnp.full((1, half), index * lat_dev + j, jnp.int32).astype(f32)
         quad = cos_turns((place + 0.5) * (0.5 / lat_total) - 0.25) * (math.pi / lat_total)
         block = rows[j].reshape(4 * ch_dev, half) * quad
-        turned[pl.ds(slot_of(j, lat_dev, index, lat_count), half, stride=PITCH), :] = block.T
+        turned[pl.ds(slot_of(j, lat_dev, index, lat_count), half, stride=PITCH), :] = block.astype(bf16).T.astype(f32)
     turned[pl.ds(lat_dev, half, stride=PITCH), :] = jnp.zeros((half, LANES), f32)
-    copies = []
-    part = lat_count // sems.shape[0]
-    for d in range(lat_count):
-        for p in range(PAIRS):
-            i = d * PAIRS + p
-            out_ref[d, p] = turned[i * PITCH : i * PITCH + PAD, :].astype(bf16)
-        if d % part == part - 1:
-            cut = slice(d + 1 - part, d + 1)
-            copies.append(pltpu.make_async_copy(out_ref.at[cut], out_hbm.at[cut], sems.at[d // part]))
-            copies[-1].start()
-    for copy in copies:
-        copy.wait()
+    narrow(turned, out_ref, out_hbm, sems)
 
 
 def inverse_table_kernel(ord_dev, lat_count, slots_ref, out_hbm, out_ref, orders, sem):
@@ -187,7 +192,7 @@
 
 
 def legendre_kernel(
-    deg_dev, index_ref, scale_ref, slots_ref, geo_ref, prod_ref, out_hbm, cur, bef, resc, start, expo, root, buf, table, sems
+    deg_dev, index_ref, slots_ref, geo_ref, prod_ref, out_hbm, cur, bef, resc, start, expo, buf, table, sems
 ):
     groups = cur.shape[0]
     pitch = 2 * PAD + 1
@@ -198,7 +203,7 @@
     order = order_column(slots_ref[...].astype(f32), jnp.where(row < deg_dev, index_ref[0] * deg_dev + row, -1))
     order = jnp.broadcast_to(jnp.where(row < deg_dev, order, 1.0 * NO_ORDER), (PAD, LANES))
     order_sq = order * order
-    for state in (cur, bef, resc, root):
+    for state in (cur, bef, resc):
         state[...] = jnp.zeros_like(state)
     picked = jnp.zeros((PAD, 1), f32)
     for g in range(prod_ref.shape[1] // LANES):
@@ -219,20 +224,23 @@
         old = [bef[g] for g in range(groups)]
         factor = [expo[g] for g in range(groups)]
         cosine = [geo_ref[0:1, g * LANES : (g + 1) * LANES] for g in range(groups)]
-        root_prev = root[...]
+        lane = lax.broadcasted_iota(jnp.int32, (PAD, LANES), 1) + 2 * index * deg_dev
+        degs = lane.astype(f32)
+        prev = degs - 1.0
+        alphas = jnp.sqrt(
+            jnp.maximum(4.0 * degs * degs - 1.0, 1.0) / jnp.maximum(degs * degs - order_sq, 1.0)
+        )
+        betas = jnp.sqrt(
+            jnp.maximum(prev * prev - order_sq, 0.0) / jnp.maximum(4.0 * prev * prev - 1.0, 1.0)
+        )
         for twin, i in [(t, k) for t in range(2) for k in range(deg_dev)]:
-            degree = (2 * index + twin) * deg_dev + i
-            deg = degree.astype(f32)
-            gap = deg * deg - order_sq
-            gap_one = jnp.maximum(gap, 1.0)
-            inv = lax.rsqrt(gap_one)
-            inv = inv * (1.5 - 0.5 * gap_one * inv * inv)
-            alpha = inv * scale_ref[0, degree]
-            beta = root_prev * scale_ref[1, degree]
-            root_prev = jnp.maximum(gap, 0.0) * inv
-            begin = jnp.where(order == deg, 1.0, 0.0)
+            at = twin * deg_dev + i
+            alpha = jnp.broadcast_to(alphas[:, at : at + 1], (PAD, LANES))
+            beta = jnp.broadcast_to(betas[:, at : at + 1], (PAD, LANES))
+            both = alpha * beta
+            begin = jnp.where(order == (2 * index * deg_dev + at).astype(f32), 1.0, 0.0)
             for g in range(groups):
-                new = alpha * (cosine[g] * now[g] - beta * old[g]) + begin
+                new = (alpha * cosine[g]) * now[g] + (begin - both * old[g])
                 old[g], now[g] = now[g], new
                 row = i % 2 * PAD + twin * PAIRS + i // 2
                 buf[g, pl.ds(row, PAD, stride=pitch), :] = new * factor[g]
@@ -245,7 +253,6 @@
                     count = resc[g] + jnp.where(large, 1.0, 0.0)
                     resc[g] = count
                     factor[g] = jnp.exp(start[g] + count * log_step)
-        root[...] = root_prev
         for g in range(groups):
             cur[g] = now[g]
             bef[g] = old[g]
@@ -288,7 +295,9 @@
     return copy
 
 
-def analysis_kernel(ord_dev, index_ref, slots_ref, rows_ref, table_hbm, out_ref, table, wide, sems):
+def analysis_kernel(
+    ord_dev, index_ref, slots_ref, rows_ref, table_hbm, out_hbm, table, wide, sems, out_ref, leave
+):
     copy = fetch_pairs(table_hbm, table, sems)
     count = rows_ref.shape[0]
     half = count * PAIRS
@@ -313,8 +322,7 @@
             lane = lax.broadcasted_iota(jnp.int32, low.shape, 1)
             wide[pl.ds(2 * p + m2, half, stride=PITCH), :] = jnp.where(lane < LANES // 2, low, high)
 
-    for i in range(half):
-        out_ref[i // PAIRS, i % PAIRS] = wide[i * PITCH : i * PITCH + PAD, :].astype(bf16)
+    narrow(wide, out_ref, out_hbm, leave)
 
 
 def weights_kernel(index_ref, weight_ref, *out_refs):
@@ -383,12 +391,15 @@
     return jnp.concatenate([turned[: LANES // 2], turned[LANES // 2 :]], axis=1)
 
 
-def synthesis_kernel(ord_dev, lon, index_ref, slots_ref, mixed_ref, table_hbm, out_ref, table, wide, sems):
+def synthesis_kernel(ord_dev, lon, index_ref, slots_ref, mixed_ref, table_hbm, out_hbm, table, wide, sems, out_ref, leave):
     copy = fetch_pairs(table_hbm, table, sems)
     widen(mixed_ref, wide)
     count = out_ref.shape[0]
     half = LANES // 2
     parity = degree_parity((half, table.shape[1]), 1, ord_dev)
+
+    def sent(p):
+        return pltpu.make_async_copy(out_ref.at[:, p], out_hbm.at[:, p], leave.at[p])
 
     @pl.loop(0, PAIRS)
     def _(p):
@@ -408,6 +419,10 @@
         for s in range(count // 2):
             out_ref[s, p] = up[s * PAD : (s + 1) * PAD]
             out_ref[count - 1 - s, p] = down[s * PAD : (s + 1) * PAD]
+        sent(p).start()
+
+    for p in range(PAIRS):
+        sent(p).wait()
 
 
 def spectrum_kernel(ord_dev, mixed_ref, pick_ref, out_ref, wide):
@@ -507,22 +522,16 @@
     k = np.arange(1, modes)
     prod = np.zeros((1, full), np.float32)
     prod[0, 1:modes] = np.cumsum(0.5 * np.log((2.0 * k - 1.0) / (2.0 * k)))
-    deg = np.arange(modes, dtype=np.float64)
-    scale = np.sqrt(np.maximum(4.0 * deg * deg - 1.0, 1.0))
-    scales = np.ones((2, modes), np.float32)
-    scales[0] = scale
-    scales[1, 1:] = 1.0 / scale[:-1]
     groups = near // LANES
     parts = 4
     state = pltpu.VMEM((groups, PAD, LANES), f32)
     table = pl.pallas_call(
         functools.partial(legendre_kernel, ord_dev),
         out_shape=jax.ShapeDtypeStruct((PAD, 2, lat_count // 2, PAD, near), bf16),
-        in_specs=[smem, smem, vmem, vmem, vmem],
+        in_specs=[smem, vmem, vmem, vmem],
         out_specs=hbm,
         scratch_shapes=[state] * 5
         + [
-            pltpu.VMEM((PAD, LANES), f32),
             pltpu.VMEM((groups, PAD * (2 * PAD + 1), LANES), f32),
             pltpu.VMEM((PAD, 2, lat_count // 2, PAD, near), bf16),
             pltpu.SemaphoreType.DMA((parts,)),
@@ -530,7 +539,7 @@
         compiler_params=params(TABLE_MIB),
         cost_estimate=cost(8e9, 2e7),
         name="legendre",
-    )(index, jnp.asarray(scales), slots, jnp.asarray(geo), jnp.asarray(prod))
+    )(index, slots, jnp.asarray(geo), jnp.asarray(prod))
     return table.reshape(PAD, full, near)
 
 
@@ -558,11 +567,13 @@
         functools.partial(analysis_kernel, ord_dev),
         out_shape=jax.ShapeDtypeStruct(rows.shape, bf16),
         in_specs=[smem, smem, vmem, hbm],
-        out_specs=vmem,
+        out_specs=hbm,
         scratch_shapes=[
             pltpu.VMEM(table.shape, bf16),
             pltpu.VMEM((lat_count * PAIRS * PITCH, LANES), f32),
             pltpu.SemaphoreType.DMA((PAIRS,)),
+            pltpu.VMEM((lat_count, PAIRS, PAD, LANES), bf16),
+            pltpu.SemaphoreType.DMA((4,)),
         ],
         compiler_params=params(),
         name="analysis",
@@ -611,10 +622,12 @@
         functools.partial(synthesis_kernel, ord_dev, lon),
         out_shape=buffer_of(mixed.shape[0]),
         in_specs=[smem, smem, vmem, hbm],
-        out_specs=vmem,
+        out_specs=hbm,
         scratch_shapes=[
             pltpu.VMEM(table.shape, bf16),
             pltpu.VMEM((lat_count * PAIRS * PITCH, LANES), f32),
+            pltpu.SemaphoreType.DMA((PAIRS,)),
+            pltpu.VMEM((lat_count, PAIRS, PAD, LANES), bf16),
             pltpu.SemaphoreType.DMA((PAIRS,)),
         ],
         compiler_params=params(),

time: 160 us -> 159 us (level)
  no operation moved by 1% of the time
where the time goes in v7:
time: 159 us
  starting transfers between devices  44.5 us (28%)
  blocking collectives  40.4 us (25%)
  Pallas kernels  38.9 us (24%)
  waiting for transfers between devices  33.9 us (21%)
    all_to_all x1, blocking collectives, on_device(): lax.all_to_all(mixed.reshape(-1, PAD, LANES), ('lat', 'ch'), 0, 0, tiled=...  40.4 us
    ppermute x7, waiting for transfers between devices, move_along(): lax.ppermute(pieces[k], 'ch', [(e, (e + k) % count) for e in range(count)])  20.6 us
    ppermute x7, starting transfers between devices, move_along(): lax.ppermute(pieces[k], 'ch', [(e, (e + k) % count) for e in range(count)])  19.2 us
    all_to_all x1, starting transfers between devices, on_device(): lax.all_to_all(coeffs.reshape(-1, PAD, LANES), ('lat', 'ch'), 0, 0, tiled...  12.3 us
    all_to_all x1, starting transfers between devices, on_device(): rows = lax.all_to_all(rows, 'lat', 0, 0, tiled=True)  8.6 us
    all_to_all x1, waiting for transfers between devices, on_device(): synth = lax.all_to_all(synth, 'lat', 0, 0, tiled=True)  8.25 us
    pallas_call x1, Pallas kernels, call_legendre(): pl.pallas_call(functools.partial(legendre_kernel, ord_dev), out_shape=jax...  6.97 us
    pallas_call x1, Pallas kernels, call_analysis(): pl.pallas_call(functools.partial(analysis_kernel, ord_dev), out_shape=jax...  5.84 us
  transfers between devices with their start and end apart: 10, of which 3 were waited for; matrix products, arithmetic and copies ran while one was open for 0% of the time, Pallas kernels for 14%

profile of v7, /device:TPU:1, one launch (start us, length us, event | category | flops | bytes accessed | tf_op | source)
XLA Modules:
  0.0 158.7 jit_solution(14279488364271086845)
XLA Ops:
  0.6 4.3 %forward.1 = bf16[32,8,16,128]{3,2,1,0:T(8,128)(2,1)} custom-call(s32[1]{0:T(128)} %bitcast.index_ref, s32[1,480]{1,0:T(1,128)} %bitcast.14, bf16[15,32,1024]{2,1,0:T(8,128)(2,1)} %field_hbm.3), custom_call_target="tpu_custom_call" | custom-call | tf_op jit(solution)/shard_map/forward/pallas_call | solution.py:492
  5.0 8.6 %all-to-all-start = ((bf16[32,8,16,128]{3,2,1,0:T(8,128)(2,1)}), bf16[32,8,16,128]{3,2,1,0:T(8,128)(2,1)S(1)}, u32[]{:S(2)}, u32[]{:S(2)}) async-start(bf16[32,8,16,128]{3,2,1,0:T(8,128)(2,1)} %forward.1), calls=%async_computation | async-start | bytes 2097152 | tf_op jit(solution)/shard_map/all_to_all | solution.py:688
  13.6 0.0 copy-start.1
  13.6 0.0 copy-start.2
  13.6 7.0 %legendre.1 = bf16[16,2,16,16,256]{4,3,2,1,0:T(8,128)(2,1)} custom-call(s32[1]{0:T(128)} %bitcast.index_ref, s32[1,480]{1,0:T(1,128)} %bitcast.15, f32[2,256]{1,0:T(2,128)} %constant.15.clone.geo_ref, f32[1,512]{1,0:T(1,128)} %constant.16.clone.prod_ref), custom_call_target="tpu_custom_call" | custom-call | flops 8000000000 | bytes 20000000 | tf_op jit(solution)/shard_map/legendre/pallas_call | solution.py:528
  20.6 0.0 copy-done.1
  20.6 3.1 %collective-permute-start = (bf16[2,2,32,256]{3,2,1,0:T(8,128)(2,1)S(1)}, bf16[2,2,32,256]{3,2,1,0:T(8,128)(2,1)S(1)}, u32[]{:S(2)}, u32[]{:S(2)}) collective-permute-start(bf16[2,2,32,256]{3,2,1,0:T(8,128)(2,1)S(1)} %get-tuple-element.25), channel_id=1, source_target_pairs={{0,2},{1,3},{2,4},{3,5},{4,6},{5,7},{6,0},{7,1},{8,10},{9,11},{10,... | collective-permute-start | bytes 196616 | tf_op jit(solution)/shard_map/ppermute | solution.py:599
  23.7 4.7 %collective-permute-start.1 = (bf16[2,2,32,256]{3,2,1,0:T(8,128)(2,1)S(1)}, bf16[2,2,32,256]{3,2,1,0:T(8,128)(2,1)S(1)}, u32[]{:S(2)}, u32[]{:S(2)}) collective-permute-start(bf16[2,2,32,256]{3,2,1,0:T(8,128)(2,1)S(1)} %get-tuple-element.26), channel_id=1, source_target_pairs={{0,3},{1,4},{2,5},{3,6},{4,7},{5,0},{6,1},{7,2},{8,11},{9,12},{10,... | collective-permute-start | bytes 196616 | tf_op jit(solution)/shard_map/ppermute | solution.py:599
  28.4 1.0 collective-permute-start.2
  29.4 3.9 %collective-permute-start.3 = (bf16[2,2,32,256]{3,2,1,0:T(8,128)(2,1)S(1)}, bf16[2,2,32,256]{3,2,1,0:T(8,128)(2,1)S(1)}, u32[]{:S(2)}, u32[]{:S(2)}) collective-permute-start(bf16[2,2,32,256]{3,2,1,0:T(8,128)(2,1)S(1)} %get-tuple-element.28), channel_id=1, source_target_pairs={{0,5},{1,6},{2,7},{3,0},{4,1},{5,2},{6,3},{7,4},{8,13},{9,14},{10,... | collective-permute-start | bytes 196616 | tf_op jit(solution)/shard_map/ppermute | solution.py:599
  33.3 0.0 all-to-all-done.rows_ref
  33.3 0.0 copy-done.2
  33.3 5.8 %analysis.1 = bf16[32,8,16,128]{3,2,1,0:T(8,128)(2,1)} custom-call(s32[1]{0:T(128)} %bitcast.index_ref, s32[480]{0:T(512)S(1)} %copy-done.2, bf16[32,8,16,128]{3,2,1,0:T(8,128)(2,1)S(1)} %all-to-all-done.rows_ref, bf16[16,512,256]{2,1,0:T(8,128)(2,1)} %bitcast.17), custom_call_target="tpu_custom_call" | custom-call | tf_op jit(solution)/shard_map/analysis/pallas_call | solution.py:566
  39.1 0.0 collective-permute-done.refs_2_
  39.1 0.0 collective-permute-done.1.refs_3_
  39.2 0.0 collective-permute-done.2.refs_4_
  39.2 0.0 collective-permute-done.3.refs_5_
  39.2 12.3 %all-to-all-start.1 = ((bf16[256,16,128]{2,1,0:T(8,128)(2,1)}), bf16[256,16,128]{2,1,0:T(8,128)(2,1)S(1)}, u32[]{:S(2)}, u32[]{:S(2)}) async-start(bf16[256,16,128]{2,1,0:T(8,128)(2,1)} %bitcast.5), calls=%async_computation.1 | async-start | bytes 2097152 | tf_op jit(solution)/shard_map/all_to_all | solution.py:700
  51.5 1.6 collective-permute-start.4
  53.1 4.0 %collective-permute-start.5 = (bf16[2,2,32,256]{3,2,1,0:T(8,128)(2,1)S(1)}, bf16[2,2,32,256]{3,2,1,0:T(8,128)(2,1)S(1)}, u32[]{:S(2)}, u32[]{:S(2)}) collective-permute-start(bf16[2,2,32,256]{3,2,1,0:T(8,128)(2,1)S(1)} %get-tuple-element.38), channel_id=1, source_target_pairs={{0,6},{1,7},{2,0},{3,1},{4,2},{5,3},{6,4},{7,5},{8,14},{9,15},{10,... | collective-permute-start | bytes 196616 | tf_op jit(solution)/shard_map/ppermute | solution.py:599
  57.1 0.9 collective-permute-start.6
  58.0 20.6 %collective-permute-done.4.refs_1_ = bf16[2,2,32,256]{3,2,1,0:T(8,128)(2,1)S(1)} collective-permute-done((bf16[2,2,32,256]{3,2,1,0:T(8,128)(2,1)S(1)}, bf16[2,2,32,256]{3,2,1,0:T(8,128)(2,1)S(1)}, u32[]{:S(2)}, u32[]{:S(2)}) %collective-permute-start.4) | collective-permute-done | bytes 65568 | tf_op jit(solution)/shard_map/ppermute | solution.py:599
  78.6 0.0 collective-permute-done.5.refs_6_
  78.6 0.0 collective-permute-done.6.refs_7_
  78.6 5.1 %all-to-all-done.1 = bf16[256,16,128]{2,1,0:T(8,128)(2,1)S(1)} async-done(((bf16[256,16,128]{2,1,0:T(8,128)(2,1)}), bf16[256,16,128]{2,1,0:T(8,128)(2,1)S(1)}, u32[]{:S(2)}, u32[]{:S(2)}) %all-to-all-start.1) | async-done | bytes 1048608 | tf_op jit(solution)/shard_map/all_to_all | solution.py:700
  83.7 3.6 %mix.1 = bf16[32,8,16,128]{3,2,1,0:T(8,128)(2,1)S(1)} custom-call(s32[1]{0:T(128)} %bitcast.1.index_ref, bf16[32,8,16,128]{3,2,1,0:T(8,128)(2,1)S(1)} %bitcast.9, bf16[2,2,32,256]{3,2,1,0:T(8,128)(2,1)S(1)} %get-tuple-element.32.refs_0_, bf16[2,2,32,256]{3,2,1,0:T(8,128)(2,1)S(1)} %collective-permute-done.4.refs_1_, ...), custom_call_target="tpu_custom_call" | custom-call | tf_op jit(solution)/shard_map/mix/pallas_call | solution.py:605
  87.3 40.4 %all_to_all.20 = bf16[256,16,128]{2,1,0:T(8,128)(2,1)S(1)} all-to-all(bf16[256,16,128]{2,1,0:T(8,128)(2,1)S(1)} %bitcast.10), channel_id=1, replica_groups=mesh['lat'=32,'ch'=8] {'lat','ch'}, dimensions={0} | all-to-all | bytes 2097152 | tf_op jit(solution)/shard_map/all_to_all | solution.py:702
  127.7 5.2 %synthesis.1 = bf16[32,8,16,128]{3,2,1,0:T(8,128)(2,1)} custom-call(s32[1]{0:T(128)} %bitcast.index_ref, s32[480]{0:T(512)S(1)} %copy-done.2, bf16[32,8,16,128]{3,2,1,0:T(8,128)(2,1)S(1)} %bitcast.11, bf16[16,512,256]{2,1,0:T(8,128)(2,1)} %bitcast.18), custom_call_target="tpu_custom_call" | custom-call | tf_op jit(solution)/shard_map/synthesis/pallas_call | solution.py:621
  132.9 4.4 %all-to-all-start.3 = ((bf16[32,8,16,128]{3,2,1,0:T(8,128)(2,1)}), bf16[32,8,16,128]{3,2,1,0:T(8,128)(2,1)S(1)}, u32[]{:S(2)}, u32[]{:S(2)}) async-start(bf16[32,8,16,128]{3,2,1,0:T(8,128)(2,1)} %synthesis.1), calls=%async_computation.3 | async-start | bytes 2097152 | tf_op jit(solution)/shard_map/all_to_all | solution.py:704
  137.4 0.0 copy-start.3
  137.4 4.1 %inverse_table.1.table_hbm = bf16[1024,1024]{1,0:T(8,128)(2,1)} custom-call(s32[1,480]{1,0:T(1,128)} %bitcast.16), custom_call_target="tpu_custom_call" | custom-call | flops 2000000000 | bytes 4000000 | tf_op jit(solution)/shard_map/inverse_table/pallas_call | solution.py:548
  141.5 0.0 copy-done.3
  141.5 0.0 copy-start
  141.5 4.6 %spectrum.1 = bf16[15,2,32,480]{3,2,1,0:T(8,128)(2,1)} custom-call(bf16[32,8,16,128]{3,2,1,0:T(8,128)(2,1)S(1)} %bitcast.12, bf16[512,480]{1,0:T(8,128)(2,1)S(1)} %copy-done.3), custom_call_target="tpu_custom_call" | custom-call | flops 3000000000 | bytes 4000000 | tf_op jit(solution)/shard_map/spectrum/pallas_call | solution.py:645
  146.1 8.2 %all-to-all-done.3.rows_ref = bf16[32,8,16,128]{3,2,1,0:T(8,128)(2,1)S(1)} async-done(((bf16[32,8,16,128]{3,2,1,0:T(8,128)(2,1)}), bf16[32,8,16,128]{3,2,1,0:T(8,128)(2,1)S(1)}, u32[]{:S(2)}, u32[]{:S(2)}) %all-to-all-start.3) | async-done | bytes 1048608 | tf_op jit(solution)/shard_map/all_to_all | solution.py:704
  154.4 0.0 copy-done
  154.4 4.2 %backward.1 = bf16[15,32,1024]{2,1,0:T(8,128)(2,1)} custom-call(s32[1]{0:T(128)} %bitcast.index_ref, bf16[32,8,16,128]{3,2,1,0:T(8,128)(2,1)S(1)} %all-to-all-done.3.rows_ref, bf16[1024,1024]{1,0:T(8,128)(2,1)} %inverse_table.1.table_hbm, bf16[15,32,1024]{2,1,0:T(8,128)(2,1)S(1)} %copy-done), custom_call_target="tpu_custom_call" | custom-call | tf_op jit(solution)/shard_map/backward/pallas_call | solution.py:661
  (1 shorter events, 0.0 us)
Async XLA Ops:
  5.0 28.3 %all-to-all-start = ((bf16[32,8,16,128]{3,2,1,0:T(8,128)(2,1)}), bf16[32,8,16,128]{3,2,1,0:T(8,128)(2,1)S(1)}, u32[]{:S(2)}, u32[]{:S(2)}) async-start(bf16[32,8,16,128]{3,2,1,0:T(8,128)(2,1)} %forward.1), calls=%async_computation | async-start | bytes 2097152 | tf_op jit(solution)/shard_map/all_to_all | solution.py:688
  13.6 7.0 %copy-start.1 = (bf16[2,256,32,15]{1,2,3,0:T(8,128)(2,1)S(1)}, bf16[2,256,32,15]{1,2,3,0:T(8,128)(2,1)}, u32[]{:S(2)}) copy-start(bf16[2,256,32,15]{1,2,3,0:T(8,128)(2,1)} %param.7) | copy-start | bytes 1474564
  13.6 19.7 %copy-start.2 = (s32[480]{0:T(512)S(1)}, s32[480]{0:T(512)}, u32[]{:S(2)}) copy-start(s32[480]{0:T(512)} %slots_ref.3) | copy-start | bytes 5764
  20.6 18.5 %collective-permute-start = (bf16[2,2,32,256]{3,2,1,0:T(8,128)(2,1)S(1)}, bf16[2,2,32,256]{3,2,1,0:T(8,128)(2,1)S(1)}, u32[]{:S(2)}, u32[]{:S(2)}) collective-permute-start(bf16[2,2,32,256]{3,2,1,0:T(8,128)(2,1)S(1)} %get-tuple-element.25), channel_id=1, source_target_pairs={{0,2},{1,3},{2,4},{3,5},{4,6},{5,7},{6,0},{7,1},{8,10},{9,11},{10,... | collective-permute-start | bytes 196616 | tf_op jit(solution)/shard_map/ppermute | solution.py:599
  23.7 15.5 %collective-permute-start.1 = (bf16[2,2,32,256]{3,2,1,0:T(8,128)(2,1)S(1)}, bf16[2,2,32,256]{3,2,1,0:T(8,128)(2,1)S(1)}, u32[]{:S(2)}, u32[]{:S(2)}) collective-permute-start(bf16[2,2,32,256]{3,2,1,0:T(8,128)(2,1)S(1)} %get-tuple-element.26), channel_id=1, source_target_pairs={{0,3},{1,4},{2,5},{3,6},{4,7},{5,0},{6,1},{7,2},{8,11},{9,12},{10,... | collective-permute-start | bytes 196616 | tf_op jit(solution)/shard_map/ppermute | solution.py:599
  28.4 10.8 %collective-permute-start.2 = (bf16[2,2,32,256]{3,2,1,0:T(8,128)(2,1)S(1)}, bf16[2,2,32,256]{3,2,1,0:T(8,128)(2,1)S(1)}, u32[]{:S(2)}, u32[]{:S(2)}) collective-permute-start(bf16[2,2,32,256]{3,2,1,0:T(8,128)(2,1)S(1)} %get-tuple-element.27), channel_id=1, source_target_pairs={{0,4},{1,5},{2,6},{3,7},{4,0},{5,1},{6,2},{7,3},{8,12},{9,13},{10,... | collective-permute-start | bytes 196616 | tf_op jit(solution)/shard_map/ppermute | solution.py:599
  29.4 9.8 %collective-permute-start.3 = (bf16[2,2,32,256]{3,2,1,0:T(8,128)(2,1)S(1)}, bf16[2,2,32,256]{3,2,1,0:T(8,128)(2,1)S(1)}, u32[]{:S(2)}, u32[]{:S(2)}) collective-permute-start(bf16[2,2,32,256]{3,2,1,0:T(8,128)(2,1)S(1)} %get-tuple-element.28), channel_id=1, source_target_pairs={{0,5},{1,6},{2,7},{3,0},{4,1},{5,2},{6,3},{7,4},{8,13},{9,14},{10,... | collective-permute-start | bytes 196616 | tf_op jit(solution)/shard_map/ppermute | solution.py:599
  39.2 44.5 %all-to-all-start.1 = ((bf16[256,16,128]{2,1,0:T(8,128)(2,1)}), bf16[256,16,128]{2,1,0:T(8,128)(2,1)S(1)}, u32[]{:S(2)}, u32[]{:S(2)}) async-start(bf16[256,16,128]{2,1,0:T(8,128)(2,1)} %bitcast.5), calls=%async_computation.1 | async-start | bytes 2097152 | tf_op jit(solution)/shard_map/all_to_all | solution.py:700
  51.5 27.1 %collective-permute-start.4 = (bf16[2,2,32,256]{3,2,1,0:T(8,128)(2,1)S(1)}, bf16[2,2,32,256]{3,2,1,0:T(8,128)(2,1)S(1)}, u32[]{:S(2)}, u32[]{:S(2)}) collective-permute-start(bf16[2,2,32,256]{3,2,1,0:T(8,128)(2,1)S(1)} %get-tuple-element.33), channel_id=1, source_target_pairs={{0,1},{1,2},{2,3},{3,4},{4,5},{5,6},{6,7},{7,0},{8,9},{9,10},{10,1... | collective-permute-start | bytes 196616 | tf_op jit(solution)/shard_map/ppermute | solution.py:599
  53.1 25.5 %collective-permute-start.5 = (bf16[2,2,32,256]{3,2,1,0:T(8,128)(2,1)S(1)}, bf16[2,2,32,256]{3,2,1,0:T(8,128)(2,1)S(1)}, u32[]{:S(2)}, u32[]{:S(2)}) collective-permute-start(bf16[2,2,32,256]{3,2,1,0:T(8,128)(2,1)S(1)} %get-tuple-element.38), channel_id=1, source_target_pairs={{0,6},{1,7},{2,0},{3,1},{4,2},{5,3},{6,4},{7,5},{8,14},{9,15},{10,... | collective-permute-start | bytes 196616 | tf_op jit(solution)/shard_map/ppermute | solution.py:599
  57.1 21.5 %collective-permute-start.6 = (bf16[2,2,32,256]{3,2,1,0:T(8,128)(2,1)S(1)}, bf16[2,2,32,256]{3,2,1,0:T(8,128)(2,1)S(1)}, u32[]{:S(2)}, u32[]{:S(2)}) collective-permute-start(bf16[2,2,32,256]{3,2,1,0:T(8,128)(2,1)S(1)} %get-tuple-element.39), channel_id=1, source_target_pairs={{0,7},{1,0},{2,1},{3,2},{4,3},{5,4},{6,5},{7,6},{8,15},{9,8},{10,9... | collective-permute-start | bytes 196616 | tf_op jit(solution)/shard_map/ppermute | solution.py:599
  132.9 21.4 %all-to-all-start.3 = ((bf16[32,8,16,128]{3,2,1,0:T(8,128)(2,1)}), bf16[32,8,16,128]{3,2,1,0:T(8,128)(2,1)S(1)}, u32[]{:S(2)}, u32[]{:S(2)}) async-start(bf16[32,8,16,128]{3,2,1,0:T(8,128)(2,1)} %synthesis.1), calls=%async_computation.3 | async-start | bytes 2097152 | tf_op jit(solution)/shard_map/all_to_all | solution.py:704
  137.4 4.1 %copy-start.3 = (bf16[512,480]{1,0:T(8,128)(2,1)S(1)}, bf16[512,480]{1,0:T(8,128)(2,1)}, u32[]{:S(2)}) copy-start(bf16[512,480]{1,0:T(8,128)(2,1)} %constant.17.clone.pick_ref) | copy-start | bytes 1474564
  141.5 12.9 %copy-start = (bf16[15,32,1024]{2,1,0:T(8,128)(2,1)S(1)}, bf16[15,32,1024]{2,1,0:T(8,128)(2,1)}, u32[]{:S(2)}) copy-start(bf16[15,32,1024]{2,1,0:T(8,128)(2,1)} %field_hbm.3) | copy-start | bytes 2949124

commit v8 on v7

--- a/solution.py
+++ b/solution.py
@@ -476,7 +476,7 @@
     return pl.CostEstimate(flops=int(flops), bytes_accessed=int(moved), transcendentals=0)
 
 
-MIX_BANDS = 8
+MIX_BANDS = 16
 vmem = pl.BlockSpec(memory_space=pltpu.VMEM)
 smem = pl.BlockSpec(memory_space=pltpu.SMEM)
 hbm = pl.BlockSpec(memory_space=pltpu.HBM)
@@ -691,7 +691,7 @@
     weights, legendre = lax.optimization_barrier((weights, legendre))
     ch_index = lax.axis_index("ch").reshape(1)
     ch_count = lax.axis_size("ch")
-    far = sorted(range(1, ch_count), key=lambda k: -min(k, ch_count - k))[: ch_count // 2]
+    far = sorted(range(1, ch_count), key=lambda k: -min(k, ch_count - k))[: ch_count // 2 - 1]
     near = [k for k in range(1, ch_count) if k not in far]
     weights = move_along(weight_pieces(ch_index, weights, ch_count), far)
     coeffs = call_analysis(ord_dev, index, order_slots, rows, legendre)

time: 159 us -> 156 us (0.981)
  starting transfers between devices: 44.5 us -> 42.8 us
    all_to_all x1, waiting for transfers between devices: 5.06 us -> 2.41 us  [on_device(): lax.all_to_all(coeffs.reshape(-1, PAD, LANES), ('lat', 'ch'), 0, 0, tiled...]
    ppermute x7, waiting for transfers between devices: 20.6 us -> 22.9 us  [move_along(): lax.ppermute(pieces[k], 'ch', [(e, (e + k) % count) for e in range(count)])]
  transfers between devices with their start and end apart: 10 -> 10, of which waited for: 3 -> 4; matrix products, arithmetic and copies ran while one was open for 0% -> 0% of each run, Pallas kernels for 14% -> 14%
where the time goes in v8:
time: 156 us
  starting transfers between devices  42.8 us (27%)
  blocking collectives  40.4 us (26%)
  Pallas kernels  38 us (24%)
  waiting for transfers between devices  33.5 us (21%)
    all_to_all x1, blocking collectives, on_device(): lax.all_to_all(mixed.reshape(-1, PAD, LANES), ('lat', 'ch'), 0, 0, tiled=...  40.4 us
    ppermute x7, waiting for transfers between devices, move_along(): lax.ppermute(pieces[k], 'ch', [(e, (e + k) % count) for e in range(count)])  22.9 us
    ppermute x7, starting transfers between devices, move_along(): lax.ppermute(pieces[k], 'ch', [(e, (e + k) % count) for e in range(count)])  18.3 us
    all_to_all x1, starting transfers between devices, on_device(): lax.all_to_all(coeffs.reshape(-1, PAD, LANES), ('lat', 'ch'), 0, 0, tiled...  11.4 us
    all_to_all x1, starting transfers between devices, on_device(): rows = lax.all_to_all(rows, 'lat', 0, 0, tiled=True)  8.6 us
    all_to_all x1, waiting for transfers between devices, on_device(): synth = lax.all_to_all(synth, 'lat', 0, 0, tiled=True)  8.25 us
    pallas_call x1, Pallas kernels, call_legendre(): pl.pallas_call(functools.partial(legendre_kernel, ord_dev), out_shape=jax...  6.97 us
    pallas_call x1, Pallas kernels, call_analysis(): pl.pallas_call(functools.partial(analysis_kernel, ord_dev), out_shape=jax...  5.83 us
  transfers between devices with their start and end apart: 10, of which 4 were waited for; matrix products, arithmetic and copies ran while one was open for 0% of the time, Pallas kernels for 14%

profile of v8, /device:TPU:1, one launch (start us, length us, event | category | flops | bytes accessed | tf_op | source)
XLA Modules:
  0.0 155.8 jit_solution(12353175110480914341)
XLA Ops:
  0.6 4.3 %forward.1 = bf16[32,8,16,128]{3,2,1,0:T(8,128)(2,1)} custom-call(s32[1]{0:T(128)} %bitcast.index_ref, s32[1,480]{1,0:T(1,128)} %bitcast.14, bf16[15,32,1024]{2,1,0:T(8,128)(2,1)} %field_hbm.3), custom_call_target="tpu_custom_call" | custom-call | tf_op jit(solution)/shard_map/forward/pallas_call | solution.py:492
  5.0 8.6 %all-to-all-start = ((bf16[32,8,16,128]{3,2,1,0:T(8,128)(2,1)}), bf16[32,8,16,128]{3,2,1,0:T(8,128)(2,1)S(1)}, u32[]{:S(2)}, u32[]{:S(2)}) async-start(bf16[32,8,16,128]{3,2,1,0:T(8,128)(2,1)} %forward.1), calls=%async_computation | async-start | bytes 2097152 | tf_op jit(solution)/shard_map/all_to_all | solution.py:688
  13.6 0.0 copy-start.1
  13.6 0.0 copy-start.2
  13.6 7.0 %legendre.1 = bf16[16,2,16,16,256]{4,3,2,1,0:T(8,128)(2,1)} custom-call(s32[1]{0:T(128)} %bitcast.index_ref, s32[1,480]{1,0:T(1,128)} %bitcast.15, f32[2,256]{1,0:T(2,128)} %constant.15.clone.geo_ref, f32[1,512]{1,0:T(1,128)} %constant.16.clone.prod_ref), custom_call_target="tpu_custom_call" | custom-call | flops 8000000000 | bytes 20000000 | tf_op jit(solution)/shard_map/legendre/pallas_call | solution.py:528
  20.6 0.0 copy-done.1
  20.6 4.4 %collective-permute-start = (bf16[2,2,32,256]{3,2,1,0:T(8,128)(2,1)S(1)}, bf16[2,2,32,256]{3,2,1,0:T(8,128)(2,1)S(1)}, u32[]{:S(2)}, u32[]{:S(2)}) collective-permute-start(bf16[2,2,32,256]{3,2,1,0:T(8,128)(2,1)S(1)} %get-tuple-element.26), channel_id=1, source_target_pairs={{0,3},{1,4},{2,5},{3,6},{4,7},{5,0},{6,1},{7,2},{8,11},{9,12},{10,... | collective-permute-start | bytes 196616 | tf_op jit(solution)/shard_map/ppermute | solution.py:599
  25.1 4.2 %collective-permute-start.1 = (bf16[2,2,32,256]{3,2,1,0:T(8,128)(2,1)S(1)}, bf16[2,2,32,256]{3,2,1,0:T(8,128)(2,1)S(1)}, u32[]{:S(2)}, u32[]{:S(2)}) collective-permute-start(bf16[2,2,32,256]{3,2,1,0:T(8,128)(2,1)S(1)} %get-tuple-element.27), channel_id=1, source_target_pairs={{0,4},{1,5},{2,6},{3,7},{4,0},{5,1},{6,2},{7,3},{8,12},{9,13},{10,... | collective-permute-start | bytes 196616 | tf_op jit(solution)/shard_map/ppermute | solution.py:599
  29.3 2.8 %collective-permute-start.2 = (bf16[2,2,32,256]{3,2,1,0:T(8,128)(2,1)S(1)}, bf16[2,2,32,256]{3,2,1,0:T(8,128)(2,1)S(1)}, u32[]{:S(2)}, u32[]{:S(2)}) collective-permute-start(bf16[2,2,32,256]{3,2,1,0:T(8,128)(2,1)S(1)} %get-tuple-element.28), channel_id=1, source_target_pairs={{0,5},{1,6},{2,7},{3,0},{4,1},{5,2},{6,3},{7,4},{8,13},{9,14},{10,... | collective-permute-start | bytes 196616 | tf_op jit(solution)/shard_map/ppermute | solution.py:599
  32.1 0.0 all-to-all-done.rows_ref
  32.1 0.0 copy-done.2
  32.1 5.8 %analysis.1 = bf16[32,8,16,128]{3,2,1,0:T(8,128)(2,1)} custom-call(s32[1]{0:T(128)} %bitcast.index_ref, s32[480]{0:T(512)S(1)} %copy-done.2, bf16[32,8,16,128]{3,2,1,0:T(8,128)(2,1)S(1)} %all-to-all-done.rows_ref, bf16[16,512,256]{2,1,0:T(8,128)(2,1)} %bitcast.17), custom_call_target="tpu_custom_call" | custom-call | tf_op jit(solution)/shard_map/analysis/pallas_call | solution.py:566
  37.9 0.0 collective-permute-done.refs_3_
  37.9 0.0 collective-permute-done.1.refs_4_
  38.0 0.0 collective-permute-done.2.refs_5_
  38.0 11.4 %all-to-all-start.1 = ((bf16[256,16,128]{2,1,0:T(8,128)(2,1)}), bf16[256,16,128]{2,1,0:T(8,128)(2,1)S(1)}, u32[]{:S(2)}, u32[]{:S(2)}) async-start(bf16[256,16,128]{2,1,0:T(8,128)(2,1)} %bitcast.5), calls=%async_computation.1 | async-start | bytes 2097152 | tf_op jit(solution)/shard_map/all_to_all | solution.py:700
  49.4 1.6 %collective-permute-start.3 = (bf16[2,2,32,256]{3,2,1,0:T(8,128)(2,1)S(1)}, bf16[2,2,32,256]{3,2,1,0:T(8,128)(2,1)S(1)}, u32[]{:S(2)}, u32[]{:S(2)}) collective-permute-start(bf16[2,2,32,256]{3,2,1,0:T(8,128)(2,1)S(1)} %get-tuple-element.33), channel_id=1, source_target_pairs={{0,1},{1,2},{2,3},{3,4},{4,5},{5,6},{6,7},{7,0},{8,9},{9,10},{10,1... | collective-permute-start | bytes 196616 | tf_op jit(solution)/shard_map/ppermute | solution.py:599
  51.0 2.6 %collective-permute-start.4 = (bf16[2,2,32,256]{3,2,1,0:T(8,128)(2,1)S(1)}, bf16[2,2,32,256]{3,2,1,0:T(8,128)(2,1)S(1)}, u32[]{:S(2)}, u32[]{:S(2)}) collective-permute-start(bf16[2,2,32,256]{3,2,1,0:T(8,128)(2,1)S(1)} %get-tuple-element.34), channel_id=1, source_target_pairs={{0,2},{1,3},{2,4},{3,5},{4,6},{5,7},{6,0},{7,1},{8,10},{9,11},{10,... | collective-permute-start | bytes 196616 | tf_op jit(solution)/shard_map/ppermute | solution.py:599
  53.6 1.4 collective-permute-start.5
  55.0 1.3 collective-permute-start.6
  56.3 20.2 %collective-permute-done.3.refs_1_ = bf16[2,2,32,256]{3,2,1,0:T(8,128)(2,1)S(1)} collective-permute-done((bf16[2,2,32,256]{3,2,1,0:T(8,128)(2,1)S(1)}, bf16[2,2,32,256]{3,2,1,0:T(8,128)(2,1)S(1)}, u32[]{:S(2)}, u32[]{:S(2)}) %collective-permute-start.3) | collective-permute-done | bytes 65568 | tf_op jit(solution)/shard_map/ppermute | solution.py:599
  76.5 2.7 %collective-permute-done.4.refs_2_ = bf16[2,2,32,256]{3,2,1,0:T(8,128)(2,1)S(1)} collective-permute-done((bf16[2,2,32,256]{3,2,1,0:T(8,128)(2,1)S(1)}, bf16[2,2,32,256]{3,2,1,0:T(8,128)(2,1)S(1)}, u32[]{:S(2)}, u32[]{:S(2)}) %collective-permute-start.4) | collective-permute-done | bytes 65568 | tf_op jit(solution)/shard_map/ppermute | solution.py:599
  79.2 0.0 collective-permute-done.5.refs_6_
  79.2 0.0 collective-permute-done.6.refs_7_
  79.2 2.4 %all-to-all-done.1 = bf16[256,16,128]{2,1,0:T(8,128)(2,1)S(1)} async-done(((bf16[256,16,128]{2,1,0:T(8,128)(2,1)}), bf16[256,16,128]{2,1,0:T(8,128)(2,1)S(1)}, u32[]{:S(2)}, u32[]{:S(2)}) %all-to-all-start.1) | async-done | bytes 1048608 | tf_op jit(solution)/shard_map/all_to_all | solution.py:700
  81.6 2.8 %mix.1 = bf16[32,8,16,128]{3,2,1,0:T(8,128)(2,1)S(1)} custom-call(s32[1]{0:T(128)} %bitcast.1.index_ref, bf16[32,8,16,128]{3,2,1,0:T(8,128)(2,1)S(1)} %bitcast.9, bf16[2,2,32,256]{3,2,1,0:T(8,128)(2,1)S(1)} %get-tuple-element.32.refs_0_, bf16[2,2,32,256]{3,2,1,0:T(8,128)(2,1)S(1)} %collective-permute-done.3.refs_1_, ...), custom_call_target="tpu_custom_call" | custom-call | tf_op jit(solution)/shard_map/mix/pallas_call | solution.py:605
  84.4 40.4 %all_to_all.20 = bf16[256,16,128]{2,1,0:T(8,128)(2,1)S(1)} all-to-all(bf16[256,16,128]{2,1,0:T(8,128)(2,1)S(1)} %bitcast.10), channel_id=1, replica_groups=mesh['lat'=32,'ch'=8] {'lat','ch'}, dimensions={0} | all-to-all | bytes 2097152 | tf_op jit(solution)/shard_map/all_to_all | solution.py:702
  124.8 5.2 %synthesis.1 = bf16[32,8,16,128]{3,2,1,0:T(8,128)(2,1)} custom-call(s32[1]{0:T(128)} %bitcast.index_ref, s32[480]{0:T(512)S(1)} %copy-done.2, bf16[32,8,16,128]{3,2,1,0:T(8,128)(2,1)S(1)} %bitcast.11, bf16[16,512,256]{2,1,0:T(8,128)(2,1)} %bitcast.18), custom_call_target="tpu_custom_call" | custom-call | tf_op jit(solution)/shard_map/synthesis/pallas_call | solution.py:621
  130.0 4.4 %all-to-all-start.3 = ((bf16[32,8,16,128]{3,2,1,0:T(8,128)(2,1)}), bf16[32,8,16,128]{3,2,1,0:T(8,128)(2,1)S(1)}, u32[]{:S(2)}, u32[]{:S(2)}) async-start(bf16[32,8,16,128]{3,2,1,0:T(8,128)(2,1)} %synthesis.1), calls=%async_computation.3 | async-start | bytes 2097152 | tf_op jit(solution)/shard_map/all_to_all | solution.py:704
  134.4 0.0 copy-start.3
  134.4 4.1 %inverse_table.1.table_hbm = bf16[1024,1024]{1,0:T(8,128)(2,1)} custom-call(s32[1,480]{1,0:T(1,128)} %bitcast.16), custom_call_target="tpu_custom_call" | custom-call | flops 2000000000 | bytes 4000000 | tf_op jit(solution)/shard_map/inverse_table/pallas_call | solution.py:548
  138.5 0.0 copy-done.3
  138.5 0.0 copy-start
  138.5 4.6 %spectrum.1 = bf16[15,2,32,480]{3,2,1,0:T(8,128)(2,1)} custom-call(bf16[32,8,16,128]{3,2,1,0:T(8,128)(2,1)S(1)} %bitcast.12, bf16[512,480]{1,0:T(8,128)(2,1)S(1)} %copy-done.3), custom_call_target="tpu_custom_call" | custom-call | flops 3000000000 | bytes 4000000 | tf_op jit(solution)/shard_map/spectrum/pallas_call | solution.py:645
  143.2 8.2 %all-to-all-done.3.rows_ref = bf16[32,8,16,128]{3,2,1,0:T(8,128)(2,1)S(1)} async-done(((bf16[32,8,16,128]{3,2,1,0:T(8,128)(2,1)}), bf16[32,8,16,128]{3,2,1,0:T(8,128)(2,1)S(1)}, u32[]{:S(2)}, u32[]{:S(2)}) %all-to-all-start.3) | async-done | bytes 1048608 | tf_op jit(solution)/shard_map/all_to_all | solution.py:704
  151.4 0.0 copy-done
  151.4 4.2 %backward.1 = bf16[15,32,1024]{2,1,0:T(8,128)(2,1)} custom-call(s32[1]{0:T(128)} %bitcast.index_ref, bf16[32,8,16,128]{3,2,1,0:T(8,128)(2,1)S(1)} %all-to-all-done.3.rows_ref, bf16[1024,1024]{1,0:T(8,128)(2,1)} %inverse_table.1.table_hbm, bf16[15,32,1024]{2,1,0:T(8,128)(2,1)S(1)} %copy-done), custom_call_target="tpu_custom_call" | custom-call | tf_op jit(solution)/shard_map/backward/pallas_call | solution.py:661
  (1 shorter events, 0.0 us)
Async XLA Ops:
  5.0 27.1 %all-to-all-start = ((bf16[32,8,16,128]{3,2,1,0:T(8,128)(2,1)}), bf16[32,8,16,128]{3,2,1,0:T(8,128)(2,1)S(1)}, u32[]{:S(2)}, u32[]{:S(2)}) async-start(bf16[32,8,16,128]{3,2,1,0:T(8,128)(2,1)} %forward.1), calls=%async_computation | async-start | bytes 2097152 | tf_op jit(solution)/shard_map/all_to_all | solution.py:688
  13.6 7.0 %copy-start.1 = (bf16[2,256,32,15]{1,2,3,0:T(8,128)(2,1)S(1)}, bf16[2,256,32,15]{1,2,3,0:T(8,128)(2,1)}, u32[]{:S(2)}) copy-start(bf16[2,256,32,15]{1,2,3,0:T(8,128)(2,1)} %param.7) | copy-start | bytes 1474564
  13.6 18.5 %copy-start.2 = (s32[480]{0:T(512)S(1)}, s32[480]{0:T(512)}, u32[]{:S(2)}) copy-start(s32[480]{0:T(512)} %slots_ref.3) | copy-start | bytes 5764
  20.6 17.3 %collective-permute-start = (bf16[2,2,32,256]{3,2,1,0:T(8,128)(2,1)S(1)}, bf16[2,2,32,256]{3,2,1,0:T(8,128)(2,1)S(1)}, u32[]{:S(2)}, u32[]{:S(2)}) collective-permute-start(bf16[2,2,32,256]{3,2,1,0:T(8,128)(2,1)S(1)} %get-tuple-element.26), channel_id=1, source_target_pairs={{0,3},{1,4},{2,5},{3,6},{4,7},{5,0},{6,1},{7,2},{8,11},{9,12},{10,... | collective-permute-start | bytes 196616 | tf_op jit(solution)/shard_map/ppermute | solution.py:599
  25.1 12.9 %collective-permute-start.1 = (bf16[2,2,32,256]{3,2,1,0:T(8,128)(2,1)S(1)}, bf16[2,2,32,256]{3,2,1,0:T(8,128)(2,1)S(1)}, u32[]{:S(2)}, u32[]{:S(2)}) collective-permute-start(bf16[2,2,32,256]{3,2,1,0:T(8,128)(2,1)S(1)} %get-tuple-element.27), channel_id=1, source_target_pairs={{0,4},{1,5},{2,6},{3,7},{4,0},{5,1},{6,2},{7,3},{8,12},{9,13},{10,... | collective-permute-start | bytes 196616 | tf_op jit(solution)/shard_map/ppermute | solution.py:599
  29.3 8.7 %collective-permute-start.2 = (bf16[2,2,32,256]{3,2,1,0:T(8,128)(2,1)S(1)}, bf16[2,2,32,256]{3,2,1,0:T(8,128)(2,1)S(1)}, u32[]{:S(2)}, u32[]{:S(2)}) collective-permute-start(bf16[2,2,32,256]{3,2,1,0:T(8,128)(2,1)S(1)} %get-tuple-element.28), channel_id=1, source_target_pairs={{0,5},{1,6},{2,7},{3,0},{4,1},{5,2},{6,3},{7,4},{8,13},{9,14},{10,... | collective-permute-start | bytes 196616 | tf_op jit(solution)/shard_map/ppermute | solution.py:599
  38.0 43.6 %all-to-all-start.1 = ((bf16[256,16,128]{2,1,0:T(8,128)(2,1)}), bf16[256,16,128]{2,1,0:T(8,128)(2,1)S(1)}, u32[]{:S(2)}, u32[]{:S(2)}) async-start(bf16[256,16,128]{2,1,0:T(8,128)(2,1)} %bitcast.5), calls=%async_computation.1 | async-start | bytes 2097152 | tf_op jit(solution)/shard_map/all_to_all | solution.py:700
  49.4 27.1 %collective-permute-start.3 = (bf16[2,2,32,256]{3,2,1,0:T(8,128)(2,1)S(1)}, bf16[2,2,32,256]{3,2,1,0:T(8,128)(2,1)S(1)}, u32[]{:S(2)}, u32[]{:S(2)}) collective-permute-start(bf16[2,2,32,256]{3,2,1,0:T(8,128)(2,1)S(1)} %get-tuple-element.33), channel_id=1, source_target_pairs={{0,1},{1,2},{2,3},{3,4},{4,5},{5,6},{6,7},{7,0},{8,9},{9,10},{10,1... | collective-permute-start | bytes 196616 | tf_op jit(solution)/shard_map/ppermute | solution.py:599
  51.0 28.2 %collective-permute-start.4 = (bf16[2,2,32,256]{3,2,1,0:T(8,128)(2,1)S(1)}, bf16[2,2,32,256]{3,2,1,0:T(8,128)(2,1)S(1)}, u32[]{:S(2)}, u32[]{:S(2)}) collective-permute-start(bf16[2,2,32,256]{3,2,1,0:T(8,128)(2,1)S(1)} %get-tuple-element.34), channel_id=1, source_target_pairs={{0,2},{1,3},{2,4},{3,5},{4,6},{5,7},{6,0},{7,1},{8,10},{9,11},{10,... | collective-permute-start | bytes 196616 | tf_op jit(solution)/shard_map/ppermute | solution.py:599
  53.6 25.5 %collective-permute-start.5 = (bf16[2,2,32,256]{3,2,1,0:T(8,128)(2,1)S(1)}, bf16[2,2,32,256]{3,2,1,0:T(8,128)(2,1)S(1)}, u32[]{:S(2)}, u32[]{:S(2)}) collective-permute-start(bf16[2,2,32,256]{3,2,1,0:T(8,128)(2,1)S(1)} %get-tuple-element.38), channel_id=1, source_target_pairs={{0,6},{1,7},{2,0},{3,1},{4,2},{5,3},{6,4},{7,5},{8,14},{9,15},{10,... | collective-permute-start | bytes 196616 | tf_op jit(solution)/shard_map/ppermute | solution.py:599
  55.0 24.2 %collective-permute-start.6 = (bf16[2,2,32,256]{3,2,1,0:T(8,128)(2,1)S(1)}, bf16[2,2,32,256]{3,2,1,0:T(8,128)(2,1)S(1)}, u32[]{:S(2)}, u32[]{:S(2)}) collective-permute-start(bf16[2,2,32,256]{3,2,1,0:T(8,128)(2,1)S(1)} %get-tuple-element.39), channel_id=1, source_target_pairs={{0,7},{1,0},{2,1},{3,2},{4,3},{5,4},{6,5},{7,6},{8,15},{9,8},{10,9... | collective-permute-start | bytes 196616 | tf_op jit(solution)/shard_map/ppermute | solution.py:599
  130.0 21.4 %all-to-all-start.3 = ((bf16[32,8,16,128]{3,2,1,0:T(8,128)(2,1)}), bf16[32,8,16,128]{3,2,1,0:T(8,128)(2,1)S(1)}, u32[]{:S(2)}, u32[]{:S(2)}) async-start(bf16[32,8,16,128]{3,2,1,0:T(8,128)(2,1)} %synthesis.1), calls=%async_computation.3 | async-start | bytes 2097152 | tf_op jit(solution)/shard_map/all_to_all | solution.py:704
  134.4 4.1 %copy-start.3 = (bf16[512,480]{1,0:T(8,128)(2,1)S(1)}, bf16[512,480]{1,0:T(8,128)(2,1)}, u32[]{:S(2)}) copy-start(bf16[512,480]{1,0:T(8,128)(2,1)} %constant.17.clone.pick_ref) | copy-start | bytes 1474564
  138.5 12.9 %copy-start = (bf16[15,32,1024]{2,1,0:T(8,128)(2,1)S(1)}, bf16[15,32,1024]{2,1,0:T(8,128)(2,1)}, u32[]{:S(2)}) copy-start(bf16[15,32,1024]{2,1,0:T(8,128)(2,1)} %field_hbm.3) | copy-start | bytes 2949124

commit v9 on v8

--- a/solution.py
+++ b/solution.py
@@ -476,7 +476,7 @@
     return pl.CostEstimate(flops=int(flops), bytes_accessed=int(moved), transcendentals=0)
 
 
-MIX_BANDS = 16
+MIX_BANDS = 32
 vmem = pl.BlockSpec(memory_space=pltpu.VMEM)
 smem = pl.BlockSpec(memory_space=pltpu.SMEM)
 hbm = pl.BlockSpec(memory_space=pltpu.HBM)

time: 156 us -> 156 us (level)
  no operation moved by 1% of the time
where the time goes in v9:
time: 156 us; the launch traced here: 155 us
  starting transfers between devices  42.8 us (27%)
  blocking collectives  40.4 us (26%)
  Pallas kernels  37.7 us (24%)
  waiting for transfers between devices  33.5 us (21%)
    all_to_all x1, blocking collectives, on_device(): lax.all_to_all(mixed.reshape(-1, PAD, LANES), ('lat', 'ch'), 0, 0, tiled=...  40.4 us
    ppermute x7, waiting for transfers between devices, move_along(): lax.ppermute(pieces[k], 'ch', [(e, (e + k) % count) for e in range(count)])  22.9 us
    ppermute x7, starting transfers between devices, move_along(): lax.ppermute(pieces[k], 'ch', [(e, (e + k) % count) for e in range(count)])  18.3 us
    all_to_all x1, starting transfers between devices, on_device(): lax.all_to_all(coeffs.reshape(-1, PAD, LANES), ('lat', 'ch'), 0, 0, tiled...  11.4 us
    all_to_all x1, starting transfers between devices, on_device(): rows = lax.all_to_all(rows, 'lat', 0, 0, tiled=True)  8.6 us
    all_to_all x1, waiting for transfers between devices, on_device(): synth = lax.all_to_all(synth, 'lat', 0, 0, tiled=True)  8.25 us
    pallas_call x1, Pallas kernels, call_legendre(): pl.pallas_call(functools.partial(legendre_kernel, ord_dev), out_shape=jax...  6.97 us
    pallas_call x1, Pallas kernels, call_analysis(): pl.pallas_call(functools.partial(analysis_kernel, ord_dev), out_shape=jax...  5.83 us
  transfers between devices with their start and end apart: 10, of which 4 were waited for; matrix products, arithmetic and copies ran while one was open for 0% of the time, Pallas kernels for 14%

profile of v9, /device:TPU:1, one launch (start us, length us, event | category | flops | bytes accessed | tf_op | source)
XLA Modules:
  0.0 155.4 jit_solution(11202174201428062952)
XLA Ops:
  0.6 4.3 %forward.1 = bf16[32,8,16,128]{3,2,1,0:T(8,128)(2,1)} custom-call(s32[1]{0:T(128)} %bitcast.index_ref, s32[1,480]{1,0:T(1,128)} %bitcast.14, bf16[15,32,1024]{2,1,0:T(8,128)(2,1)} %field_hbm.3), custom_call_target="tpu_custom_call" | custom-call | tf_op jit(solution)/shard_map/forward/pallas_call | solution.py:492
  5.0 8.6 %all-to-all-start = ((bf16[32,8,16,128]{3,2,1,0:T(8,128)(2,1)}), bf16[32,8,16,128]{3,2,1,0:T(8,128)(2,1)S(1)}, u32[]{:S(2)}, u32[]{:S(2)}) async-start(bf16[32,8,16,128]{3,2,1,0:T(8,128)(2,1)} %forward.1), calls=%async_computation | async-start | bytes 2097152 | tf_op jit(solution)/shard_map/all_to_all | solution.py:688
  13.6 0.0 copy-start.1
  13.6 0.0 copy-start.2
  13.6 7.0 %legendre.1 = bf16[16,2,16,16,256]{4,3,2,1,0:T(8,128)(2,1)} custom-call(s32[1]{0:T(128)} %bitcast.index_ref, s32[1,480]{1,0:T(1,128)} %bitcast.15, f32[2,256]{1,0:T(2,128)} %constant.15.clone.geo_ref, f32[1,512]{1,0:T(1,128)} %constant.16.clone.prod_ref), custom_call_target="tpu_custom_call" | custom-call | flops 8000000000 | bytes 20000000 | tf_op jit(solution)/shard_map/legendre/pallas_call | solution.py:528
  20.6 0.0 copy-done.1
  20.6 4.4 %collective-permute-start = (bf16[2,2,32,256]{3,2,1,0:T(8,128)(2,1)S(1)}, bf16[2,2,32,256]{3,2,1,0:T(8,128)(2,1)S(1)}, u32[]{:S(2)}, u32[]{:S(2)}) collective-permute-start(bf16[2,2,32,256]{3,2,1,0:T(8,128)(2,1)S(1)} %get-tuple-element.26), channel_id=1, source_target_pairs={{0,3},{1,4},{2,5},{3,6},{4,7},{5,0},{6,1},{7,2},{8,11},{9,12},{10,... | collective-permute-start | bytes 196616 | tf_op jit(solution)/shard_map/ppermute | solution.py:599
  25.1 4.2 %collective-permute-start.1 = (bf16[2,2,32,256]{3,2,1,0:T(8,128)(2,1)S(1)}, bf16[2,2,32,256]{3,2,1,0:T(8,128)(2,1)S(1)}, u32[]{:S(2)}, u32[]{:S(2)}) collective-permute-start(bf16[2,2,32,256]{3,2,1,0:T(8,128)(2,1)S(1)} %get-tuple-element.27), channel_id=1, source_target_pairs={{0,4},{1,5},{2,6},{3,7},{4,0},{5,1},{6,2},{7,3},{8,12},{9,13},{10,... | collective-permute-start | bytes 196616 | tf_op jit(solution)/shard_map/ppermute | solution.py:599
  29.3 2.8 %collective-permute-start.2 = (bf16[2,2,32,256]{3,2,1,0:T(8,128)(2,1)S(1)}, bf16[2,2,32,256]{3,2,1,0:T(8,128)(2,1)S(1)}, u32[]{:S(2)}, u32[]{:S(2)}) collective-permute-start(bf16[2,2,32,256]{3,2,1,0:T(8,128)(2,1)S(1)} %get-tuple-element.28), channel_id=1, source_target_pairs={{0,5},{1,6},{2,7},{3,0},{4,1},{5,2},{6,3},{7,4},{8,13},{9,14},{10,... | collective-permute-start | bytes 196616 | tf_op jit(solution)/shard_map/ppermute | solution.py:599
  32.1 0.0 all-to-all-done.rows_ref
  32.1 0.0 copy-done.2
  32.1 5.8 %analysis.1 = bf16[32,8,16,128]{3,2,1,0:T(8,128)(2,1)} custom-call(s32[1]{0:T(128)} %bitcast.index_ref, s32[480]{0:T(512)S(1)} %copy-done.2, bf16[32,8,16,128]{3,2,1,0:T(8,128)(2,1)S(1)} %all-to-all-done.rows_ref, bf16[16,512,256]{2,1,0:T(8,128)(2,1)} %bitcast.17), custom_call_target="tpu_custom_call" | custom-call | tf_op jit(solution)/shard_map/analysis/pallas_call | solution.py:566
  37.9 0.0 collective-permute-done.refs_3_
  37.9 0.0 collective-permute-done.1.refs_4_
  38.0 0.0 collective-permute-done.2.refs_5_
  38.0 11.4 %all-to-all-start.1 = ((bf16[256,16,128]{2,1,0:T(8,128)(2,1)}), bf16[256,16,128]{2,1,0:T(8,128)(2,1)S(1)}, u32[]{:S(2)}, u32[]{:S(2)}) async-start(bf16[256,16,128]{2,1,0:T(8,128)(2,1)} %bitcast.5), calls=%async_computation.1 | async-start | bytes 2097152 | tf_op jit(solution)/shard_map/all_to_all | solution.py:700
  49.4 1.6 %collective-permute-start.3 = (bf16[2,2,32,256]{3,2,1,0:T(8,128)(2,1)S(1)}, bf16[2,2,32,256]{3,2,1,0:T(8,128)(2,1)S(1)}, u32[]{:S(2)}, u32[]{:S(2)}) collective-permute-start(bf16[2,2,32,256]{3,2,1,0:T(8,128)(2,1)S(1)} %get-tuple-element.33), channel_id=1, source_target_pairs={{0,1},{1,2},{2,3},{3,4},{4,5},{5,6},{6,7},{7,0},{8,9},{9,10},{10,1... | collective-permute-start | bytes 196616 | tf_op jit(solution)/shard_map/ppermute | solution.py:599
  51.0 2.6 %collective-permute-start.4 = (bf16[2,2,32,256]{3,2,1,0:T(8,128)(2,1)S(1)}, bf16[2,2,32,256]{3,2,1,0:T(8,128)(2,1)S(1)}, u32[]{:S(2)}, u32[]{:S(2)}) collective-permute-start(bf16[2,2,32,256]{3,2,1,0:T(8,128)(2,1)S(1)} %get-tuple-element.34), channel_id=1, source_target_pairs={{0,2},{1,3},{2,4},{3,5},{4,6},{5,7},{6,0},{7,1},{8,10},{9,11},{10,... | collective-permute-start | bytes 196616 | tf_op jit(solution)/shard_map/ppermute | solution.py:599
  53.6 1.4 collective-permute-start.5
  55.0 1.3 collective-permute-start.6
  56.3 20.2 %collective-permute-done.3.refs_1_ = bf16[2,2,32,256]{3,2,1,0:T(8,128)(2,1)S(1)} collective-permute-done((bf16[2,2,32,256]{3,2,1,0:T(8,128)(2,1)S(1)}, bf16[2,2,32,256]{3,2,1,0:T(8,128)(2,1)S(1)}, u32[]{:S(2)}, u32[]{:S(2)}) %collective-permute-start.3) | collective-permute-done | bytes 65568 | tf_op jit(solution)/shard_map/ppermute | solution.py:599
  76.5 2.7 %collective-permute-done.4.refs_2_ = bf16[2,2,32,256]{3,2,1,0:T(8,128)(2,1)S(1)} collective-permute-done((bf16[2,2,32,256]{3,2,1,0:T(8,128)(2,1)S(1)}, bf16[2,2,32,256]{3,2,1,0:T(8,128)(2,1)S(1)}, u32[]{:S(2)}, u32[]{:S(2)}) %collective-permute-start.4) | collective-permute-done | bytes 65568 | tf_op jit(solution)/shard_map/ppermute | solution.py:599
  79.2 0.0 collective-permute-done.5.refs_6_
  79.2 0.0 collective-permute-done.6.refs_7_
  79.2 2.4 %all-to-all-done.1 = bf16[256,16,128]{2,1,0:T(8,128)(2,1)S(1)} async-done(((bf16[256,16,128]{2,1,0:T(8,128)(2,1)}), bf16[256,16,128]{2,1,0:T(8,128)(2,1)S(1)}, u32[]{:S(2)}, u32[]{:S(2)}) %all-to-all-start.1) | async-done | bytes 1048608 | tf_op jit(solution)/shard_map/all_to_all | solution.py:700
  81.6 2.4 %mix.1 = bf16[32,8,16,128]{3,2,1,0:T(8,128)(2,1)S(1)} custom-call(s32[1]{0:T(128)} %bitcast.1.index_ref, bf16[32,8,16,128]{3,2,1,0:T(8,128)(2,1)S(1)} %bitcast.9, bf16[2,2,32,256]{3,2,1,0:T(8,128)(2,1)S(1)} %get-tuple-element.32.refs_0_, bf16[2,2,32,256]{3,2,1,0:T(8,128)(2,1)S(1)} %collective-permute-done.3.refs_1_, ...), custom_call_target="tpu_custom_call" | custom-call | tf_op jit(solution)/shard_map/mix/pallas_call | solution.py:605
  84.0 40.4 %all_to_all.20 = bf16[256,16,128]{2,1,0:T(8,128)(2,1)S(1)} all-to-all(bf16[256,16,128]{2,1,0:T(8,128)(2,1)S(1)} %bitcast.10), channel_id=1, replica_groups=mesh['lat'=32,'ch'=8] {'lat','ch'}, dimensions={0} | all-to-all | bytes 2097152 | tf_op jit(solution)/shard_map/all_to_all | solution.py:702
  124.4 5.2 %synthesis.1 = bf16[32,8,16,128]{3,2,1,0:T(8,128)(2,1)} custom-call(s32[1]{0:T(128)} %bitcast.index_ref, s32[480]{0:T(512)S(1)} %copy-done.2, bf16[32,8,16,128]{3,2,1,0:T(8,128)(2,1)S(1)} %bitcast.11, bf16[16,512,256]{2,1,0:T(8,128)(2,1)} %bitcast.18), custom_call_target="tpu_custom_call" | custom-call | tf_op jit(solution)/shard_map/synthesis/pallas_call | solution.py:621
  129.6 4.4 %all-to-all-start.3 = ((bf16[32,8,16,128]{3,2,1,0:T(8,128)(2,1)}), bf16[32,8,16,128]{3,2,1,0:T(8,128)(2,1)S(1)}, u32[]{:S(2)}, u32[]{:S(2)}) async-start(bf16[32,8,16,128]{3,2,1,0:T(8,128)(2,1)} %synthesis.1), calls=%async_computation.3 | async-start | bytes 2097152 | tf_op jit(solution)/shard_map/all_to_all | solution.py:704
  134.1 0.0 copy-start.3
  134.1 4.1 %inverse_table.1.table_hbm = bf16[1024,1024]{1,0:T(8,128)(2,1)} custom-call(s32[1,480]{1,0:T(1,128)} %bitcast.16), custom_call_target="tpu_custom_call" | custom-call | flops 2000000000 | bytes 4000000 | tf_op jit(solution)/shard_map/inverse_table/pallas_call | solution.py:548
  138.2 0.0 copy-done.3
  138.2 0.0 copy-start
  138.2 4.6 %spectrum.1 = bf16[15,2,32,480]{3,2,1,0:T(8,128)(2,1)} custom-call(bf16[32,8,16,128]{3,2,1,0:T(8,128)(2,1)S(1)} %bitcast.12, bf16[512,480]{1,0:T(8,128)(2,1)S(1)} %copy-done.3), custom_call_target="tpu_custom_call" | custom-call | flops 3000000000 | bytes 4000000 | tf_op jit(solution)/shard_map/spectrum/pallas_call | solution.py:645
  142.8 8.2 %all-to-all-done.3.rows_ref = bf16[32,8,16,128]{3,2,1,0:T(8,128)(2,1)S(1)} async-done(((bf16[32,8,16,128]{3,2,1,0:T(8,128)(2,1)}), bf16[32,8,16,128]{3,2,1,0:T(8,128)(2,1)S(1)}, u32[]{:S(2)}, u32[]{:S(2)}) %all-to-all-start.3) | async-done | bytes 1048608 | tf_op jit(solution)/shard_map/all_to_all | solution.py:704
  151.1 0.0 copy-done
  151.1 4.2 %backward.1 = bf16[15,32,1024]{2,1,0:T(8,128)(2,1)} custom-call(s32[1]{0:T(128)} %bitcast.index_ref, bf16[32,8,16,128]{3,2,1,0:T(8,128)(2,1)S(1)} %all-to-all-done.3.rows_ref, bf16[1024,1024]{1,0:T(8,128)(2,1)} %inverse_table.1.table_hbm, bf16[15,32,1024]{2,1,0:T(8,128)(2,1)S(1)} %copy-done), custom_call_target="tpu_custom_call" | custom-call | tf_op jit(solution)/shard_map/backward/pallas_call | solution.py:661
  (1 shorter events, 0.0 us)
Async XLA Ops:
  5.0 27.1 %all-to-all-start = ((bf16[32,8,16,128]{3,2,1,0:T(8,128)(2,1)}), bf16[32,8,16,128]{3,2,1,0:T(8,128)(2,1)S(1)}, u32[]{:S(2)}, u32[]{:S(2)}) async-start(bf16[32,8,16,128]{3,2,1,0:T(8,128)(2,1)} %forward.1), calls=%async_computation | async-start | bytes 2097152 | tf_op jit(solution)/shard_map/all_to_all | solution.py:688
  13.6 7.0 %copy-start.1 = (bf16[2,256,32,15]{1,2,3,0:T(8,128)(2,1)S(1)}, bf16[2,256,32,15]{1,2,3,0:T(8,128)(2,1)}, u32[]{:S(2)}) copy-start(bf16[2,256,32,15]{1,2,3,0:T(8,128)(2,1)} %param.7) | copy-start | bytes 1474564
  13.6 18.5 %copy-start.2 = (s32[480]{0:T(512)S(1)}, s32[480]{0:T(512)}, u32[]{:S(2)}) copy-start(s32[480]{0:T(512)} %slots_ref.3) | copy-start | bytes 5764
  20.6 17.3 %collective-permute-start = (bf16[2,2,32,256]{3,2,1,0:T(8,128)(2,1)S(1)}, bf16[2,2,32,256]{3,2,1,0:T(8,128)(2,1)S(1)}, u32[]{:S(2)}, u32[]{:S(2)}) collective-permute-start(bf16[2,2,32,256]{3,2,1,0:T(8,128)(2,1)S(1)} %get-tuple-element.26), channel_id=1, source_target_pairs={{0,3},{1,4},{2,5},{3,6},{4,7},{5,0},{6,1},{7,2},{8,11},{9,12},{10,... | collective-permute-start | bytes 196616 | tf_op jit(solution)/shard_map/ppermute | solution.py:599
  25.1 12.9 %collective-permute-start.1 = (bf16[2,2,32,256]{3,2,1,0:T(8,128)(2,1)S(1)}, bf16[2,2,32,256]{3,2,1,0:T(8,128)(2,1)S(1)}, u32[]{:S(2)}, u32[]{:S(2)}) collective-permute-start(bf16[2,2,32,256]{3,2,1,0:T(8,128)(2,1)S(1)} %get-tuple-element.27), channel_id=1, source_target_pairs={{0,4},{1,5},{2,6},{3,7},{4,0},{5,1},{6,2},{7,3},{8,12},{9,13},{10,... | collective-permute-start | bytes 196616 | tf_op jit(solution)/shard_map/ppermute | solution.py:599
  29.3 8.7 %collective-permute-start.2 = (bf16[2,2,32,256]{3,2,1,0:T(8,128)(2,1)S(1)}, bf16[2,2,32,256]{3,2,1,0:T(8,128)(2,1)S(1)}, u32[]{:S(2)}, u32[]{:S(2)}) collective-permute-start(bf16[2,2,32,256]{3,2,1,0:T(8,128)(2,1)S(1)} %get-tuple-element.28), channel_id=1, source_target_pairs={{0,5},{1,6},{2,7},{3,0},{4,1},{5,2},{6,3},{7,4},{8,13},{9,14},{10,... | collective-permute-start | bytes 196616 | tf_op jit(solution)/shard_map/ppermute | solution.py:599
  38.0 43.6 %all-to-all-start.1 = ((bf16[256,16,128]{2,1,0:T(8,128)(2,1)}), bf16[256,16,128]{2,1,0:T(8,128)(2,1)S(1)}, u32[]{:S(2)}, u32[]{:S(2)}) async-start(bf16[256,16,128]{2,1,0:T(8,128)(2,1)} %bitcast.5), calls=%async_computation.1 | async-start | bytes 2097152 | tf_op jit(solution)/shard_map/all_to_all | solution.py:700
  49.4 27.1 %collective-permute-start.3 = (bf16[2,2,32,256]{3,2,1,0:T(8,128)(2,1)S(1)}, bf16[2,2,32,256]{3,2,1,0:T(8,128)(2,1)S(1)}, u32[]{:S(2)}, u32[]{:S(2)}) collective-permute-start(bf16[2,2,32,256]{3,2,1,0:T(8,128)(2,1)S(1)} %get-tuple-element.33), channel_id=1, source_target_pairs={{0,1},{1,2},{2,3},{3,4},{4,5},{5,6},{6,7},{7,0},{8,9},{9,10},{10,1... | collective-permute-start | bytes 196616 | tf_op jit(solution)/shard_map/ppermute | solution.py:599
  51.0 28.2 %collective-permute-start.4 = (bf16[2,2,32,256]{3,2,1,0:T(8,128)(2,1)S(1)}, bf16[2,2,32,256]{3,2,1,0:T(8,128)(2,1)S(1)}, u32[]{:S(2)}, u32[]{:S(2)}) collective-permute-start(bf16[2,2,32,256]{3,2,1,0:T(8,128)(2,1)S(1)} %get-tuple-element.34), channel_id=1, source_target_pairs={{0,2},{1,3},{2,4},{3,5},{4,6},{5,7},{6,0},{7,1},{8,10},{9,11},{10,... | collective-permute-start | bytes 196616 | tf_op jit(solution)/shard_map/ppermute | solution.py:599
  53.6 25.5 %collective-permute-start.5 = (bf16[2,2,32,256]{3,2,1,0:T(8,128)(2,1)S(1)}, bf16[2,2,32,256]{3,2,1,0:T(8,128)(2,1)S(1)}, u32[]{:S(2)}, u32[]{:S(2)}) collective-permute-start(bf16[2,2,32,256]{3,2,1,0:T(8,128)(2,1)S(1)} %get-tuple-element.38), channel_id=1, source_target_pairs={{0,6},{1,7},{2,0},{3,1},{4,2},{5,3},{6,4},{7,5},{8,14},{9,15},{10,... | collective-permute-start | bytes 196616 | tf_op jit(solution)/shard_map/ppermute | solution.py:599
  55.0 24.2 %collective-permute-start.6 = (bf16[2,2,32,256]{3,2,1,0:T(8,128)(2,1)S(1)}, bf16[2,2,32,256]{3,2,1,0:T(8,128)(2,1)S(1)}, u32[]{:S(2)}, u32[]{:S(2)}) collective-permute-start(bf16[2,2,32,256]{3,2,1,0:T(8,128)(2,1)S(1)} %get-tuple-element.39), channel_id=1, source_target_pairs={{0,7},{1,0},{2,1},{3,2},{4,3},{5,4},{6,5},{7,6},{8,15},{9,8},{10,9... | collective-permute-start | bytes 196616 | tf_op jit(solution)/shard_map/ppermute | solution.py:599
  129.6 21.4 %all-to-all-start.3 = ((bf16[32,8,16,128]{3,2,1,0:T(8,128)(2,1)}), bf16[32,8,16,128]{3,2,1,0:T(8,128)(2,1)S(1)}, u32[]{:S(2)}, u32[]{:S(2)}) async-start(bf16[32,8,16,128]{3,2,1,0:T(8,128)(2,1)} %synthesis.1), calls=%async_computation.3 | async-start | bytes 2097152 | tf_op jit(solution)/shard_map/all_to_all | solution.py:704
  134.1 4.1 %copy-start.3 = (bf16[512,480]{1,0:T(8,128)(2,1)S(1)}, bf16[512,480]{1,0:T(8,128)(2,1)}, u32[]{:S(2)}) copy-start(bf16[512,480]{1,0:T(8,128)(2,1)} %constant.17.clone.pick_ref) | copy-start | bytes 1474564
  138.2 12.9 %copy-start = (bf16[15,32,1024]{2,1,0:T(8,128)(2,1)S(1)}, bf16[15,32,1024]{2,1,0:T(8,128)(2,1)}, u32[]{:S(2)}) copy-start(bf16[15,32,1024]{2,1,0:T(8,128)(2,1)} %field_hbm.3) | copy-start | bytes 2949124
